TPU v7x, 32 devices: a whole 2x2x4 slice. The times are simulated.
32 devices in a mesh: space: 4 (over z), dir: 4 (over y, x), band: 2 (over core).
Axes of the slice: x: 2, y: 2, z: 4, core: 2. Of those that a mesh axis runs over, the one named last changes fastest.
Arguments:
- adjoint_start: float32 [64, 32, 24, 1152], P('dir', 'band', 'space'), may hold values from 0.5 to 1.5
- primal_deviations: float32 [64, 32, 24, 1152], P('dir', 'band', 'space'), may hold values from 0.5 to 1.5
- density: float32 [24, 1152], P('space'), may hold values from 0 to 1
- material: int32 [24, 1152], P('space'), may hold values from 0 to 3
- rate_table: float32 [4, 32], P(None, 'band'), may hold values from 0.05 to 2
- group_speed: float32 [32], P('band'), may hold values from 0.3 to 3
- heat_capacity: float32 [32], replicated, may hold values from 0.1 to 4, as said below
- objective_weight: float32 [24, 1152], P('space'), may hold values from -6 to 6
Outputs:
- dual_intensity: float32 [64, 32, 24, 1152], P('dir', 'band', 'space')
- design_gradient: float32 [24, 1152], P('space')
Inputs may be any that keep to these rules, and one draw needn't show every extreme that they name: `heat_capacity`: heat capacities of the bands, positive.
All inputs are finite; a program needn't handle non-finite values.
Results may differ from a plain program's by a relative error of at most 0.0003.
Values sent between devices are 32-bit elements; how exact they have to be, the bound alone decides.
No kernel may reach another device: no remote copies, remote signals or barrier semaphores. Data moves between devices by JAX's collectives and lax.ppermute only.
A program may use at most 128 MiB of HBM per device.

v0:
```python
import jax
import jax.numpy as jnp
from jax import lax
from jax.sharding import PartitionSpec as P

NDIR = 64
NB = 32
NY = 192
ITERS = 2


def passed_along(value, axis, steps):
    count = lax.axis_size(axis)
    leading, last = (max(0, -steps), min(count, count - steps))
    return lax.ppermute(value, axis, [(source, source + steps) for source in range(leading, last)])


def local_directions(count):
    block = lax.axis_index("dir")
    slot = jnp.arange(count, dtype=jnp.int32)
    half = count // 2
    side = slot // half
    pair = slot % half
    azimuth = jnp.pi * ((block * half + pair).astype(jnp.float32) + 0.5) / (NDIR // 2) - jnp.pi / 2
    along_z = 0.4 * (1.0 - 2.0 * (pair % 2).astype(jnp.float32))
    tilt = jnp.sqrt(1.0 - along_z * along_z)
    along_x = (1.0 - 2.0 * side.astype(jnp.float32)) * tilt * jnp.cos(azimuth)
    along_y = tilt * jnp.sin(azimuth)
    return (along_x, along_y, along_z)


def plane_move(field, offset):
    last = field.ndim - 1
    size = field.shape[last]
    if offset > 0:
        rest = lax.slice_in_dim(field, offset, size, axis=last)
        pad_block = jnp.zeros_like(lax.slice_in_dim(field, 0, offset, axis=last))
        return jnp.concatenate([rest, pad_block], last)
    rest = lax.slice_in_dim(field, 0, size + offset, axis=last)
    pad_block = jnp.zeros_like(lax.slice_in_dim(field, 0, -offset, axis=last))
    return jnp.concatenate([pad_block, rest], last)


def first_neighbours(dual_intensity):
    half = dual_intensity.shape[0] // 2
    edge_ahead = passed_along(dual_intensity[:half, :, :1], "space", -1)
    edge_behind = passed_along(dual_intensity[half:, :, -1:], "space", 1)
    forward_side = jnp.concatenate([dual_intensity[:half, :, 1:], edge_ahead], axis=2)
    backward_side = jnp.concatenate([edge_behind, dual_intensity[half:, :, :-1]], axis=2)
    return jnp.concatenate([forward_side, backward_side], axis=0)


def reduce_volumes(partials):
    summed = lax.psum(partials, "band")
    summed = lax.psum(summed, "dir")
    return summed


def on_device(
    adjoint_start,
    primal_deviations,
    density,
    material,
    rate_table,
    group_speed,
    heat_capacity,
    objective_weight,
):
    count = adjoint_start.shape[0]
    bands = adjoint_start.shape[1]
    plane = adjoint_start.shape[3]
    along_x, along_y, along_z = local_directions(count)
    position = jnp.arange(plane, dtype=jnp.int32) % NY
    keep_ahead = (position < NY - 1).astype(jnp.float32)
    keep_behind = (position > 0).astype(jnp.float32)
    speed = group_speed[None, :, None, None]
    speed_x = speed * jnp.abs(along_x)[:, None, None, None]
    speed_y = speed * jnp.abs(along_y)[:, None, None, None]
    speed_z = speed * jnp.abs(along_z)[:, None, None, None]
    rising_y = (along_y > 0)[:, None, None, None]
    rising_z = (along_z > 0)[:, None, None, None]
    indicator = (
        material[None] == jnp.arange(rate_table.shape[0], dtype=jnp.int32)[:, None, None]
    ).astype(jnp.float32)
    base = jnp.einsum("mb,mxp->bxp", rate_table, indicator, precision=lax.Precision.HIGHEST)
    relaxation_frequency = base * (0.2 + 0.8 * density)[None]
    relaxation_slope = 0.8 * base
    local_heat = lax.dynamic_slice_in_dim(heat_capacity, lax.axis_index("band") * bands, bands)
    weights = local_heat / (NDIR * jnp.sum(heat_capacity))
    column = weights[None, :, None, None]
    thermal_share = jnp.sum(column * primal_deviations, axis=(0, 1))
    relaxation_share = jnp.sum(relaxation_frequency[None] * adjoint_start, axis=(0, 1))
    crystal_kelvin, exchange_link = reduce_volumes((thermal_share, relaxation_share))
    diagonal = speed_x + speed_y + speed_z + relaxation_frequency[None]
    cell_source = NDIR * NB * objective_weight
    dual_intensity = adjoint_start
    gradient_part = jnp.zeros_like(density)
    for step in range(ITERS):
        source = column * (exchange_link + cell_source)[None, None]
        near = speed_x * first_neighbours(dual_intensity)
        near = near + speed_y * jnp.where(
            rising_y,
            plane_move(dual_intensity, 1) * keep_ahead,
            plane_move(dual_intensity, -1) * keep_behind,
        )
        near = near + speed_z * jnp.where(
            rising_z, plane_move(dual_intensity, NY), plane_move(dual_intensity, -NY)
        )
        dual_intensity = (source + near) / diagonal
        gradient_part = gradient_part + jnp.sum(
            relaxation_slope[None]
            * dual_intensity
            * (primal_deviations - crystal_kelvin[None, None]),
            axis=(0, 1),
        )
        if step + 1 < ITERS:
            (exchange_link,) = reduce_volumes(
                (jnp.sum(relaxation_frequency[None] * dual_intensity, axis=(0, 1)),)
            )
    (gradient,) = reduce_volumes((gradient_part,))
    return (dual_intensity, gradient * (-0.125 / ITERS))


def solution(mesh):
    placed = (
        P("dir", "band", "space", None),
        P("dir", "band", "space", None),
        P("space", None),
        P("space", None),
        P(None, "band"),
        P("band"),
        P(),
        P("space", None),
    )
    return jax.shard_map(
        on_device,
        mesh=mesh,
        in_specs=placed,
        out_specs=(P("dir", "band", "space", None), P("space", None)),
        check_vma=False,
    )
```

profile of v0, /device:TPU:16, one launch (start us, length us, event | category | flops | bytes accessed | tf_op | source)
XLA Modules:
  0.0 179.0 jit_solution(2327723472785373144)
XLA Ops:
  0.6 2.3 %fusion.34 = (f32[8,16,1,1152]{3,1,2,0:T(8,128)}, f32[8,16,1,1152]{3,1,2,0:T(8,128)}) fusion(f32[16,16,6,1152]{3,1,2,0:T(8,128)} %param.8), kind=kLoop, calls=%fused_computation.72 | loop fusion | bytes 2359296 | tf_op jit(solution)/shard_map/slice | solution.py:46
  3.0 2.3 %collective-permute-start = (f32[8,16,1,1152]{3,1,2,0:T(8,128)}, f32[8,16,1,1152]{3,1,2,0:T(8,128)}, u32[]{:S(2)}, u32[]{:S(2)}) collective-permute-start(f32[8,16,1,1152]{3,1,2,0:T(8,128)} %get-tuple-element.21), channel_id=1, source_target_pairs={{8,0},{16,8},{24,16},{9,1},{17,9},{25,17},{10,2},{18,10},{26,18},{... | collective-permute-start | bytes 1769480 | tf_op jit(solution)/shard_map/ppermute | solution.py:15
  5.3 4.3 %collective-permute-start.1 = (f32[8,16,1,1152]{3,1,2,0:T(8,128)}, f32[8,16,1,1152]{3,1,2,0:T(8,128)}, u32[]{:S(2)}, u32[]{:S(2)}) collective-permute-start(f32[8,16,1,1152]{3,1,2,0:T(8,128)} %get-tuple-element.22), channel_id=1, source_target_pairs={{0,8},{8,16},{16,24},{1,9},{9,17},{17,25},{2,10},{10,18},{18,26},{... | collective-permute-start | bytes 1769480 | tf_op jit(solution)/shard_map/ppermute | solution.py:15
  9.8 5.8 %fusion.33 = (f32[8,16,5,1152]{3,1,2,0:T(8,128)}, f32[8,16,5,1152]{3,1,2,0:T(8,128)}) fusion(f32[16,16,6,1152]{3,1,2,0:T(8,128)} %param.8), kind=kLoop, calls=%fused_computation.71 | loop fusion | bytes 11796480 | tf_op jit(solution)/shard_map/slice | solution.py:48
  15.6 12.4 %fusion.35 = (f32[16,16,6,1151]{3,1,2,0:T(8,128)}, f32[16,16,6,1151]{3,1,2,0:T(8,128)}) fusion(f32[16,16,6,1152]{3,1,2,0:T(8,128)} %param.8), kind=kLoop, calls=%fused_computation.73 | loop fusion | bytes 28286976 | tf_op jit(solution)/shard_map/slice | solution.py:36
  28.0 1.2 multiply_bitcast_fusion
  29.9 3.6 %multiply_reduce_fusion.4 = f32[6,1152]{1,0:T(8,128)S(1)} fusion(f32[16,16,6,1152]{3,1,2,0:T(8,128)} %param.8, f32[16,6,1152]{2,0,1:T(8,128)S(1)} %get-tuple-element.28), kind=kLoop, calls=%fused_computation.14 | loop fusion | flops 3532032 | bytes 7547904 | tf_op jit(solution)/shard_map/reduce_sum | solution.py:92
  33.6 3.5 %psum.56 = f32[6,1152]{1,0:T(8,128)S(1)} all-reduce(f32[6,1152]{1,0:T(8,128)S(1)} %multiply_reduce_fusion.4), channel_id=1, replica_groups=mesh['space'=4,'dir'=4,'band'=2] {'band'}, use_global_device_ids=true, to_apply=%region_2.3 | all-reduce | flops 6912 | bytes 55296 | tf_op jit(solution)/shard_map/psum | solution.py:54
  37.0 16.7 %psum.57 = f32[6,1152]{1,0:T(8,128)S(1)} all-reduce(f32[6,1152]{1,0:T(8,128)S(1)} %psum.56), channel_id=1, replica_groups=mesh['space'=4,'dir'=4,'band'=2] {'dir'}, use_global_device_ids=true, to_apply=%region_3.4 | all-reduce | flops 6912 | bytes 55296 | tf_op jit(solution)/shard_map/psum | solution.py:55
  55.1 3.6 %multiply_reduce_fusion.2 = f32[6,1152]{1,0:T(8,128)S(1)} fusion(f32[16,16,6,1152]{3,1,2,0:T(8,128)} %param.9, f32[16]{0:T(128)S(1)} %dynamic-slice_divide_fusion), kind=kLoop, calls=%fused_computation.12 | loop fusion | flops 3532032 | bytes 7105600 | tf_op jit(solution)/shard_map/reduce_sum | solution.py:91
  59.6 9.9 %fusion.36 = (f32[16,16,6,960]{3,1,2,0:T(8,128)S(1)}, f32[16,16,6,960]{3,1,2,0:T(8,128)}) fusion(f32[16,16,6,1152]{3,1,2,0:T(8,128)} %param.8), kind=kLoop, calls=%fused_computation.74 | loop fusion | bytes 23592960 | tf_op jit(solution)/shard_map/slice | solution.py:36
  69.5 14.2 %multiply_reduce_fusion.3 = (f32[6,1152]{1,0:T(8,128)S(1)}, f32[16,16,6,1152]{3,1,2,0:T(8,128)}) fusion(f32[16,6,1152]{2,0,1:T(8,128)} %copy-done.2, f32[16,16]{1,0:T(8,128)S(1)} %get-tuple-element.30, f32[16,16,6,960]{3,1,2,0:T(8,128)} %get-tuple-element.26, f32[16,16,6,960]{3,1,2,0:T(8,128)S(1)} %get-tuple-element.25, ...), kind=kLoop, calls=%fused_computation.13 | loop fusion | flops 30074112 | bytes 41021472 | tf_op jit(solution)/shard_map/reduce_sum | solution.py:118
  83.8 2.3 %fusion.30 = (f32[8,16,1,1152]{3,1,2,0:T(8,128)}, f32[8,16,1,1152]{3,1,2,0:T(8,128)}) fusion(f32[16,16,6,1152]{3,1,2,0:T(8,128)} %get-tuple-element.10), kind=kLoop, calls=%fused_computation.68 | loop fusion | bytes 2359296 | tf_op jit(solution)/shard_map/slice | solution.py:46
  86.1 5.7 %fusion.29 = (f32[8,16,5,1152]{3,1,2,0:T(8,128)}, f32[8,16,5,1152]{3,1,2,0:T(8,128)}) fusion(f32[16,16,6,1152]{3,1,2,0:T(8,128)} %get-tuple-element.10), kind=kLoop, calls=%fused_computation.67 | loop fusion | bytes 11796480 | tf_op jit(solution)/shard_map/slice | solution.py:48
  91.8 11.9 %fusion.31 = (f32[16,16,6,1151]{3,1,2,0:T(8,128)}, f32[16,16,6,1151]{3,1,2,0:T(8,128)}) fusion(f32[16,16,6,1152]{3,1,2,0:T(8,128)} %get-tuple-element.10), kind=kLoop, calls=%fused_computation.69 | loop fusion | bytes 28286976 | tf_op jit(solution)/shard_map/slice | solution.py:36
  103.7 3.5 %all-reduce.9 = (f32[6,1152]{1,0:T(8,128)S(1)}, f32[6,1152]{1,0:T(8,128)S(1)}) all-reduce(f32[6,1152]{1,0:T(8,128)S(1)} %get-tuple-element.9, f32[6,1152]{1,0:T(8,128)S(1)} %multiply_reduce_fusion.2), channel_id=1, replica_groups=mesh['space'=4,'dir'=4,'band'=2] {'band'}, use_global_device_ids=true, to_apply=%region_5.6 | all-reduce | flops 13824 | bytes 110592 | tf_op jit(solution)/shard_map/psum | solution.py:54
  107.2 15.4 %all-reduce.8 = (f32[6,1152]{1,0:T(8,128)S(1)}, f32[6,1152]{1,0:T(8,128)S(1)}) all-reduce(f32[6,1152]{1,0:T(8,128)S(1)} %get-tuple-element.6, f32[6,1152]{1,0:T(8,128)S(1)} %get-tuple-element.7), channel_id=1, replica_groups=mesh['space'=4,'dir'=4,'band'=2] {'dir'}, use_global_device_ids=true, to_apply=%region_6.7 | all-reduce | flops 13824 | bytes 110592 | tf_op jit(solution)/shard_map/psum | solution.py:55
  122.6 0.9 broadcast_multiply_fusion
  123.5 1.9 %collective-permute-start.2 = (f32[8,16,1,1152]{3,1,2,0:T(8,128)}, f32[8,16,1,1152]{3,1,2,0:T(8,128)}, u32[]{:S(2)}, u32[]{:S(2)}) collective-permute-start(f32[8,16,1,1152]{3,1,2,0:T(8,128)} %get-tuple-element.13), channel_id=1, source_target_pairs={{8,0},{16,8},{24,16},{9,1},{17,9},{25,17},{10,2},{18,10},{26,18},{... | collective-permute-start | bytes 1769480 | tf_op jit(solution)/shard_map/ppermute | solution.py:15
  125.4 5.0 %collective-permute-start.3 = (f32[8,16,1,1152]{3,1,2,0:T(8,128)}, f32[8,16,1,1152]{3,1,2,0:T(8,128)}, u32[]{:S(2)}, u32[]{:S(2)}) collective-permute-start(f32[8,16,1,1152]{3,1,2,0:T(8,128)} %get-tuple-element.14), channel_id=1, source_target_pairs={{0,8},{8,16},{16,24},{1,9},{9,17},{17,25},{2,10},{10,18},{18,26},{... | collective-permute-start | bytes 1769480 | tf_op jit(solution)/shard_map/ppermute | solution.py:15
  130.4 9.8 %fusion.32 = (f32[16,16,6,960]{3,1,2,0:T(8,128)S(1)}, f32[16,16,6,960]{3,1,2,0:T(8,128)}) fusion(f32[16,16,6,1152]{3,1,2,0:T(8,128)} %get-tuple-element.10), kind=kLoop, calls=%fused_computation.70 | loop fusion | bytes 23592960 | tf_op jit(solution)/shard_map/slice | solution.py:36
  140.2 18.7 %multiply_reduce_fusion = (f32[6,1152]{1,0:T(8,128)S(1)}, f32[6,1152]{1,0:T(8,128)S(1)}, f32[16,16,6,1152]{3,1,2,0:T(8,128)}) fusion(f32[16,16,6,1152]{3,1,2,0:T(8,128)} %param.9, f32[6,1152]{1,0:T(8,128)S(1)} %get-tuple-element.5, f32[16,6,1152]{2,0,1:T(8,128)} %get-tuple-element.27, f32[16,16,6,1152]{3,1,2,0:T(8,128)} %get-tuple-element.10, ...), kind=kLoop, calls=%fused_computation.10 | loop fusion | flops 38914560 | bytes 55674912 | tf_op jit(solution)/shard_map/reduce_sum | solution.py:110
  158.9 3.5 %psum.62 = f32[6,1152]{1,0:T(8,128)S(1)} all-reduce(f32[6,1152]{1,0:T(8,128)S(1)} %add.252), channel_id=1, replica_groups=mesh['space'=4,'dir'=4,'band'=2] {'band'}, use_global_device_ids=true, to_apply=%region_12.13 | all-reduce | flops 6912 | bytes 55296 | tf_op jit(solution)/shard_map/psum | solution.py:54
  162.4 16.0 %psum.63 = f32[6,1152]{1,0:T(8,128)S(1)} all-reduce(f32[6,1152]{1,0:T(8,128)S(1)} %psum.62), channel_id=1, replica_groups=mesh['space'=4,'dir'=4,'band'=2] {'dir'}, use_global_device_ids=true, to_apply=%region_13.14 | all-reduce | flops 6912 | bytes 55296 | tf_op jit(solution)/shard_map/psum | solution.py:55
  (33 shorter events, 3.2 us)
Async XLA Ops:
  0.6 27.4 %copy-start = (f32[4,16]{1,0:T(4,128)S(1)}, f32[4,16]{1,0:T(4,128)}, u32[]{:S(2)}) copy-start(f32[4,16]{1,0:T(4,128)} %param.12) | copy-start | bytes 772
  3.0 66.6 %collective-permute-start = (f32[8,16,1,1152]{3,1,2,0:T(8,128)}, f32[8,16,1,1152]{3,1,2,0:T(8,128)}, u32[]{:S(2)}, u32[]{:S(2)}) collective-permute-start(f32[8,16,1,1152]{3,1,2,0:T(8,128)} %get-tuple-element.21), channel_id=1, source_target_pairs={{8,0},{16,8},{24,16},{9,1},{17,9},{25,17},{10,2},{18,10},{26,18},{... | collective-permute-start | bytes 1769480 | tf_op jit(solution)/shard_map/ppermute | solution.py:15
  5.3 64.2 %collective-permute-start.1 = (f32[8,16,1,1152]{3,1,2,0:T(8,128)}, f32[8,16,1,1152]{3,1,2,0:T(8,128)}, u32[]{:S(2)}, u32[]{:S(2)}) collective-permute-start(f32[8,16,1,1152]{3,1,2,0:T(8,128)} %get-tuple-element.22), channel_id=1, source_target_pairs={{0,8},{8,16},{16,24},{1,9},{9,17},{17,25},{2,10},{10,18},{18,26},{... | collective-permute-start | bytes 1769480 | tf_op jit(solution)/shard_map/ppermute | solution.py:15
  15.5 12.4 %copy-start.4 = (f32[6,1152]{1,0:T(8,128)S(1)}, f32[6,1152]{1,0:T(8,128)}, u32[]{:S(2)}) copy-start(f32[6,1152]{1,0:T(8,128)} %param.10) | copy-start | bytes 82948
  15.5 12.4 %copy-start.5 = (s32[6,1152]{1,0:T(8,128)S(1)}, s32[6,1152]{1,0:T(8,128)}, u32[]{:S(2)}) copy-start(s32[6,1152]{1,0:T(8,128)} %param.11) | copy-start | bytes 82948
  28.0 25.7 %copy-start.7 = (f32[32]{0:T(128)S(1)}, f32[32]{0:T(128)}, u32[]{:S(2)}) copy-start(f32[32]{0:T(128)} %param.14) | copy-start | bytes 388
  29.2 0.8 copy-start.2
  29.9 28.7 %copy-start.3 = (f32[6,1152]{1,0:T(8,128)S(1)}, f32[6,1152]{1,0:T(8,128)}, u32[]{:S(2)}) copy-start(f32[6,1152]{1,0:T(8,128)} %param.15) | copy-start | bytes 82948
  29.9 29.6 %copy-start.6 = (f32[16]{0:T(128)S(1)}, f32[16]{0:T(128)}, u32[]{:S(2)}) copy-start(f32[16]{0:T(128)} %param.13) | copy-start | bytes 196
  123.5 16.7 %collective-permute-start.2 = (f32[8,16,1,1152]{3,1,2,0:T(8,128)}, f32[8,16,1,1152]{3,1,2,0:T(8,128)}, u32[]{:S(2)}, u32[]{:S(2)}) collective-permute-start(f32[8,16,1,1152]{3,1,2,0:T(8,128)} %get-tuple-element.13), channel_id=1, source_target_pairs={{8,0},{16,8},{24,16},{9,1},{17,9},{25,17},{10,2},{18,10},{26,18},{... | collective-permute-start | bytes 1769480 | tf_op jit(solution)/shard_map/ppermute | solution.py:15
  125.4 14.8 %collective-permute-start.3 = (f32[8,16,1,1152]{3,1,2,0:T(8,128)}, f32[8,16,1,1152]{3,1,2,0:T(8,128)}, u32[]{:S(2)}, u32[]{:S(2)}) collective-permute-start(f32[8,16,1,1152]{3,1,2,0:T(8,128)} %get-tuple-element.14), channel_id=1, source_target_pairs={{0,8},{8,16},{16,24},{1,9},{9,17},{17,25},{2,10},{10,18},{18,26},{... | collective-permute-start | bytes 1769480 | tf_op jit(solution)/shard_map/ppermute | solution.py:15
  140.2 38.8 %copy-start.1 = (f32[4,16]{1,0:T(4,128)S(1)}, f32[4,16]{1,0:T(4,128)}, u32[]{:S(2)}) copy-start(f32[4,16]{1,0:T(4,128)} %param.12) | copy-start | bytes 772
where the time goes:
time: 181 us; the launch traced here: 179 us
  local copies, waits for them, and re-layouts  61 us (34%)
  blocking collectives  58.4 us (32%)
  other arithmetic  43.4 us (24%)
  starting transfers between devices  13.5 us (7%)
    psum x3, blocking collectives, reduce_volumes(): summed = lax.psum(summed, 'dir')  48 us
    slice x4, local copies, waits for them, and re-layouts, plane_move(): rest = lax.slice_in_dim(field, offset, size, axis=last)  44.1 us
    reduce_sum x1, other arithmetic, on_device(): jnp.sum(relaxation_slope[None] * dual_intensity * (primal_deviations - cr...  18.7 us
    reduce_sum x1, other arithmetic, on_device(): jnp.sum(relaxation_frequency[None] * dual_intensity, axis=(0, 1))  14.2 us
    ppermute x4, starting transfers between devices, passed_along(): lax.ppermute(value, axis, [(source, source + steps) for source in range(l...  13.5 us
    slice x2, local copies, waits for them, and re-layouts, first_neighbours(): dual_intensity[:half, :, 1:]  11.5 us
    psum x3, blocking collectives, reduce_volumes(): summed = lax.psum(partials, 'band')  10.4 us
    slice x2, local copies, waits for them, and re-layouts, first_neighbours(): edge_ahead = passed_along(dual_intensity[:half, :, :1], 'space', -1)  4.67 us
  transfers between devices with their start and end apart: 4, of which 0 were waited for; matrix products, arithmetic and copies ran while one was open for 27% of the time, Pallas kernels for 0%

commit v1 on v0

v1 whole, which is shorter than its diff:
```python
import math

import jax
import jax.numpy as jnp
import numpy as np
from jax import lax
from jax.experimental import pallas as pl
from jax.experimental.pallas import tpu as pltpu
from jax.sharding import PartitionSpec as P

NDIR = 64
NB = 32
NY = 192
ITERS = 2
LANES = 128
SUB = 8
PAIR = 2
VMEM_LIMIT = 40 * 1024 * 1024


def direction_table(count):
    d = np.arange(NDIR)
    half = count // 2
    block, slot = d // count, d % count
    side, pair = slot // half, slot % half
    azimuth = np.pi * (block * half + pair + 0.5) / (NDIR // 2) - np.pi / 2
    along_z = 0.4 * (1.0 - 2.0 * (pair % 2))
    tilt = np.sqrt(1.0 - along_z * along_z)
    along_x = (1.0 - 2.0 * side) * tilt * np.cos(azimuth)
    along_y = tilt * np.sin(azimuth)
    return np.stack([along_x, along_y, along_z], axis=1).astype(np.float32).reshape(-1)


def lane_ids():
    return lax.broadcasted_iota(jnp.int32, (SUB, LANES), 1)


def shift_ahead(v, offset, lane, masked=None):
    n = len(v)
    q, rem = divmod(offset, LANES)
    zero = jnp.zeros((SUB, LANES), jnp.float32)
    rolled = [pltpu.roll(t, LANES - rem, 1) if rem and j >= q else t for j, t in enumerate(v)]
    out = []
    for j in range(n):
        near = rolled[j + q] if j + q < n else None
        far = rolled[j + q + 1] if rem and j + q + 1 < n else None
        bad = [k for k in range(LANES) if masked is not None and masked(j * LANES + k)]
        if rem and far is not None and all(k in bad for k in range(LANES - rem, LANES)):
            far, bad = None, [k for k in bad if k < LANES - rem]
        if near is None:
            out.append(None)
            continue
        t = near
        if rem:
            t = jnp.where(lane < LANES - rem, near, zero if far is None else far)
        for k in bad:
            if not (rem and far is None and k >= LANES - rem):
                t = jnp.where(lane == k, zero, t)
        out.append(t)
    return out


def shift_behind(v, offset, lane, masked=None):
    n = len(v)
    q, rem = divmod(offset, LANES)
    zero = jnp.zeros((SUB, LANES), jnp.float32)
    rolled = [pltpu.roll(t, rem, 1) if rem and j + q < n else t for j, t in enumerate(v)]
    out = []
    for j in range(n):
        near = rolled[j - q] if j - q >= 0 else None
        far = rolled[j - q - 1] if rem and j - q - 1 >= 0 else None
        bad = [k for k in range(LANES) if masked is not None and masked(j * LANES + k)]
        if rem and far is not None and all(k in bad for k in range(rem)):
            far, bad = None, [k for k in bad if k >= rem]
        if near is None:
            out.append(None)
            continue
        t = near
        if rem:
            t = jnp.where(lane >= rem, near, zero if far is None else far)
        for k in bad:
            if not (rem and far is None and k < rem):
                t = jnp.where(lane == k, zero, t)
        out.append(t)
    return out


def shift_y(v, rising, lane):
    if rising:
        return shift_ahead(v, 1, lane, lambda p: p % NY == NY - 1)
    return shift_behind(v, 1, lane, lambda p: p % NY == 0)


def shift_z(v, rising, lane):
    return shift_ahead(v, NY, lane) if rising else shift_behind(v, NY, lane)


def inverse(x):
    r = pl.reciprocal(x, approx=True)
    return r * (2.0 - x * r)


def column(row, offset, n):
    shape = (n, row.shape[1])
    i0 = lax.broadcasted_iota(jnp.int32, shape, 0)
    i1 = lax.broadcasted_iota(jnp.int32, shape, 1)
    picked = jnp.sum(jnp.where(i1 == i0 + offset, row, 0.0), axis=1, keepdims=True)
    return jnp.broadcast_to(picked, (n, LANES))


def fill_columns(cols, heat, speed, table):
    nb = cols.shape[1]
    row = heat[...]
    total = jnp.sum(row, axis=1, keepdims=True) * float(NDIR)
    cols[0] = column(speed[...], 0, nb)
    cols[1] = column(row / total, lax.axis_index("band") * nb, nb)
    for m in range(table.shape[0]):
        cols[2 + m] = column(table[m : m + 1], 0, nb)


def base_tile(cols, material, hs):
    base = jnp.broadcast_to(cols[2, hs], (SUB, LANES))
    for m in range(1, cols.shape[0] - 2):
        base = jnp.where(material == m, cols[2 + m, hs], base)
    return base


def halves(nb):
    return [slice(h * SUB, (h + 1) * SUB) for h in range(nb // SUB)]


def tiles(plane):
    return [slice(j * LANES, (j + 1) * LANES) for j in range(plane // LANES)]


def sub_sum(t):
    return jnp.sum(t, axis=0, keepdims=True)


def add_terms(terms):
    terms = [t for t in terms if t is not None]
    total = terms[0]
    for t in terms[1:]:
        total = total + t
    return total


def times(a, b):
    return None if b is None else a * b


def cosines(dirs, d):
    at = 3 * d
    return dirs[at], dirs[at + 1], dirs[at + 2]


def faces_kernel(heat, speed, table, density, material, objective, up0, down0, down1, up1, out_ahead, out_behind, cols):
    fill_columns(cols, heat, speed, table)
    half, _, nb, plane = up0.shape
    last = density.shape[0] - 1
    for own, other, x, out in ((up0, down0, 0, out_ahead), (down1, up1, last, out_behind)):

        def copy(d, total):
            out[pl.ds(pl.multiple_of(d * nb, nb), nb)] = own[d, 0]
            return total + (own[d, 0] + other[d, 0])

        total = lax.fori_loop(0, half, copy, jnp.zeros((nb, plane), jnp.float32))
        base = half * nb
        for cs in tiles(plane):
            share = 0.0
            for hs in halves(nb):
                rate = base_tile(cols, material[x : x + 1, cs], hs) * (0.2 + 0.8 * density[x : x + 1, cs])
                share = share + rate * total[hs, cs]
            out[base : base + 1, cs] = sub_sum(share)
        out[base + 1 : base + 2] = density[x : x + 1]
        out[base + 2 : base + 3] = material[x : x + 1].astype(jnp.float32)
        out[base + 3 : base + 4] = objective[x : x + 1]
        out[base + 4 : base + 8] = jnp.zeros((4, plane), jnp.float32)


def first_kernel(
    dirs, heat, speed, table, density, material, field, excess, flow, face_ahead, face_behind, sums, cols, rate, acc
):
    g = pl.program_id(0)
    steps = pl.num_programs(0)
    _, nx, nb, plane = field.shape
    cuts, bands = tiles(plane), halves(nb)

    @pl.when(g == 0)
    def _():
        fill_columns(cols, heat, speed, table)
        for x in range(nx):
            for cs in cuts:
                factor = 0.2 + 0.8 * density[x : x + 1, cs]
                for hs in bands:
                    rate[x, hs, cs] = base_tile(cols, material[x : x + 1, cs], hs) * factor
        acc[...] = jnp.zeros_like(acc)

    block = lax.axis_index("dir")
    count = steps * PAIR
    first = block * count + g * PAIR
    ahead = g < steps // 2
    lane = lane_ids()

    def run(rising):
        def layer(x, _):
            edge = jnp.where(ahead, x == nx - 1, x == 0)
            beside = jnp.where(edge, x, jnp.where(ahead, x + 1, x - 1))
            for hs in bands:
                pace = cols[0, hs]
                rates = [rate[x, hs, cs] for cs in cuts]
                kept = [[] for _ in cuts]
                for dd in range(PAIR):
                    ax, ay, az = [jnp.abs(a) for a in cosines(dirs, first + dd)]
                    cx, cy, cz = pace * jnp.where(edge, 0.0, ax), pace * ay, pace * az
                    speeds = pace * (ax + ay + az)
                    v = [field[dd, x, hs, cs] for cs in cuts]
                    along_y = shift_y(v, rising, lane)
                    along_z = shift_z(v, dd == 0, lane)
                    for j, cs in enumerate(cuts):
                        inv = inverse(speeds + rates[j])
                        near = add_terms(
                            [times(cx, field[dd, beside, hs, cs]), times(cy, along_y[j]), times(cz, along_z[j])]
                        )
                        a = near * inv
                        flow[dd, x, hs, cs] = a
                        kept[j].append((v[j], excess[dd, x, hs, cs], a, inv))
                for j, cs in enumerate(cuts):
                    for f in range(4):
                        acc[f, x, hs, cs] += add_terms([k[f] for k in kept[j]])
            return 0

        lax.fori_loop(0, nx, layer, 0)

    rises = cosines(dirs, first)[1] > 0
    pl.when(rises)(lambda: run(True))
    pl.when(jnp.logical_not(rises))(lambda: run(False))

    @pl.when(ahead)
    def _():
        for dd in range(PAIR):
            face_ahead[dd * nb : (dd + 1) * nb] = flow[dd, 0]

    @pl.when(jnp.logical_not(ahead))
    def _():
        for dd in range(PAIR):
            face_behind[dd * nb : (dd + 1) * nb] = flow[dd, nx - 1]

    @pl.when(g == steps - 1)
    def _():
        for x in range(nx):
            for cs in cuts:
                totals = [0.0] * 4
                for hs in bands:
                    r, w = rate[x, hs, cs], cols[1, hs]
                    for f, scale in enumerate((r, w, r, r * w)):
                        totals[f] = totals[f] + scale * acc[f, x, hs, cs]
                for f in range(4):
                    sums[f * nx + x : f * nx + x + 1, cs] = sub_sum(totals[f])
        sums[4 * nx :] = jnp.zeros((sums.shape[0] - 4 * nx, plane), jnp.float32)


def edges_kernel(dirs, heat, speed, table, density, material, from_ahead, from_behind, sums, out, cols):
    fill_columns(cols, heat, speed, table)
    nx, plane = density.shape
    nb = cols.shape[1]
    half = (from_ahead.shape[0] - SUB) // nb
    count = 2 * half
    block = lax.axis_index("dir")
    out[...] = sums[...]
    cuts = tiles(plane)
    for side, (halo, x) in enumerate(((from_ahead, nx - 1), (from_behind, 0))):
        rates = []
        for hs in halves(nb):
            rates.append(
                [base_tile(cols, material[x : x + 1, cs], hs) * (0.2 + 0.8 * density[x : x + 1, cs]) for cs in cuts]
            )

        def add(d, totals):
            ax, ay, az = [jnp.abs(a) for a in cosines(dirs, block * count + side * half + d)]
            new = list(totals)
            for h, hs in enumerate(halves(nb)):
                pace = cols[0, hs]
                cx, speeds = pace * ax, pace * (ax + ay + az)
                rows = halo.at[pl.ds(pl.multiple_of(d * nb + h * SUB, SUB), SUB)]
                for j, cs in enumerate(cuts):
                    r = rates[h][j]
                    new[j] = new[j] + (cx * rows[:, cs]) * (r * inverse(speeds + r))
            return tuple(new)

        totals = lax.fori_loop(0, half, add, tuple(jnp.zeros((SUB, LANES), jnp.float32) for _ in cuts))
        row = 2 * nx + x
        for j, cs in enumerate(cuts):
            out[row : row + 1, cs] = out[row : row + 1, cs] + sub_sum(totals[j])
        out[4 * nx + side : 4 * nx + side + 1] = halo[half * nb : half * nb + 1]


def second_kernel(
    dirs, heat, speed, table, density, material, objective,
    sum0, sum1, sum2, sum3, params_ahead, params_behind, halo0_ahead, halo0_behind, halo1_ahead, halo1_behind,
    flow, excess, dual, gradient,
    cols, rate, source0, source1, warm, prev, seed, acc,
):
    g = pl.program_id(0)
    steps = pl.num_programs(0)
    _, nx, nb, plane = flow.shape
    cuts, bands = tiles(plane), halves(nb)
    scale = float(NDIR * NB)

    @pl.when(g == 0)
    def _():
        fill_columns(cols, heat, speed, table)
        total = (sum0[...] + sum1[...]) + (sum2[...] + sum3[...])
        for x in range(nx):
            warm[x] = jnp.broadcast_to(total[nx + x : nx + x + 1], (SUB, plane))
        for x in range(nx + 2):
            for cs in cuts:
                if x < nx:
                    dens, mat = density[x : x + 1, cs], material[x : x + 1, cs]
                    drive = total[x : x + 1, cs] + scale * objective[x : x + 1, cs]
                    again = (
                        total[2 * nx + x : 2 * nx + x + 1, cs]
                        + drive * total[3 * nx + x : 3 * nx + x + 1, cs]
                        + scale * objective[x : x + 1, cs]
                    )
                else:
                    params = params_ahead if x == nx else params_behind
                    dens, mat = params[1:2, cs], params[2:3, cs].astype(jnp.int32)
                    drive = total[3 * nx + x : 3 * nx + x + 1, cs] + scale * params[3:4, cs]
                factor = 0.2 + 0.8 * dens
                for hs in bands:
                    w = cols[1, hs]
                    rate[x, hs, cs] = base_tile(cols, mat, hs) * factor
                    source0[x, hs, cs] = w * drive
                    if x < nx:
                        source1[x, hs, cs] = w * again
        acc[...] = jnp.zeros_like(acc)

    block = lax.axis_index("dir")
    count = steps * PAIR
    first = block * count + g * PAIR
    ahead = g < steps // 2
    lane = lane_ids()

    def enter(halo0, halo1, x):
        for dd in range(PAIR):
            ax, ay, az = [jnp.abs(a) for a in cosines(dirs, first + dd)]
            for h, hs in enumerate(bands):
                pace = cols[0, hs]
                speeds, cx = pace * (ax + ay + az), pace * ax
                rows = slice(dd * nb + h * SUB, dd * nb + (h + 1) * SUB)
                for cs in cuts:
                    prev[dd, hs, cs] = halo1[rows, cs] + source0[x, hs, cs] * inverse(speeds + rate[x, hs, cs])
                    seed[dd, hs, cs] = cx * halo0[rows, cs]

    pl.when(ahead)(lambda: enter(halo0_ahead, halo1_ahead, nx))
    pl.when(jnp.logical_not(ahead))(lambda: enter(halo0_behind, halo1_behind, nx + 1))

    def run(rising):
        def layer(i, at_edge):
            x = jnp.where(ahead, nx - 1 - i, i)
            for hs in bands:
                pace = cols[0, hs]
                rates = [rate[x, hs, cs] for cs in cuts]
                kept = [[] for _ in cuts]
                for dd in range(PAIR):
                    ax, ay, az = [jnp.abs(a) for a in cosines(dirs, first + dd)]
                    cx, cy, cz = pace * ax, pace * ay, pace * az
                    speeds = pace * (ax + ay + az)
                    inv = [inverse(speeds + rates[j]) for j in range(len(cuts))]
                    v = []
                    for j, cs in enumerate(cuts):
                        s = source0[x, hs, cs]
                        if at_edge:
                            s = s + seed[dd, hs, cs]
                        v.append(flow[dd, x, hs, cs] + s * inv[j])
                    along_y = shift_y(v, rising, lane)
                    along_z = shift_z(v, dd == 0, lane)
                    for j, cs in enumerate(cuts):
                        near = add_terms([
                            times(cx, prev[dd, hs, cs]), times(cy, along_y[j]), times(cz, along_z[j]), source1[x, hs, cs]
                        ])
                        new = near * inv[j]
                        prev[dd, hs, cs] = v[j]
                        dual[dd, x, hs, cs] = new
                        kept[j].append((v[j] + new) * (excess[dd, x, hs, cs] - warm[x, :, cs]))
                for j, cs in enumerate(cuts):
                    acc[x, hs, cs] += add_terms(kept[j])

        layer(0, True)

        def later(i, _):
            layer(i, False)
            return 0

        lax.fori_loop(1, nx, later, 0)

    rises = cosines(dirs, first)[1] > 0
    pl.when(rises)(lambda: run(True))
    pl.when(jnp.logical_not(rises))(lambda: run(False))

    @pl.when(g == steps - 1)
    def _():
        for x in range(nx):
            for cs in cuts:
                total = 0.0
                for hs in bands:
                    total = total + base_tile(cols, material[x : x + 1, cs], hs) * acc[x, hs, cs]
                gradient[x : x + 1, cs] = sub_sum(total) * 0.8


def passed_along(value, steps):
    count = lax.axis_size("space")
    return lax.ppermute(value, "space", [(s, s + steps) for s in range(count) if 0 <= s + steps < count])


def shares(partial):
    size = lax.axis_size("band")
    total = partial
    for k in range(1, size):
        total = total + lax.ppermute(partial, "band", [(s, (s + k) % size) for s in range(size)])
    count = lax.axis_size("dir")
    pairs = count & (count - 1) == 0
    hops = [[(s, s ^ k if pairs else (s + k) % count) for s in range(count)] for k in range(1, count)]
    return [total] + [lax.ppermute(total, "dir", hop) for hop in hops]


def whole(array):
    return pl.BlockSpec(array.shape, lambda *g: (0,) * array.ndim)


def on_device(
    adjoint_start, primal_deviations, density, material, rate_table, group_speed, heat_capacity, objective_weight
):
    count, nb, nx, plane = adjoint_start.shape
    half = count // 2
    steps = count // PAIR
    nmat = rate_table.shape[0]
    start = adjoint_start.transpose(0, 2, 1, 3)
    excess = primal_deviations.transpose(0, 2, 1, 3)
    f32 = jnp.float32
    smem = pl.BlockSpec(memory_space=pltpu.SMEM)
    dirs = jnp.asarray(direction_table(count))
    heat = heat_capacity.reshape(1, -1)
    speed = group_speed.reshape(1, -1)
    tables = (heat, speed, rate_table)
    cells = (density, material)
    cols = pltpu.VMEM((2 + nmat, nb, LANES), f32)
    params = pltpu.CompilerParams(vmem_limit_bytes=VMEM_LIMIT)
    size = count * nb * nx * plane

    def face(d, x):
        return pl.BlockSpec((half, 1, nb, plane), lambda g: (d, x, 0, 0))

    rows = half * nb + SUB
    small = (*tables, *cells, objective_weight)
    to_behind, to_ahead = pl.pallas_call(
        faces_kernel,
        grid=(1,),
        out_shape=(jax.ShapeDtypeStruct((rows, plane), f32),) * 2,
        in_specs=[whole(a) for a in small] + [face(0, 0), face(1, 0), face(1, nx - 1), face(0, nx - 1)],
        out_specs=[pl.BlockSpec((rows, plane), lambda g: (0, 0))] * 2,
        scratch_shapes=[cols],
        compiler_params=params,
        cost_estimate=pl.CostEstimate(flops=size // 3, bytes_accessed=size * 2, transcendentals=0),
        name="faces",
    )(*small, start, start, start, start)
    halo0_ahead = passed_along(to_behind, -1)
    halo0_behind = passed_along(to_ahead, 1)

    group = pl.BlockSpec((PAIR, nx, nb, plane), lambda g: (g, 0, 0, 0))
    early = pl.BlockSpec((PAIR * nb, plane), lambda g: (jnp.minimum(g, steps // 2 - 1), 0))
    late = pl.BlockSpec((PAIR * nb, plane), lambda g: (jnp.maximum(g - steps // 2, 0), 0))
    sum_rows = -(-(4 * nx + 2) // SUB) * SUB
    small = (*tables, *cells)
    flow, face_ahead, face_behind, sums = pl.pallas_call(
        first_kernel,
        grid=(steps,),
        out_shape=(
            jax.ShapeDtypeStruct(start.shape, f32),
            jax.ShapeDtypeStruct((half * nb, plane), f32),
            jax.ShapeDtypeStruct((half * nb, plane), f32),
            jax.ShapeDtypeStruct((sum_rows, plane), f32),
        ),
        in_specs=[smem] + [whole(a) for a in small] + [group, group],
        out_specs=[group, early, late, pl.BlockSpec((sum_rows, plane), lambda g: (0, 0))],
        scratch_shapes=[cols, pltpu.VMEM((nx, nb, plane), f32), pltpu.VMEM((4, nx, nb, plane), f32)],
        compiler_params=params,
        cost_estimate=pl.CostEstimate(flops=size * 20, bytes_accessed=size * 12, transcendentals=size),
        name="first",
    )(dirs, *small, start, excess)
    halo1_ahead = passed_along(face_ahead, -1)
    halo1_behind = passed_along(face_behind, 1)

    sums = pl.pallas_call(
        edges_kernel,
        out_shape=jax.ShapeDtypeStruct(sums.shape, f32),
        in_specs=[smem] + [pl.BlockSpec(memory_space=pltpu.VMEM)] * (len(small) + 3),
        out_specs=pl.BlockSpec(memory_space=pltpu.VMEM),
        scratch_shapes=[cols],
        compiler_params=params,
        cost_estimate=pl.CostEstimate(flops=size, bytes_accessed=size, transcendentals=0),
        name="edges",
    )(dirs, *small, halo0_ahead, halo0_behind, sums)
    parts = shares(sums)
    parts = parts[:3] + [sum(parts[3:], jnp.zeros_like(sums))] if len(parts) > 4 else parts + [jnp.zeros_like(sums)] * (4 - len(parts))

    small = (*tables, *cells, objective_weight, *parts)
    tail = pl.BlockSpec((SUB, plane), lambda g: (half * nb // SUB, 0))
    dual, gradient = pl.pallas_call(
        second_kernel,
        grid=(steps,),
        out_shape=(jax.ShapeDtypeStruct(start.shape, f32), jax.ShapeDtypeStruct((nx, plane), f32)),
        in_specs=[smem] + [whole(a) for a in small] + [tail, tail, early, late, early, late, group, group],
        out_specs=[group, pl.BlockSpec((nx, plane), lambda g: (0, 0))],
        scratch_shapes=[
            cols,
            pltpu.VMEM((nx + 2, nb, plane), f32),
            pltpu.VMEM((nx + 2, nb, plane), f32),
            pltpu.VMEM((nx, nb, plane), f32),
            pltpu.VMEM((nx, SUB, plane), f32),
            pltpu.VMEM((PAIR, nb, plane), f32),
            pltpu.VMEM((PAIR, nb, plane), f32),
            pltpu.VMEM((nx, nb, plane), f32),
        ],
        compiler_params=params,
        cost_estimate=pl.CostEstimate(flops=size * 30, bytes_accessed=size * 12, transcendentals=size),
        name="second",
    )(dirs, *small, halo0_ahead, halo0_behind, halo0_ahead, halo0_behind, halo1_ahead, halo1_behind, flow, excess)
    gradient = sum(shares(gradient)) * (-0.125 / ITERS)
    return (dual.transpose(0, 2, 1, 3), gradient)


def solution(mesh):
    placed = (
        P("dir", "band", "space", None),
        P("dir", "band", "space", None),
        P("space", None),
        P("space", None),
        P(None, "band"),
        P("band"),
        P(),
        P("space", None),
    )
    return jax.shard_map(
        on_device,
        mesh=mesh,
        in_specs=placed,
        out_specs=(P("dir", "band", "space", None), P("space", None)),
        check_vma=False,
    )
```

time: 181 us -> 69.3 us (0.38)
  the two profiles are of different devices: /device:TPU:16 before, /device:TPU:0 now
where the time goes in v1:
time: 69.3 us; the launch traced here: 68.5 us
  Pallas kernels  26.9 us (39%)
  starting transfers between devices  19.9 us (29%)
  waiting for transfers between devices  13 us (19%)
  local copies, waits for them, and re-layouts  7.31 us (11%)
  between operations  0.75 us (1%)
    pallas_call x1, Pallas kernels, on_device(): pl.pallas_call(second_kernel, grid=(steps,), out_shape=(jax.ShapeDtypeStr...  13.3 us
    ppermute x4, starting transfers between devices, passed_along(): lax.ppermute(value, 'space', [(s, s + steps) for s in range(count) if 0 <...  12.8 us
    pallas_call x1, Pallas kernels, on_device(): pl.pallas_call(first_kernel, grid=(steps,), out_shape=(jax.ShapeDtypeStru...  11.7 us
    unnamed x18, local copies, waits for them, and re-layouts  7.31 us
    ppermute x6, starting transfers between devices, shares(): return [total] + [lax.ppermute(total, 'dir', hop) for hop in hops]  7.09 us
    ppermute x4, waiting for transfers between devices, passed_along(): lax.ppermute(value, 'space', [(s, s + steps) for s in range(count) if 0 <...  5.46 us
    ppermute x6, waiting for transfers between devices, shares(): return [total] + [lax.ppermute(total, 'dir', hop) for hop in hops]  4.94 us
    ppermute x2, waiting for transfers between devices, shares(): lax.ppermute(partial, 'band', [(s, (s + k) % size) for s in range(size)])  2.57 us
  transfers between devices with their start and end apart: 12, of which 9 were waited for; matrix products, arithmetic and copies ran while one was open for 0% of the time, Pallas kernels for 19%

profile of v1, /device:TPU:0, one launch (start us, length us, event | category | flops | bytes accessed | tf_op | source)
XLA Modules:
  0.0 68.5 jit_solution(13490692314342738825)
XLA Ops:
  0.6 3.0 %copy-done = f32[16,16,6,1152]{3,1,2,0:T(8,128)S(1)} copy-done((f32[16,16,6,1152]{3,1,2,0:T(8,128)S(1)}, f32[16,16,6,1152]{3,1,2,0:T(8,128)}, u32[]{:S(2)}) %copy-start) | copy-done | bytes 7077912
  3.6 0.8 %copy-done.1 = f32[6,1152]{1,0:T(8,128)S(1)} copy-done((f32[6,1152]{1,0:T(8,128)S(1)}, f32[6,1152]{1,0:T(8,128)}, u32[]{:S(2)}) %copy-start.1) | copy-done | bytes 27672
  4.4 0.8 %copy-done.2 = s32[6,1152]{1,0:T(8,128)S(1)} copy-done((s32[6,1152]{1,0:T(8,128)S(1)}, s32[6,1152]{1,0:T(8,128)}, u32[]{:S(2)}) %copy-start.2) | copy-done | bytes 27672
  5.2 0.8 %copy-done.3 = f32[6,1152]{1,0:T(8,128)S(1)} copy-done((f32[6,1152]{1,0:T(8,128)S(1)}, f32[6,1152]{1,0:T(8,128)}, u32[]{:S(2)}) %copy-start.3) | copy-done | bytes 27672
  6.0 0.7 copy-done.5
  6.6 0.7 copy-done.7
  8.4 1.3 %collective-permute-start = (f32[136,1152]{1,0:T(8,128)S(1)}, f32[136,1152]{1,0:T(8,128)S(1)}, u32[]{:S(2)}, u32[]{:S(2)}) collective-permute-start(f32[136,1152]{1,0:T(8,128)S(1)} %get-tuple-element.10), channel_id=1, source_target_pairs={{8,0},{16,8},{24,16},{9,1},{17,9},{25,17},{10,2},{18,10},{26,18},{... | collective-permute-start | bytes 1880072 | tf_op jit(solution)/shard_map/ppermute | solution.py:414
  9.7 5.6 %collective-permute-start.1 = (f32[136,1152]{1,0:T(8,128)S(1)}, f32[136,1152]{1,0:T(8,128)S(1)}, u32[]{:S(2)}, u32[]{:S(2)}) collective-permute-start(f32[136,1152]{1,0:T(8,128)S(1)} %get-tuple-element.11), channel_id=1, source_target_pairs={{0,8},{8,16},{16,24},{1,9},{9,17},{17,25},{2,10},{10,18},{18,26},{... | collective-permute-start | bytes 1880072 | tf_op jit(solution)/shard_map/ppermute | solution.py:414
  15.4 11.7 %first.1 = (f32[16,6,16,1152]{3,2,1,0:T(8,128)S(1)}, f32[128,1152]{1,0:T(8,128)S(1)}, f32[128,1152]{1,0:T(8,128)S(1)}, f32[32,1152]{1,0:T(8,128)S(1)}) custom-call(f32[192]{0:T(256)S(1)} %copy-done.6, f32[1,32]{1,0:T(1,128)S(1)} %bitcast.11, f32[1,16]{1,0:T(1,128)S(1)} %bitcast.15, f32[4,16]{1,0:T(4,128)S(1)} %copy-done.5, f32[6,1152]{1,0:T(8,128)S(1)} %copy-done.1, ...), custom_call_target="tpu_custom_call" | custom-call | flops 35389440 | bytes 21233664 | tf_op jit(solution)/shard_map/first/pallas_call | solution.py:476
  27.0 1.3 %collective-permute-start.6 = (f32[128,1152]{1,0:T(8,128)S(1)}, f32[128,1152]{1,0:T(8,128)S(1)}, u32[]{:S(2)}, u32[]{:S(2)}) collective-permute-start(f32[128,1152]{1,0:T(8,128)S(1)} %get-tuple-element.13), channel_id=1, source_target_pairs={{8,0},{16,8},{24,16},{9,1},{17,9},{25,17},{10,2},{18,10},{26,18},{... | collective-permute-start | bytes 1769480 | tf_op jit(solution)/shard_map/ppermute | solution.py:414
  28.3 4.6 %collective-permute-start.7 = (f32[128,1152]{1,0:T(8,128)S(1)}, f32[128,1152]{1,0:T(8,128)S(1)}, u32[]{:S(2)}, u32[]{:S(2)}) collective-permute-start(f32[128,1152]{1,0:T(8,128)S(1)} %get-tuple-element.14), channel_id=1, source_target_pairs={{0,8},{8,16},{16,24},{1,9},{9,17},{17,25},{2,10},{10,18},{18,26},{... | collective-permute-start | bytes 1769480 | tf_op jit(solution)/shard_map/ppermute | solution.py:414
  33.0 1.4 %edges.1 = f32[32,1152]{1,0:T(8,128)S(1)} custom-call(f32[192]{0:T(256)S(1)} %copy-done.6, f32[1,32]{1,0:T(1,128)S(1)} %bitcast.12, f32[1,16]{1,0:T(1,128)S(1)} %bitcast.16, f32[4,16]{1,0:T(4,128)S(1)} %copy-done.5, f32[6,1152]{1,0:T(8,128)S(1)} %copy-done.1, s32[6,1152]{1,0:T(8,128)S(1)} %copy-done.2, ...), custom_call_target="tpu_custom_call" | custom-call | flops 1769472 | bytes 1769472 | tf_op jit(solution)/shard_map/edges/pallas_call | solution.py:495
  34.5 1.4 %collective-permute-done.2 = f32[32,1152]{1,0:T(8,128)S(1)} collective-permute-done((f32[32,1152]{1,0:T(8,128)S(1)}, f32[32,1152]{1,0:T(8,128)S(1)}, u32[]{:S(2)}, u32[]{:S(2)}) %collective-permute-start.2) | collective-permute-done | bytes 147488 | tf_op jit(solution)/shard_map/ppermute | solution.py:421
  35.8 3.0 %collective-permute-start.5 = (f32[32,1152]{1,0:T(8,128)S(1)}, f32[32,1152]{1,0:T(8,128)S(1)}, u32[]{:S(2)}, u32[]{:S(2)}) collective-permute-start(f32[32,1152]{1,0:T(8,128)S(1)} %add.15.sum0), channel_id=1, source_target_pairs={{0,6},{2,4},{4,2},{6,0},{1,7},{3,5},{5,3},{7,1},{8,14},{10,12},{12... | collective-permute-start | bytes 442376 | tf_op jit(solution)/shard_map/ppermute | solution.py:425
  39.4 4.3 %collective-permute-done.6.halo1_ahead = f32[128,1152]{1,0:T(8,128)S(1)} collective-permute-done((f32[128,1152]{1,0:T(8,128)S(1)}, f32[128,1152]{1,0:T(8,128)S(1)}, u32[]{:S(2)}, u32[]{:S(2)}) %collective-permute-start.6) | collective-permute-done | bytes 589856 | tf_op jit(solution)/shard_map/ppermute | solution.py:414
  43.7 1.2 %collective-permute-done.7.halo1_behind = f32[128,1152]{1,0:T(8,128)S(1)} collective-permute-done((f32[128,1152]{1,0:T(8,128)S(1)}, f32[128,1152]{1,0:T(8,128)S(1)}, u32[]{:S(2)}, u32[]{:S(2)}) %collective-permute-start.7) | collective-permute-done | bytes 589856 | tf_op jit(solution)/shard_map/ppermute | solution.py:414
  44.9 1.2 %collective-permute-done.4.sum2 = f32[32,1152]{1,0:T(8,128)S(1)} collective-permute-done((f32[32,1152]{1,0:T(8,128)S(1)}, f32[32,1152]{1,0:T(8,128)S(1)}, u32[]{:S(2)}, u32[]{:S(2)}) %collective-permute-start.4) | collective-permute-done | bytes 147488 | tf_op jit(solution)/shard_map/ppermute | solution.py:425
  46.4 13.3 %second.1 = (f32[16,6,16,1152]{3,2,1,0:T(8,128)}, f32[6,1152]{1,0:T(8,128)S(1)}) custom-call(f32[192]{0:T(256)S(1)} %copy-done.6, f32[1,32]{1,0:T(1,128)S(1)} %bitcast.13, f32[1,16]{1,0:T(1,128)S(1)} %bitcast.17, f32[4,16]{1,0:T(4,128)S(1)} %copy-done.5, f32[6,1152]{1,0:T(8,128)S(1)} %copy-done.1, s32[6,1152]{1,0:T(8,128)S(1)} %copy-done.2, ...), custom_call_target="tpu_custom_call" | custom-call | flops 53084160 | bytes 21233664 | tf_op jit(solution)/shard_map/second/pallas_call | solution.py:510
  59.7 1.2 %collective-permute-done.8 = f32[6,1152]{1,0:T(8,128)S(1)} collective-permute-done((f32[6,1152]{1,0:T(8,128)S(1)}, f32[6,1152]{1,0:T(8,128)S(1)}, u32[]{:S(2)}, u32[]{:S(2)}) %collective-permute-start.8) | collective-permute-done | bytes 27680 | tf_op jit(solution)/shard_map/ppermute | solution.py:421
  60.9 1.6 %collective-permute-start.11 = (f32[6,1152]{1,0:T(8,128)S(1)}, f32[6,1152]{1,0:T(8,128)S(1)}, u32[]{:S(2)}, u32[]{:S(2)}) collective-permute-start(f32[6,1152]{1,0:T(8,128)S(1)} %add.16), channel_id=1, source_target_pairs={{0,6},{2,4},{4,2},{6,0},{1,7},{3,5},{5,3},{7,1},{8,14},{10,12},{12... | collective-permute-start | bytes 82952 | tf_op jit(solution)/shard_map/ppermute | solution.py:425
  62.5 1.4 %collective-permute-start.10 = (f32[6,1152]{1,0:T(8,128)S(1)}, f32[6,1152]{1,0:T(8,128)S(1)}, u32[]{:S(2)}, u32[]{:S(2)}) collective-permute-start(f32[6,1152]{1,0:T(8,128)S(1)} %add.16), channel_id=1, source_target_pairs={{0,4},{2,6},{4,0},{6,2},{1,5},{3,7},{5,1},{7,3},{8,12},{10,14},{12... | collective-permute-start | bytes 82952 | tf_op jit(solution)/shard_map/ppermute | solution.py:425
  64.4 1.4 %collective-permute-done.11 = f32[6,1152]{1,0:T(8,128)S(1)} collective-permute-done((f32[6,1152]{1,0:T(8,128)S(1)}, f32[6,1152]{1,0:T(8,128)S(1)}, u32[]{:S(2)}, u32[]{:S(2)}) %collective-permute-start.11) | collective-permute-done | bytes 27680 | tf_op jit(solution)/shard_map/ppermute | solution.py:425
  65.8 0.7 collective-permute-done.10
  66.5 1.4 %collective-permute-done.9 = f32[6,1152]{1,0:T(8,128)S(1)} collective-permute-done((f32[6,1152]{1,0:T(8,128)S(1)}, f32[6,1152]{1,0:T(8,128)S(1)}, u32[]{:S(2)}, u32[]{:S(2)}) %collective-permute-start.9) | collective-permute-done | bytes 27680 | tf_op jit(solution)/shard_map/ppermute | solution.py:425
  (25 shorter events, 3.4 us)
Async XLA Ops:
  0.6 3.0 %copy-start = (f32[16,16,6,1152]{3,1,2,0:T(8,128)S(1)}, f32[16,16,6,1152]{3,1,2,0:T(8,128)}, u32[]{:S(2)}) copy-start(f32[16,16,6,1152]{3,1,2,0:T(8,128)} %param.9) | copy-start | bytes 21233668
  3.6 0.8 %copy-start.1 = (f32[6,1152]{1,0:T(8,128)S(1)}, f32[6,1152]{1,0:T(8,128)}, u32[]{:S(2)}) copy-start(f32[6,1152]{1,0:T(8,128)} %density.7) | copy-start | bytes 82948
  4.4 0.8 %copy-start.2 = (s32[6,1152]{1,0:T(8,128)S(1)}, s32[6,1152]{1,0:T(8,128)}, u32[]{:S(2)}) copy-start(s32[6,1152]{1,0:T(8,128)} %material.7) | copy-start | bytes 82948
  5.2 0.8 %copy-start.3 = (f32[6,1152]{1,0:T(8,128)S(1)}, f32[6,1152]{1,0:T(8,128)}, u32[]{:S(2)}) copy-start(f32[6,1152]{1,0:T(8,128)} %objective.3) | copy-start | bytes 82948
  5.9 0.7 copy-start.5
  6.6 0.7 copy-start.7
  7.3 0.7 copy-start.8
  7.9 7.4 %copy-start.6 = (f32[192]{0:T(256)S(1)}, f32[192]{0:T(256)}, u32[]{:S(2)}) copy-start(f32[192]{0:T(256)} %constant.4.clone.dirs) | copy-start | bytes 2308
  8.4 24.5 %collective-permute-start = (f32[136,1152]{1,0:T(8,128)S(1)}, f32[136,1152]{1,0:T(8,128)S(1)}, u32[]{:S(2)}, u32[]{:S(2)}) collective-permute-start(f32[136,1152]{1,0:T(8,128)S(1)} %get-tuple-element.10), channel_id=1, source_target_pairs={{8,0},{16,8},{24,16},{9,1},{17,9},{25,17},{10,2},{18,10},{26,18},{... | collective-permute-start | bytes 1880072 | tf_op jit(solution)/shard_map/ppermute | solution.py:414
  9.7 23.2 %collective-permute-start.1 = (f32[136,1152]{1,0:T(8,128)S(1)}, f32[136,1152]{1,0:T(8,128)S(1)}, u32[]{:S(2)}, u32[]{:S(2)}) collective-permute-start(f32[136,1152]{1,0:T(8,128)S(1)} %get-tuple-element.11), channel_id=1, source_target_pairs={{0,8},{8,16},{16,24},{1,9},{9,17},{17,25},{2,10},{10,18},{18,26},{... | collective-permute-start | bytes 1880072 | tf_op jit(solution)/shard_map/ppermute | solution.py:414
  15.4 31.1 %copy-start.4 = (f32[6,1152]{1,0:T(8,128)S(1)}, f32[6,1152]{1,0:T(8,128)}, u32[]{:S(2)}) copy-start(f32[6,1152]{1,0:T(8,128)} %objective.3) | copy-start | bytes 82948
  27.0 16.7 %collective-permute-start.6 = (f32[128,1152]{1,0:T(8,128)S(1)}, f32[128,1152]{1,0:T(8,128)S(1)}, u32[]{:S(2)}, u32[]{:S(2)}) collective-permute-start(f32[128,1152]{1,0:T(8,128)S(1)} %get-tuple-element.13), channel_id=1, source_target_pairs={{8,0},{16,8},{24,16},{9,1},{17,9},{25,17},{10,2},{18,10},{26,18},{... | collective-permute-start | bytes 1769480 | tf_op jit(solution)/shard_map/ppermute | solution.py:414
  28.3 16.6 %collective-permute-start.7 = (f32[128,1152]{1,0:T(8,128)S(1)}, f32[128,1152]{1,0:T(8,128)S(1)}, u32[]{:S(2)}, u32[]{:S(2)}) collective-permute-start(f32[128,1152]{1,0:T(8,128)S(1)} %get-tuple-element.14), channel_id=1, source_target_pairs={{0,8},{8,16},{16,24},{1,9},{9,17},{17,25},{2,10},{10,18},{18,26},{... | collective-permute-start | bytes 1769480 | tf_op jit(solution)/shard_map/ppermute | solution.py:414
  34.4 1.4 %collective-permute-start.2 = (f32[32,1152]{1,0:T(8,128)S(1)}, f32[32,1152]{1,0:T(8,128)S(1)}, u32[]{:S(2)}, u32[]{:S(2)}) collective-permute-start(f32[32,1152]{1,0:T(8,128)S(1)} %edges.1), channel_id=1, source_target_pairs={{0,1},{1,0},{2,3},{3,2},{4,5},{5,4},{6,7},{7,6},{8,9},{9,8},{10,11... | collective-permute-start | bytes 442376 | tf_op jit(solution)/shard_map/ppermute | solution.py:421
  35.8 9.1 %collective-permute-start.5 = (f32[32,1152]{1,0:T(8,128)S(1)}, f32[32,1152]{1,0:T(8,128)S(1)}, u32[]{:S(2)}, u32[]{:S(2)}) collective-permute-start(f32[32,1152]{1,0:T(8,128)S(1)} %add.15.sum0), channel_id=1, source_target_pairs={{0,6},{2,4},{4,2},{6,0},{1,7},{3,5},{5,3},{7,1},{8,14},{10,12},{12... | collective-permute-start | bytes 442376 | tf_op jit(solution)/shard_map/ppermute | solution.py:425
  38.8 7.3 %collective-permute-start.4 = (f32[32,1152]{1,0:T(8,128)S(1)}, f32[32,1152]{1,0:T(8,128)S(1)}, u32[]{:S(2)}, u32[]{:S(2)}) collective-permute-start(f32[32,1152]{1,0:T(8,128)S(1)} %add.15.sum0), channel_id=1, source_target_pairs={{0,4},{2,6},{4,0},{6,2},{1,5},{3,7},{5,1},{7,3},{8,12},{10,14},{12... | collective-permute-start | bytes 442376 | tf_op jit(solution)/shard_map/ppermute | solution.py:425
  39.3 7.1 %collective-permute-start.3 = (f32[32,1152]{1,0:T(8,128)S(1)}, f32[32,1152]{1,0:T(8,128)S(1)}, u32[]{:S(2)}, u32[]{:S(2)}) collective-permute-start(f32[32,1152]{1,0:T(8,128)S(1)} %add.15.sum0), channel_id=1, source_target_pairs={{0,2},{2,0},{4,6},{6,4},{1,3},{3,1},{5,7},{7,5},{8,10},{10,8},{12,... | collective-permute-start | bytes 442376 | tf_op jit(solution)/shard_map/ppermute | solution.py:425
  59.7 1.2 %collective-permute-start.8 = (f32[6,1152]{1,0:T(8,128)S(1)}, f32[6,1152]{1,0:T(8,128)S(1)}, u32[]{:S(2)}, u32[]{:S(2)}) collective-permute-start(f32[6,1152]{1,0:T(8,128)S(1)} %get-tuple-element.17), channel_id=1, source_target_pairs={{0,1},{1,0},{2,3},{3,2},{4,5},{5,4},{6,7},{7,6},{8,9},{9,8},{10,11... | collective-permute-start | bytes 82952 | tf_op jit(solution)/shard_map/ppermute | solution.py:421
  60.9 4.9 %collective-permute-start.11 = (f32[6,1152]{1,0:T(8,128)S(1)}, f32[6,1152]{1,0:T(8,128)S(1)}, u32[]{:S(2)}, u32[]{:S(2)}) collective-permute-start(f32[6,1152]{1,0:T(8,128)S(1)} %add.16), channel_id=1, source_target_pairs={{0,6},{2,4},{4,2},{6,0},{1,7},{3,5},{5,3},{7,1},{8,14},{10,12},{12... | collective-permute-start | bytes 82952 | tf_op jit(solution)/shard_map/ppermute | solution.py:425
  62.5 4.0 %collective-permute-start.10 = (f32[6,1152]{1,0:T(8,128)S(1)}, f32[6,1152]{1,0:T(8,128)S(1)}, u32[]{:S(2)}, u32[]{:S(2)}) collective-permute-start(f32[6,1152]{1,0:T(8,128)S(1)} %add.16), channel_id=1, source_target_pairs={{0,4},{2,6},{4,0},{6,2},{1,5},{3,7},{5,1},{7,3},{8,12},{10,14},{12... | collective-permute-start | bytes 82952 | tf_op jit(solution)/shard_map/ppermute | solution.py:425
  63.9 4.0 %collective-permute-start.9 = (f32[6,1152]{1,0:T(8,128)S(1)}, f32[6,1152]{1,0:T(8,128)S(1)}, u32[]{:S(2)}, u32[]{:S(2)}) collective-permute-start(f32[6,1152]{1,0:T(8,128)S(1)} %add.16), channel_id=1, source_target_pairs={{0,2},{2,0},{4,6},{6,4},{1,3},{3,1},{5,7},{7,5},{8,10},{10,8},{12,... | collective-permute-start | bytes 82952 | tf_op jit(solution)/shard_map/ppermute | solution.py:425

commit v2 on v1

v2 whole, which is shorter than its diff:
```python
import math

import jax
import jax.numpy as jnp
import numpy as np
from jax import lax
from jax.experimental import pallas as pl
from jax.experimental.pallas import tpu as pltpu
from jax.sharding import PartitionSpec as P

NDIR = 64
NB = 32
NY = 192
ITERS = 2
LANES = 128
SUB = 8
FIRST_GROUP = 8
SECOND_GROUP = 4
VMEM_LIMIT = 24 * 1024 * 1024


def direction_table(count):
    d = np.arange(NDIR)
    half = count // 2
    block, slot = d // count, d % count
    side, pair = slot // half, slot % half
    azimuth = np.pi * (block * half + pair + 0.5) / (NDIR // 2) - np.pi / 2
    along_z = 0.4 * (1.0 - 2.0 * (pair % 2))
    tilt = np.sqrt(1.0 - along_z * along_z)
    along_x = (1.0 - 2.0 * side) * tilt * np.cos(azimuth)
    along_y = tilt * np.sin(azimuth)
    return np.stack([along_x, along_y, along_z], axis=1).astype(np.float32).reshape(-1)


def lane_ids():
    return lax.broadcasted_iota(jnp.int32, (SUB, LANES), 1)


def lazily(make):
    made = {}

    def get(j):
        if j not in made:
            made[j] = make(j)
        return made[j]

    return get


def shifted(v, n, offset, lane, masked=None):
    q, rem = divmod(offset, LANES)
    zero = jnp.zeros((SUB, LANES), jnp.float32)
    rolled = lazily(lambda j: pltpu.roll(v(j), LANES - rem, 1) if rem else v(j))

    def tile(j):
        parts = []
        for k, low, high in ((j + q, 0, LANES - rem), (j + q + 1, LANES - rem, LANES)):
            kept = low < high and 0 <= k < n
            kept = kept and not all(masked is not None and masked(j * LANES + i) for i in range(low, high))
            parts.append(rolled(k) if kept else None)
        if parts[0] is None and parts[1] is None:
            return None
        t = parts[0]
        if rem:
            t = jnp.where(lane < LANES - rem, *[zero if part is None else part for part in parts])
        for i in range(LANES):
            if masked is not None and masked(j * LANES + i) and parts[int(i >= LANES - rem)] is not None:
                t = jnp.where(lane == i, zero, t)
        return t

    return lazily(tile)


def shift_y(v, n, rising, lane):
    if rising:
        return shifted(v, n, 1, lane, lambda p: p % NY == NY - 1)
    return shifted(v, n, -1, lane, lambda p: p % NY == 0)


def shift_z(v, n, rising, lane):
    return shifted(v, n, NY if rising else -NY, lane)


def inverse(x):
    r = pl.reciprocal(x, approx=True)
    return r * (2.0 - x * r)


def column(row, offset, n):
    shape = (n, row.shape[1])
    i0 = lax.broadcasted_iota(jnp.int32, shape, 0)
    i1 = lax.broadcasted_iota(jnp.int32, shape, 1)
    picked = jnp.sum(jnp.where(i1 == i0 + offset, row, 0.0), axis=1, keepdims=True)
    return jnp.broadcast_to(picked, (n, LANES))


def fill_columns(cols, heat, speed, table):
    nb = cols.shape[1]
    row = heat[...]
    total = jnp.sum(row, axis=1, keepdims=True) * float(NDIR)
    cols[0] = column(speed[...], 0, nb)
    cols[1] = column(row / total, lax.axis_index("band") * nb, nb)
    for m in range(table.shape[0]):
        cols[2 + m] = column(table[m : m + 1], 0, nb)


def base_tile(cols, material, hs):
    base = jnp.broadcast_to(cols[2, hs], (SUB, LANES))
    for m in range(1, cols.shape[0] - 2):
        base = jnp.where(material == m, cols[2 + m, hs], base)
    return base


def halves(nb):
    return [slice(h * SUB, (h + 1) * SUB) for h in range(nb // SUB)]


def tiles(plane):
    return [slice(j * LANES, (j + 1) * LANES) for j in range(plane // LANES)]


def sub_sum(t):
    return jnp.sum(t, axis=0, keepdims=True)


def add_terms(terms):
    terms = [t for t in terms if t is not None]
    total = terms[0]
    for t in terms[1:]:
        total = total + t
    return total


def times(a, b):
    return None if b is None else a * b


def cosines(dirs, d):
    at = 3 * d
    return dirs[at], dirs[at + 1], dirs[at + 2]


def is_even():
    return lax.axis_index("space") % 2 == 0


def faces_kernel(table_in, density_in, material_in, objective_in, start, out_a, out_b, table, density, material, objective, others, cols, sems):
    half, nb, plane = others.shape[1:]
    last = density.shape[0] - 1
    even = is_even()
    copies = []
    for n, (src, dst) in enumerate(
        ((table_in, table), (density_in, density), (material_in, material), (objective_in, objective))
    ):
        copies.append(pltpu.make_async_copy(src, dst, sems.at[n]))
    for side, out in enumerate((out_a, out_b)):
        upper = even if side == 0 else jnp.logical_not(even)
        first, second, x = jnp.where(upper, half, 0), jnp.where(upper, 0, half), jnp.where(upper, last, 0)
        at = 4 + side * (half + 1)
        for d in range(half):
            copies.append(
                pltpu.make_async_copy(start.at[first + d, x], out.at[pl.ds(d * nb, nb)], sems.at[at + d])
            )
        copies.append(pltpu.make_async_copy(start.at[pl.ds(second, half), x], others.at[side], sems.at[at + half]))
    for copy in copies:
        copy.start()
    for copy in copies:
        copy.wait()
    for m in range(table.shape[0]):
        cols[2 + m] = column(table[m : m + 1], 0, nb)
    for side, out in enumerate((out_a, out_b)):
        upper = even if side == 0 else jnp.logical_not(even)
        row = lambda ref, cs: jnp.where(upper, ref[last : last + 1, cs], ref[0:1, cs])
        base = half * nb
        for cs in tiles(plane):
            dens, mat = row(density, cs), row(material, cs)
            share = 0.0
            for h, hs in enumerate(halves(nb)):
                total = others[side, 0, hs, cs]
                for d in range(1, half):
                    total = total + others[side, d, hs, cs]
                for d in range(half):
                    total = total + out[d * nb + h * SUB : d * nb + (h + 1) * SUB, cs]
                share = share + base_tile(cols, mat, hs) * (0.2 + 0.8 * dens) * total
            out[base : base + 1, cs] = sub_sum(share)
            out[base + 1 : base + 2, cs] = dens
            out[base + 2 : base + 3, cs] = mat.astype(jnp.float32)
            out[base + 3 : base + 4, cs] = row(objective, cs)
            out[base + 4 : base + 8, cs] = jnp.zeros((4, LANES), jnp.float32)


def first_kernel(
    dirs, heat, speed, table, density, material, field, excess, flow, face_a, face_b, sums, cols, rate, acc
):
    g = pl.program_id(0)
    steps = pl.num_programs(0)
    count, nx, nb, plane = field.shape
    per = count // steps
    cuts, bands = tiles(plane), halves(nb)
    n = len(cuts)

    @pl.when(g == 0)
    def _():
        fill_columns(cols, heat, speed, table)
        for x in range(nx):
            for cs in cuts:
                factor = 0.2 + 0.8 * density[x : x + 1, cs]
                for hs in bands:
                    rate[x, hs, cs] = base_tile(cols, material[x : x + 1, cs], hs) * factor
        acc[...] = jnp.zeros_like(acc)

    block = lax.axis_index("dir")
    first = block * count + g * per
    ahead = g < steps // 2
    lane = lane_ids()

    def run(rising):
        def layer(x, _):
            edge = jnp.where(ahead, x == nx - 1, x == 0)
            beside = jnp.where(edge, x, jnp.where(ahead, x + 1, x - 1))
            for hs in bands:
                pace = cols[0, hs]
                ways = []
                for dd in range(per):
                    ax, ay, az = [jnp.abs(a) for a in cosines(dirs, first + dd)]
                    v = lazily(lambda j, dd=dd: field[g * per + dd, x, hs, cuts[j]])
                    speeds = (pace * jnp.where(edge, 0.0, ax), pace * ay, pace * az, pace * (ax + ay + az))
                    ways.append((v, shift_y(v, n, rising, lane), shift_z(v, n, dd % 2 == 0, lane), speeds))
                for j, cs in enumerate(cuts):
                    r = rate[x, hs, cs]
                    kept = []
                    for dd, (v, along_y, along_z, (cx, cy, cz, speeds)) in enumerate(ways):
                        d = g * per + dd
                        inv = inverse(speeds + r)
                        a = inv * add_terms(
                            [times(cx, field[d, beside, hs, cs]), times(cy, along_y(j)), times(cz, along_z(j))]
                        )
                        flow[d, x, hs, cs] = a
                        kept.append((v(j), excess[d, x, hs, cs], a, inv))
                    for f in range(4):
                        acc[f, x, hs, cs] += add_terms([k[f] for k in kept])
            return 0

        lax.fori_loop(0, nx, layer, 0)

    rises = cosines(dirs, first)[1] > 0
    pl.when(rises)(lambda: run(True))
    pl.when(jnp.logical_not(rises))(lambda: run(False))

    def give(face):
        x = jnp.where(ahead, 0, nx - 1)
        skip = jnp.where(ahead, 0, steps // 2)
        for dd in range(per):
            face[pl.ds(pl.multiple_of(((g - skip) * per + dd) * nb, nb), nb)] = flow[g * per + dd, x]

    pl.when(ahead != is_even())(lambda: give(face_a))
    pl.when(ahead == is_even())(lambda: give(face_b))

    @pl.when(g == steps - 1)
    def _():
        for x in range(nx):
            for cs in cuts:
                totals = [0.0] * 4
                for hs in bands:
                    r, w = rate[x, hs, cs], cols[1, hs]
                    for f, scale in enumerate((r, w, r, r * w)):
                        totals[f] = totals[f] + scale * acc[f, x, hs, cs]
                for f in range(4):
                    sums[f * nx + x : f * nx + x + 1, cs] = sub_sum(totals[f])
        sums[4 * nx :] = jnp.zeros((sums.shape[0] - 4 * nx, plane), jnp.float32)


def edges_kernel(dirs, heat, speed, table, density, material, halo_a, halo_b, sums, out, cols):
    fill_columns(cols, heat, speed, table)
    nx, plane = density.shape
    nb = cols.shape[1]
    half = (halo_a.shape[0] - SUB) // nb
    count = 2 * half
    block = lax.axis_index("dir")
    even = is_even()
    out[...] = sums[...]
    cuts = tiles(plane)
    gains = []
    for side, halo in enumerate((halo_a, halo_b)):
        ahead = even if side == 0 else jnp.logical_not(even)
        rates = []
        for hs in halves(nb):
            rates.append([])
            for cs in cuts:
                mat = jnp.where(ahead, material[nx - 1 : nx, cs], material[0:1, cs])
                dens = jnp.where(ahead, density[nx - 1 : nx, cs], density[0:1, cs])
                rates[-1].append(base_tile(cols, mat, hs) * (0.2 + 0.8 * dens))
        first = block * count + jnp.where(ahead, 0, half)

        def add(d, totals):
            ax, ay, az = [jnp.abs(a) for a in cosines(dirs, first + d)]
            new = list(totals)
            for h, hs in enumerate(halves(nb)):
                pace = cols[0, hs]
                cx, speeds = pace * ax, pace * (ax + ay + az)
                rows = halo.at[pl.ds(pl.multiple_of(d * nb + h * SUB, SUB), SUB)]
                for j, cs in enumerate(cuts):
                    r = rates[h][j]
                    new[j] = new[j] + (cx * rows[:, cs]) * (r * inverse(speeds + r))
            return tuple(new)

        totals = lax.fori_loop(0, half, add, tuple(jnp.zeros((SUB, LANES), jnp.float32) for _ in cuts))
        gains.append([sub_sum(t) for t in totals])
    base = half * nb
    for side, x in enumerate((nx - 1, 0)):
        near, far = (0, 1) if side == 0 else (1, 0)
        row = 2 * nx + x
        for j, cs in enumerate(cuts):
            out[row : row + 1, cs] = out[row : row + 1, cs] + jnp.where(even, gains[near][j], gains[far][j])
            a, b = halo_a[base : base + 1, cs], halo_b[base : base + 1, cs]
            out[4 * nx + side : 4 * nx + side + 1, cs] = jnp.where(even, a, b) if side == 0 else jnp.where(even, b, a)


def second_kernel(
    dirs, heat, speed, table, density, material, objective,
    sum0, sum1, sum2, sum3, halo0_a, halo0_b, halo1_a, halo1_b,
    flow, excess, dual, gradient,
    cols, rate, source0, source1, warm, prev, seed, acc,
):
    g = pl.program_id(0)
    steps = pl.num_programs(0)
    count, nx, nb, plane = flow.shape
    per = count // steps
    cuts, bands = tiles(plane), halves(nb)
    n = len(cuts)
    scale = float(NDIR * NB)
    edge = halo0_a.shape[0] - SUB

    @pl.when(g == 0)
    def _():
        fill_columns(cols, heat, speed, table)
        total = (sum0[...] + sum1[...]) + (sum2[...] + sum3[...])
        for x in range(nx):
            warm[x] = jnp.broadcast_to(total[nx + x : nx + x + 1], (SUB, plane))
        for x in range(nx + 2):
            for cs in cuts:
                if x < nx:
                    dens, mat = density[x : x + 1, cs], material[x : x + 1, cs]
                    drive = total[x : x + 1, cs] + scale * objective[x : x + 1, cs]
                    again = (
                        total[2 * nx + x : 2 * nx + x + 1, cs]
                        + drive * total[3 * nx + x : 3 * nx + x + 1, cs]
                        + scale * objective[x : x + 1, cs]
                    )
                else:
                    from_a = is_even() if x == nx else jnp.logical_not(is_even())
                    dens, mat, aim = [
                        jnp.where(from_a, halo0_a[edge + k : edge + k + 1, cs], halo0_b[edge + k : edge + k + 1, cs])
                        for k in (1, 2, 3)
                    ]
                    mat = mat.astype(jnp.int32)
                    drive = total[3 * nx + x : 3 * nx + x + 1, cs] + scale * aim
                factor = 0.2 + 0.8 * dens
                for hs in bands:
                    w = cols[1, hs]
                    rate[x, hs, cs] = base_tile(cols, mat, hs) * factor
                    source0[x, hs, cs] = w * drive
                    if x < nx:
                        source1[x, hs, cs] = w * again
        acc[...] = jnp.zeros_like(acc)

    block = lax.axis_index("dir")
    first = block * count + g * per
    ahead = g < steps // 2
    lane = lane_ids()

    def enter(halo0, halo1):
        x = jnp.where(ahead, nx, nx + 1)
        skip = jnp.where(ahead, 0, steps // 2)
        for dd in range(per):
            ax, ay, az = [jnp.abs(a) for a in cosines(dirs, first + dd)]
            for h, hs in enumerate(bands):
                pace = cols[0, hs]
                speeds, cx = pace * (ax + ay + az), pace * ax
                rows = pl.ds(pl.multiple_of(((g - skip) * per + dd) * nb + h * SUB, SUB), SUB)
                for cs in cuts:
                    prev[dd, hs, cs] = halo1[rows, cs] + source0[x, hs, cs] * inverse(speeds + rate[x, hs, cs])
                    seed[dd, hs, cs] = cx * halo0[rows, cs]

    pl.when(ahead == is_even())(lambda: enter(halo0_a, halo1_a))
    pl.when(ahead != is_even())(lambda: enter(halo0_b, halo1_b))

    def run(rising):
        def layer(i, at_edge):
            x = jnp.where(ahead, nx - 1 - i, i)
            for hs in bands:
                pace = cols[0, hs]
                rates = lazily(lambda j: rate[x, hs, cuts[j]])
                sources = lazily(lambda j: source0[x, hs, cuts[j]])
                ways = []
                for dd in range(per):
                    ax, ay, az = [jnp.abs(a) for a in cosines(dirs, first + dd)]
                    speeds = pace * (ax + ay + az)
                    inv = lazily(lambda j, speeds=speeds: inverse(speeds + rates(j)))

                    def fresh(j, dd=dd, inv=inv):
                        s = sources(j)
                        if at_edge:
                            s = s + seed[dd, hs, cuts[j]]
                        return flow[g * per + dd, x, hs, cuts[j]] + s * inv(j)

                    v = lazily(fresh)
                    shifts = (shift_y(v, n, rising, lane), shift_z(v, n, dd % 2 == 0, lane))
                    ways.append((v, inv, *shifts, (pace * ax, pace * ay, pace * az)))
                for j, cs in enumerate(cuts):
                    kept = []
                    again, level = source1[x, hs, cs], warm[x, :, cs]
                    for dd, (v, inv, along_y, along_z, (cx, cy, cz)) in enumerate(ways):
                        new = inv(j) * add_terms([
                            times(cx, prev[dd, hs, cs]), times(cy, along_y(j)), times(cz, along_z(j)), again
                        ])
                        prev[dd, hs, cs] = v(j)
                        dual[dd, x, hs, cs] = new
                        kept.append((v(j) + new) * (excess[g * per + dd, x, hs, cs] - level))
                    acc[x, hs, cs] += add_terms(kept)

        layer(0, True)

        def later(i, _):
            layer(i, False)
            return 0

        lax.fori_loop(1, nx, later, 0)

    rises = cosines(dirs, first)[1] > 0
    pl.when(rises)(lambda: run(True))
    pl.when(jnp.logical_not(rises))(lambda: run(False))

    @pl.when(g == steps - 1)
    def _():
        for x in range(nx):
            for cs in cuts:
                total = 0.0
                for hs in bands:
                    total = total + base_tile(cols, material[x : x + 1, cs], hs) * acc[x, hs, cs]
                gradient[x : x + 1, cs] = sub_sum(total) * 0.8


def swapped(value, start):
    count = lax.axis_size("space")
    pairs = [(s, s + 1) for s in range(start, count - 1, 2)]
    return lax.ppermute(value, "space", pairs + [(b, a) for a, b in pairs])


def shares(partial):
    size = lax.axis_size("band")
    total = partial
    for k in range(1, size):
        total = total + lax.ppermute(partial, "band", [(s, (s + k) % size) for s in range(size)])
    count = lax.axis_size("dir")
    pairs = count & (count - 1) == 0
    hops = [[(s, s ^ k if pairs else (s + k) % count) for s in range(count)] for k in range(1, count)]
    return [total] + [lax.ppermute(total, "dir", hop) for hop in hops]


def whole(array):
    return pl.BlockSpec(array.shape, lambda *g: (0,) * array.ndim)


def on_device(
    adjoint_start, primal_deviations, density, material, rate_table, group_speed, heat_capacity, objective_weight
):
    count, nb, nx, plane = adjoint_start.shape
    half = count // 2
    first_steps = count // math.gcd(FIRST_GROUP, half)
    second_steps = count // math.gcd(SECOND_GROUP, half)
    nmat = rate_table.shape[0]
    start = adjoint_start.transpose(0, 2, 1, 3)
    excess = primal_deviations.transpose(0, 2, 1, 3)
    f32 = jnp.float32
    vmem = pl.BlockSpec(memory_space=pltpu.VMEM)
    smem = pl.BlockSpec(memory_space=pltpu.SMEM)
    dirs = jnp.asarray(direction_table(count))
    heat = heat_capacity.reshape(1, -1)
    speed = group_speed.reshape(1, -1)
    tables = (heat, speed, rate_table)
    cells = (density, material)
    cols = pltpu.VMEM((2 + nmat, nb, LANES), f32)
    params = pltpu.CompilerParams(vmem_limit_bytes=VMEM_LIMIT)
    size = count * nb * nx * plane

    rows = half * nb + SUB
    hbm = pl.BlockSpec(memory_space=pltpu.HBM)
    small = (rate_table, *cells, objective_weight)
    face_a, face_b = pl.pallas_call(
        faces_kernel,
        out_shape=(jax.ShapeDtypeStruct((rows, plane), f32),) * 2,
        in_specs=[hbm] * 5,
        out_specs=[vmem] * 2,
        scratch_shapes=[pltpu.VMEM(a.shape, a.dtype) for a in small]
        + [pltpu.VMEM((2, half, nb, plane), f32), cols, pltpu.SemaphoreType.DMA((4 + 2 * (half + 1),))],
        compiler_params=params,
        cost_estimate=pl.CostEstimate(flops=size // 3, bytes_accessed=size * 2, transcendentals=0),
        name="faces",
    )(*small, start)
    halo0_a, halo0_b = swapped(face_a, 0), swapped(face_b, 1)

    sum_rows = -(-(4 * nx + 2) // SUB) * SUB
    small = (*tables, *cells)
    flow, face_a, face_b, sums = pl.pallas_call(
        first_kernel,
        grid=(first_steps,),
        out_shape=(
            jax.ShapeDtypeStruct(start.shape, f32),
            jax.ShapeDtypeStruct((half * nb, plane), f32),
            jax.ShapeDtypeStruct((half * nb, plane), f32),
            jax.ShapeDtypeStruct((sum_rows, plane), f32),
        ),
        in_specs=[smem] + [vmem] * (len(small) + 2),
        out_specs=[vmem] * 4,
        scratch_shapes=[cols, pltpu.VMEM((nx, nb, plane), f32), pltpu.VMEM((4, nx, nb, plane), f32)],
        compiler_params=params,
        cost_estimate=pl.CostEstimate(flops=size * 20, bytes_accessed=size * 12, transcendentals=size),
        name="first",
    )(dirs, *small, start, excess)
    halo1_a, halo1_b = swapped(face_a, 0), swapped(face_b, 1)

    sums = pl.pallas_call(
        edges_kernel,
        out_shape=jax.ShapeDtypeStruct(sums.shape, f32),
        in_specs=[smem] + [pl.BlockSpec(memory_space=pltpu.VMEM)] * (len(small) + 3),
        out_specs=pl.BlockSpec(memory_space=pltpu.VMEM),
        scratch_shapes=[cols],
        compiler_params=params,
        cost_estimate=pl.CostEstimate(flops=size, bytes_accessed=size, transcendentals=0),
        name="edges",
    )(dirs, *small, halo0_a, halo0_b, sums)
    parts = shares(sums)
    parts = parts[:3] + [sum(parts[3:], jnp.zeros_like(sums))] if len(parts) > 4 else parts + [jnp.zeros_like(sums)] * (4 - len(parts))

    small = (*tables, *cells, objective_weight, *parts)
    dual, gradient = pl.pallas_call(
        second_kernel,
        grid=(second_steps,),
        out_shape=(jax.ShapeDtypeStruct(start.shape, f32), jax.ShapeDtypeStruct((nx, plane), f32)),
        in_specs=[smem] + [vmem] * (len(small) + 6),
        out_specs=[pl.BlockSpec((count // second_steps, nx, nb, plane), lambda g: (g, 0, 0, 0)), vmem],
        scratch_shapes=[
            cols,
            pltpu.VMEM((nx + 2, nb, plane), f32),
            pltpu.VMEM((nx + 2, nb, plane), f32),
            pltpu.VMEM((nx, nb, plane), f32),
            pltpu.VMEM((nx, SUB, plane), f32),
            pltpu.VMEM((count // second_steps, nb, plane), f32),
            pltpu.VMEM((count // second_steps, nb, plane), f32),
            pltpu.VMEM((nx, nb, plane), f32),
        ],
        compiler_params=params,
        cost_estimate=pl.CostEstimate(flops=size * 30, bytes_accessed=size * 12, transcendentals=size),
        name="second",
    )(dirs, *small, halo0_a, halo0_b, halo1_a, halo1_b, flow, excess)
    gradient = sum(shares(gradient)) * (-0.125 / ITERS)
    return (dual.transpose(0, 2, 1, 3), gradient)


def solution(mesh):
    placed = (
        P("dir", "band", "space", None),
        P("dir", "band", "space", None),
        P("space", None),
        P("space", None),
        P(None, "band"),
        P("band"),
        P(),
        P("space", None),
    )
    return jax.shard_map(
        on_device,
        mesh=mesh,
        in_specs=placed,
        out_specs=(P("dir", "band", "space", None), P("space", None)),
        check_vma=False,
    )
```

time: 69.3 us -> 61.3 us (0.88)
  the two profiles are of different devices: /device:TPU:0 before, /device:TPU:16 now
where the time goes in v2:
time: 61.3 us; the launch traced here: 61.1 us
  Pallas kernels  19.8 us (32%)
  waiting for transfers between devices  15.8 us (26%)
  starting transfers between devices  14.7 us (24%)
  local copies, waits for them, and re-layouts  9.42 us (15%)
  between operations  0.77 us (1%)
  other arithmetic  0.65 us (1%)
    pallas_call x1, Pallas kernels, on_device(): pl.pallas_call(second_kernel, grid=(second_steps,), out_shape=(jax.ShapeD...  9.46 us
    unnamed x22, local copies, waits for them, and re-layouts  9.42 us
    ppermute x4, waiting for transfers between devices, swapped(): return lax.ppermute(value, 'space', pairs + [(b, a) for a, b in pairs])  7.94 us
    ppermute x4, starting transfers between devices, swapped(): return lax.ppermute(value, 'space', pairs + [(b, a) for a, b in pairs])  7.54 us
    ppermute x6, starting transfers between devices, shares(): return [total] + [lax.ppermute(total, 'dir', hop) for hop in hops]  7.04 us
    pallas_call x1, Pallas kernels, on_device(): pl.pallas_call(first_kernel, grid=(first_steps,), out_shape=(jax.ShapeDty...  6.72 us
    ppermute x6, waiting for transfers between devices, shares(): return [total] + [lax.ppermute(total, 'dir', hop) for hop in hops]  5.26 us
    ppermute x2, waiting for transfers between devices, shares(): lax.ppermute(partial, 'band', [(s, (s + k) % size) for s in range(size)])  2.57 us
  transfers between devices with their start and end apart: 12, of which 10 were waited for; matrix products, arithmetic and copies ran while one was open for 0% of the time, Pallas kernels for 13%

profile of v2, /device:TPU:16, one launch (start us, length us, event | category | flops | bytes accessed | tf_op | source)
XLA Modules:
  0.0 61.1 jit_solution(10869849758052073328)
XLA Ops:
  0.7 3.1 %copy-done.1 = f32[16,16,6,1152]{3,1,2,0:T(8,128)S(1)} copy-done((f32[16,16,6,1152]{3,1,2,0:T(8,128)S(1)}, f32[16,16,6,1152]{3,1,2,0:T(8,128)}, u32[]{:S(2)}) %copy-start.1) | copy-done | bytes 7077912
  3.8 1.0 %copy-done.3 = f32[6,1152]{1,0:T(8,128)S(1)} copy-done((f32[6,1152]{1,0:T(8,128)S(1)}, f32[6,1152]{1,0:T(8,128)}, u32[]{:S(2)}) %copy-start.3) | copy-done | bytes 27672
  4.8 0.8 %copy-done.4 = s32[6,1152]{1,0:T(8,128)S(1)} copy-done((s32[6,1152]{1,0:T(8,128)S(1)}, s32[6,1152]{1,0:T(8,128)}, u32[]{:S(2)}) %copy-start.4) | copy-done | bytes 27672
  5.6 0.8 %copy-done.5 = f32[6,1152]{1,0:T(8,128)S(1)} copy-done((f32[6,1152]{1,0:T(8,128)S(1)}, f32[6,1152]{1,0:T(8,128)}, u32[]{:S(2)}) %copy-start.5) | copy-done | bytes 27672
  7.1 2.2 %faces.1 = (f32[136,1152]{1,0:T(8,128)S(1)}, f32[136,1152]{1,0:T(8,128)S(1)}) custom-call(f32[4,16]{1,0:T(4,128)S(1)} %copy-done.7, f32[6,1152]{1,0:T(8,128)S(1)} %copy-done.3, s32[6,1152]{1,0:T(8,128)S(1)} %copy-done.4, f32[6,1152]{1,0:T(8,128)S(1)} %copy-done.5, f32[16,6,16,1152]{3,2,1,0:T(8,128)S(1)} %bitcast.7), custom_call_target="tpu_custom_call" | custom-call | flops 589824 | bytes 3538944 | tf_op jit(solution)/shard_map/faces/pallas_call | solution.py:490
  9.3 1.6 %collective-permute-start = (f32[136,1152]{1,0:T(8,128)S(1)}, f32[136,1152]{1,0:T(8,128)S(1)}, u32[]{:S(2)}, u32[]{:S(2)}) collective-permute-start(f32[136,1152]{1,0:T(8,128)S(1)} %get-tuple-element.10), channel_id=1, source_target_pairs={{0,8},{16,24},{8,0},{24,16},{1,9},{17,25},{9,1},{25,17},{2,10},{18... | collective-permute-start | bytes 1880072 | tf_op jit(solution)/shard_map/ppermute | solution.py:447
  10.9 1.9 %collective-permute-start.1 = (f32[136,1152]{1,0:T(8,128)S(1)}, f32[136,1152]{1,0:T(8,128)S(1)}, u32[]{:S(2)}, u32[]{:S(2)}) collective-permute-start(f32[136,1152]{1,0:T(8,128)S(1)} %get-tuple-element.11), channel_id=1, source_target_pairs={{8,16},{16,8},{9,17},{17,9},{10,18},{18,10},{11,19},{19,11},{12,20... | collective-permute-start | bytes 1880072 | tf_op jit(solution)/shard_map/ppermute | solution.py:447
  12.9 3.0 %copy-done.2 = f32[16,16,6,1152]{3,1,2,0:T(8,128)S(1)} copy-done((f32[16,16,6,1152]{3,1,2,0:T(8,128)S(1)}, f32[16,16,6,1152]{3,1,2,0:T(8,128)}, u32[]{:S(2)}) %copy-start.2) | copy-done | bytes 7077912
  15.9 6.7 %first.1 = (f32[16,6,16,1152]{3,2,1,0:T(8,128)S(1)}, f32[128,1152]{1,0:T(8,128)S(1)}, f32[128,1152]{1,0:T(8,128)S(1)}, f32[32,1152]{1,0:T(8,128)S(1)}) custom-call(f32[192]{0:T(256)S(1)} %copy-done.8, f32[1,32]{1,0:T(1,128)S(1)} %bitcast.9, f32[1,16]{1,0:T(1,128)S(1)} %bitcast.12, f32[4,16]{1,0:T(4,128)S(1)} %copy-done.7, f32[6,1152]{1,0:T(8,128)S(1)} %copy-done.3, ...), custom_call_target="tpu_custom_call" | custom-call | flops 35389440 | bytes 21233664 | tf_op jit(solution)/shard_map/first/pallas_call | solution.py:505
  22.7 3.9 %collective-permute-start.7 = (f32[128,1152]{1,0:T(8,128)S(1)}, f32[128,1152]{1,0:T(8,128)S(1)}, u32[]{:S(2)}, u32[]{:S(2)}) collective-permute-start(f32[128,1152]{1,0:T(8,128)S(1)} %get-tuple-element.14), channel_id=1, source_target_pairs={{8,16},{16,8},{9,17},{17,9},{10,18},{18,10},{11,19},{19,11},{12,20... | collective-permute-start | bytes 1769480 | tf_op jit(solution)/shard_map/ppermute | solution.py:447
  26.6 3.2 %collective-permute-done.1.halo_b.halo0_b = f32[136,1152]{1,0:T(8,128)S(1)} collective-permute-done((f32[136,1152]{1,0:T(8,128)S(1)}, f32[136,1152]{1,0:T(8,128)S(1)}, u32[]{:S(2)}, u32[]{:S(2)}) %collective-permute-start.1) | collective-permute-done | bytes 626720 | tf_op jit(solution)/shard_map/ppermute | solution.py:447
  29.9 1.4 %edges.1 = f32[32,1152]{1,0:T(8,128)S(1)} custom-call(f32[192]{0:T(256)S(1)} %copy-done.8, f32[1,32]{1,0:T(1,128)S(1)} %bitcast.10, f32[1,16]{1,0:T(1,128)S(1)} %bitcast.13, f32[4,16]{1,0:T(4,128)S(1)} %copy-done.7, f32[6,1152]{1,0:T(8,128)S(1)} %copy-done.3, s32[6,1152]{1,0:T(8,128)S(1)} %copy-done.4, f32[136,1152]{1,0:T(8,128)S(1)} %collective-permute-done.halo_a.halo0_a, ...), custom_call_target="tpu_custom_call" | custom-call | flops 1769472 | bytes 1769472 | tf_op jit(solution)/shard_map/edges/pallas_call | solution.py:523
  31.4 1.4 %collective-permute-done.2 = f32[32,1152]{1,0:T(8,128)S(1)} collective-permute-done((f32[32,1152]{1,0:T(8,128)S(1)}, f32[32,1152]{1,0:T(8,128)S(1)}, u32[]{:S(2)}, u32[]{:S(2)}) %collective-permute-start.2) | collective-permute-done | bytes 147488 | tf_op jit(solution)/shard_map/ppermute | solution.py:454
  32.7 2.5 %collective-permute-start.5 = (f32[32,1152]{1,0:T(8,128)S(1)}, f32[32,1152]{1,0:T(8,128)S(1)}, u32[]{:S(2)}, u32[]{:S(2)}) collective-permute-start(f32[32,1152]{1,0:T(8,128)S(1)} %add.15.sum0), channel_id=1, source_target_pairs={{0,6},{2,4},{4,2},{6,0},{1,7},{3,5},{5,3},{7,1},{8,14},{10,12},{12... | collective-permute-start | bytes 442376 | tf_op jit(solution)/shard_map/ppermute | solution.py:458
  36.3 1.6 %collective-permute-done.6.halo1_a = f32[128,1152]{1,0:T(8,128)S(1)} collective-permute-done((f32[128,1152]{1,0:T(8,128)S(1)}, f32[128,1152]{1,0:T(8,128)S(1)}, u32[]{:S(2)}, u32[]{:S(2)}) %collective-permute-start.6) | collective-permute-done | bytes 589856 | tf_op jit(solution)/shard_map/ppermute | solution.py:447
  37.8 3.2 %collective-permute-done.7.halo1_b = f32[128,1152]{1,0:T(8,128)S(1)} collective-permute-done((f32[128,1152]{1,0:T(8,128)S(1)}, f32[128,1152]{1,0:T(8,128)S(1)}, u32[]{:S(2)}, u32[]{:S(2)}) %collective-permute-start.7) | collective-permute-done | bytes 589856 | tf_op jit(solution)/shard_map/ppermute | solution.py:447
  41.0 1.7 %collective-permute-done.4.sum2 = f32[32,1152]{1,0:T(8,128)S(1)} collective-permute-done((f32[32,1152]{1,0:T(8,128)S(1)}, f32[32,1152]{1,0:T(8,128)S(1)}, u32[]{:S(2)}, u32[]{:S(2)}) %collective-permute-start.4) | collective-permute-done | bytes 147488 | tf_op jit(solution)/shard_map/ppermute | solution.py:458
  42.9 9.5 %second.1 = (f32[16,6,16,1152]{3,2,1,0:T(8,128)}, f32[6,1152]{1,0:T(8,128)S(1)}) custom-call(f32[192]{0:T(256)S(1)} %copy-done.8, f32[1,32]{1,0:T(1,128)S(1)} %bitcast.11, f32[1,16]{1,0:T(1,128)S(1)} %bitcast.14, f32[4,16]{1,0:T(4,128)S(1)} %copy-done.7, f32[6,1152]{1,0:T(8,128)S(1)} %copy-done.3, s32[6,1152]{1,0:T(8,128)S(1)} %copy-done.4, ...), custom_call_target="tpu_custom_call" | custom-call | flops 53084160 | bytes 21233664 | tf_op jit(solution)/shard_map/second/pallas_call | solution.py:537
  52.3 1.2 %collective-permute-done.8 = f32[6,1152]{1,0:T(8,128)S(1)} collective-permute-done((f32[6,1152]{1,0:T(8,128)S(1)}, f32[6,1152]{1,0:T(8,128)S(1)}, u32[]{:S(2)}, u32[]{:S(2)}) %collective-permute-start.8) | collective-permute-done | bytes 27680 | tf_op jit(solution)/shard_map/ppermute | solution.py:454
  53.5 1.6 %collective-permute-start.11 = (f32[6,1152]{1,0:T(8,128)S(1)}, f32[6,1152]{1,0:T(8,128)S(1)}, u32[]{:S(2)}, u32[]{:S(2)}) collective-permute-start(f32[6,1152]{1,0:T(8,128)S(1)} %add.16), channel_id=1, source_target_pairs={{0,6},{2,4},{4,2},{6,0},{1,7},{3,5},{5,3},{7,1},{8,14},{10,12},{12... | collective-permute-start | bytes 82952 | tf_op jit(solution)/shard_map/ppermute | solution.py:458
  55.1 1.4 %collective-permute-start.10 = (f32[6,1152]{1,0:T(8,128)S(1)}, f32[6,1152]{1,0:T(8,128)S(1)}, u32[]{:S(2)}, u32[]{:S(2)}) collective-permute-start(f32[6,1152]{1,0:T(8,128)S(1)} %add.16), channel_id=1, source_target_pairs={{0,4},{2,6},{4,0},{6,2},{1,5},{3,7},{5,1},{7,3},{8,12},{10,14},{12... | collective-permute-start | bytes 82952 | tf_op jit(solution)/shard_map/ppermute | solution.py:458
  57.0 1.4 %collective-permute-done.11 = f32[6,1152]{1,0:T(8,128)S(1)} collective-permute-done((f32[6,1152]{1,0:T(8,128)S(1)}, f32[6,1152]{1,0:T(8,128)S(1)}, u32[]{:S(2)}, u32[]{:S(2)}) %collective-permute-start.11) | collective-permute-done | bytes 27680 | tf_op jit(solution)/shard_map/ppermute | solution.py:458
  58.4 0.7 %collective-permute-done.10 = f32[6,1152]{1,0:T(8,128)S(1)} collective-permute-done((f32[6,1152]{1,0:T(8,128)S(1)}, f32[6,1152]{1,0:T(8,128)S(1)}, u32[]{:S(2)}, u32[]{:S(2)}) %collective-permute-start.10) | collective-permute-done | bytes 27680 | tf_op jit(solution)/shard_map/ppermute | solution.py:458
  59.1 1.4 %collective-permute-done.9 = f32[6,1152]{1,0:T(8,128)S(1)} collective-permute-done((f32[6,1152]{1,0:T(8,128)S(1)}, f32[6,1152]{1,0:T(8,128)S(1)}, u32[]{:S(2)}, u32[]{:S(2)}) %collective-permute-start.9) | collective-permute-done | bytes 27680 | tf_op jit(solution)/shard_map/ppermute | solution.py:458
  (29 shorter events, 3.2 us)
Async XLA Ops:
  0.6 12.2 %copy-start = (f32[16,16,6,1152]{3,1,2,0:T(8,128)S(1)}, f32[16,16,6,1152]{3,1,2,0:T(8,128)}, u32[]{:S(2)}) copy-start(f32[16,16,6,1152]{3,1,2,0:T(8,128)} %param.10) | copy-start | bytes 21233668
  0.6 3.2 %copy-start.1 = (f32[16,16,6,1152]{3,1,2,0:T(8,128)S(1)}, f32[16,16,6,1152]{3,1,2,0:T(8,128)}, u32[]{:S(2)}) copy-start(f32[16,16,6,1152]{3,1,2,0:T(8,128)} %param.9) | copy-start | bytes 21233668
  3.8 1.0 %copy-start.3 = (f32[6,1152]{1,0:T(8,128)S(1)}, f32[6,1152]{1,0:T(8,128)}, u32[]{:S(2)}) copy-start(f32[6,1152]{1,0:T(8,128)} %density.5) | copy-start | bytes 82948
  4.8 0.8 %copy-start.4 = (s32[6,1152]{1,0:T(8,128)S(1)}, s32[6,1152]{1,0:T(8,128)}, u32[]{:S(2)}) copy-start(s32[6,1152]{1,0:T(8,128)} %material.5) | copy-start | bytes 82948
  5.6 0.8 %copy-start.5 = (f32[6,1152]{1,0:T(8,128)S(1)}, f32[6,1152]{1,0:T(8,128)}, u32[]{:S(2)}) copy-start(f32[6,1152]{1,0:T(8,128)} %objective.1) | copy-start | bytes 82948
  6.4 0.7 %copy-start.7 = (f32[4,16]{1,0:T(4,128)S(1)}, f32[4,16]{1,0:T(4,128)}, u32[]{:S(2)}) copy-start(f32[4,16]{1,0:T(4,128)} %table.5) | copy-start | bytes 772
  7.0 5.8 %copy-start.8 = (f32[192]{0:T(256)S(1)}, f32[192]{0:T(256)}, u32[]{:S(2)}) copy-start(f32[192]{0:T(256)} %constant.4.clone.dirs) | copy-start | bytes 2308
  7.1 5.8 %copy-start.9 = (f32[32]{0:T(128)S(1)}, f32[32]{0:T(128)}, u32[]{:S(2)}) copy-start(f32[32]{0:T(128)} %param.15) | copy-start | bytes 388
  7.1 5.8 %copy-start.10 = (f32[16]{0:T(128)S(1)}, f32[16]{0:T(128)}, u32[]{:S(2)}) copy-start(f32[16]{0:T(128)} %param.14) | copy-start | bytes 196
  9.3 17.4 %collective-permute-start = (f32[136,1152]{1,0:T(8,128)S(1)}, f32[136,1152]{1,0:T(8,128)S(1)}, u32[]{:S(2)}, u32[]{:S(2)}) collective-permute-start(f32[136,1152]{1,0:T(8,128)S(1)} %get-tuple-element.10), channel_id=1, source_target_pairs={{0,8},{16,24},{8,0},{24,16},{1,9},{17,25},{9,1},{25,17},{2,10},{18... | collective-permute-start | bytes 1880072 | tf_op jit(solution)/shard_map/ppermute | solution.py:447
  10.9 18.9 %collective-permute-start.1 = (f32[136,1152]{1,0:T(8,128)S(1)}, f32[136,1152]{1,0:T(8,128)S(1)}, u32[]{:S(2)}, u32[]{:S(2)}) collective-permute-start(f32[136,1152]{1,0:T(8,128)S(1)} %get-tuple-element.11), channel_id=1, source_target_pairs={{8,16},{16,8},{9,17},{17,9},{10,18},{18,10},{11,19},{19,11},{12,20... | collective-permute-start | bytes 1880072 | tf_op jit(solution)/shard_map/ppermute | solution.py:447
  12.9 3.0 %copy-start.2 = (f32[16,16,6,1152]{3,1,2,0:T(8,128)S(1)}, f32[16,16,6,1152]{3,1,2,0:T(8,128)}, u32[]{:S(2)}) copy-start(f32[16,16,6,1152]{3,1,2,0:T(8,128)} %param.9) | copy-start | bytes 21233668
  15.9 27.0 %copy-start.6 = (f32[6,1152]{1,0:T(8,128)S(1)}, f32[6,1152]{1,0:T(8,128)}, u32[]{:S(2)}) copy-start(f32[6,1152]{1,0:T(8,128)} %objective.1) | copy-start | bytes 82948
  22.6 15.2 %collective-permute-start.6 = (f32[128,1152]{1,0:T(8,128)S(1)}, f32[128,1152]{1,0:T(8,128)S(1)}, u32[]{:S(2)}, u32[]{:S(2)}) collective-permute-start(f32[128,1152]{1,0:T(8,128)S(1)} %get-tuple-element.13), channel_id=1, source_target_pairs={{0,8},{16,24},{8,0},{24,16},{1,9},{17,25},{9,1},{25,17},{2,10},{18... | collective-permute-start | bytes 1769480 | tf_op jit(solution)/shard_map/ppermute | solution.py:447
  22.7 18.3 %collective-permute-start.7 = (f32[128,1152]{1,0:T(8,128)S(1)}, f32[128,1152]{1,0:T(8,128)S(1)}, u32[]{:S(2)}, u32[]{:S(2)}) collective-permute-start(f32[128,1152]{1,0:T(8,128)S(1)} %get-tuple-element.14), channel_id=1, source_target_pairs={{8,16},{16,8},{9,17},{17,9},{10,18},{18,10},{11,19},{19,11},{12,20... | collective-permute-start | bytes 1769480 | tf_op jit(solution)/shard_map/ppermute | solution.py:447
  31.3 1.4 %collective-permute-start.2 = (f32[32,1152]{1,0:T(8,128)S(1)}, f32[32,1152]{1,0:T(8,128)S(1)}, u32[]{:S(2)}, u32[]{:S(2)}) collective-permute-start(f32[32,1152]{1,0:T(8,128)S(1)} %edges.1), channel_id=1, source_target_pairs={{0,1},{1,0},{2,3},{3,2},{4,5},{5,4},{6,7},{7,6},{8,9},{9,8},{10,11... | collective-permute-start | bytes 442376 | tf_op jit(solution)/shard_map/ppermute | solution.py:454
  32.7 8.3 %collective-permute-start.5 = (f32[32,1152]{1,0:T(8,128)S(1)}, f32[32,1152]{1,0:T(8,128)S(1)}, u32[]{:S(2)}, u32[]{:S(2)}) collective-permute-start(f32[32,1152]{1,0:T(8,128)S(1)} %add.15.sum0), channel_id=1, source_target_pairs={{0,6},{2,4},{4,2},{6,0},{1,7},{3,5},{5,3},{7,1},{8,14},{10,12},{12... | collective-permute-start | bytes 442376 | tf_op jit(solution)/shard_map/ppermute | solution.py:458
  35.3 7.5 %collective-permute-start.4 = (f32[32,1152]{1,0:T(8,128)S(1)}, f32[32,1152]{1,0:T(8,128)S(1)}, u32[]{:S(2)}, u32[]{:S(2)}) collective-permute-start(f32[32,1152]{1,0:T(8,128)S(1)} %add.15.sum0), channel_id=1, source_target_pairs={{0,4},{2,6},{4,0},{6,2},{1,5},{3,7},{5,1},{7,3},{8,12},{10,14},{12... | collective-permute-start | bytes 442376 | tf_op jit(solution)/shard_map/ppermute | solution.py:458
  35.8 7.1 %collective-permute-start.3 = (f32[32,1152]{1,0:T(8,128)S(1)}, f32[32,1152]{1,0:T(8,128)S(1)}, u32[]{:S(2)}, u32[]{:S(2)}) collective-permute-start(f32[32,1152]{1,0:T(8,128)S(1)} %add.15.sum0), channel_id=1, source_target_pairs={{0,2},{2,0},{4,6},{6,4},{1,3},{3,1},{5,7},{7,5},{8,10},{10,8},{12,... | collective-permute-start | bytes 442376 | tf_op jit(solution)/shard_map/ppermute | solution.py:458
  52.3 1.2 %collective-permute-start.8 = (f32[6,1152]{1,0:T(8,128)S(1)}, f32[6,1152]{1,0:T(8,128)S(1)}, u32[]{:S(2)}, u32[]{:S(2)}) collective-permute-start(f32[6,1152]{1,0:T(8,128)S(1)} %get-tuple-element.17), channel_id=1, source_target_pairs={{0,1},{1,0},{2,3},{3,2},{4,5},{5,4},{6,7},{7,6},{8,9},{9,8},{10,11... | collective-permute-start | bytes 82952 | tf_op jit(solution)/shard_map/ppermute | solution.py:454
  53.5 4.9 %collective-permute-start.11 = (f32[6,1152]{1,0:T(8,128)S(1)}, f32[6,1152]{1,0:T(8,128)S(1)}, u32[]{:S(2)}, u32[]{:S(2)}) collective-permute-start(f32[6,1152]{1,0:T(8,128)S(1)} %add.16), channel_id=1, source_target_pairs={{0,6},{2,4},{4,2},{6,0},{1,7},{3,5},{5,3},{7,1},{8,14},{10,12},{12... | collective-permute-start | bytes 82952 | tf_op jit(solution)/shard_map/ppermute | solution.py:458
  55.1 4.0 %collective-permute-start.10 = (f32[6,1152]{1,0:T(8,128)S(1)}, f32[6,1152]{1,0:T(8,128)S(1)}, u32[]{:S(2)}, u32[]{:S(2)}) collective-permute-start(f32[6,1152]{1,0:T(8,128)S(1)} %add.16), channel_id=1, source_target_pairs={{0,4},{2,6},{4,0},{6,2},{1,5},{3,7},{5,1},{7,3},{8,12},{10,14},{12... | collective-permute-start | bytes 82952 | tf_op jit(solution)/shard_map/ppermute | solution.py:458
  56.5 4.0 %collective-permute-start.9 = (f32[6,1152]{1,0:T(8,128)S(1)}, f32[6,1152]{1,0:T(8,128)S(1)}, u32[]{:S(2)}, u32[]{:S(2)}) collective-permute-start(f32[6,1152]{1,0:T(8,128)S(1)} %add.16), channel_id=1, source_target_pairs={{0,2},{2,0},{4,6},{6,4},{1,3},{3,1},{5,7},{7,5},{8,10},{10,8},{12,... | collective-permute-start | bytes 82952 | tf_op jit(solution)/shard_map/ppermute | solution.py:458

commit v3 on v2

v3 whole, which is shorter than its diff:
```python
import math

import jax
import jax.numpy as jnp
import numpy as np
from jax import lax
from jax.experimental import pallas as pl
from jax.experimental.pallas import tpu as pltpu
from jax.sharding import PartitionSpec as P

NDIR = 64
NB = 32
NY = 192
ITERS = 2
LANES = 128
SUB = 8
FIRST_GROUP = 8
SECOND_GROUP = 4
VMEM_LIMIT = 16 * 1024 * 1024


def direction_table(count):
    d = np.arange(NDIR)
    half = count // 2
    block, slot = d // count, d % count
    side, pair = slot // half, slot % half
    azimuth = np.pi * (block * half + pair + 0.5) / (NDIR // 2) - np.pi / 2
    along_z = 0.4 * (1.0 - 2.0 * (pair % 2))
    tilt = np.sqrt(1.0 - along_z * along_z)
    along_x = (1.0 - 2.0 * side) * tilt * np.cos(azimuth)
    along_y = tilt * np.sin(azimuth)
    return np.stack([along_x, along_y, along_z], axis=1).astype(np.float32).reshape(-1)


def lane_ids():
    return lax.broadcasted_iota(jnp.int32, (SUB, LANES), 1)


def lazily(make):
    made = {}

    def get(j):
        if j not in made:
            made[j] = make(j)
        return made[j]

    return get


def shifted(v, n, offset, lane, masked=None):
    q, rem = divmod(offset, LANES)
    zero = jnp.zeros((SUB, LANES), jnp.float32)
    rolled = lazily(lambda j: pltpu.roll(v(j), LANES - rem, 1) if rem else v(j))

    def tile(j):
        parts = []
        for k, low, high in ((j + q, 0, LANES - rem), (j + q + 1, LANES - rem, LANES)):
            kept = low < high and 0 <= k < n
            kept = kept and not all(masked is not None and masked(j * LANES + i) for i in range(low, high))
            parts.append(rolled(k) if kept else None)
        if parts[0] is None and parts[1] is None:
            return None
        t = parts[0]
        if rem:
            t = jnp.where(lane < LANES - rem, *[zero if part is None else part for part in parts])
        for i in range(LANES):
            if masked is not None and masked(j * LANES + i) and parts[int(i >= LANES - rem)] is not None:
                t = jnp.where(lane == i, zero, t)
        return t

    return lazily(tile)


def shift_y(v, n, rising, lane):
    if rising:
        return shifted(v, n, 1, lane, lambda p: p % NY == NY - 1)
    return shifted(v, n, -1, lane, lambda p: p % NY == 0)


def shift_z(v, n, rising, lane):
    return shifted(v, n, NY if rising else -NY, lane)


def inverse(x):
    r = pl.reciprocal(x, approx=True)
    return r * (2.0 - x * r)


def column(row, offset, n):
    shape = (n, row.shape[1])
    i0 = lax.broadcasted_iota(jnp.int32, shape, 0)
    i1 = lax.broadcasted_iota(jnp.int32, shape, 1)
    picked = jnp.sum(jnp.where(i1 == i0 + offset, row, 0.0), axis=1, keepdims=True)
    return jnp.broadcast_to(picked, (n, LANES))


def fill_columns(cols, heat, speed, table):
    nb = cols.shape[1]
    row = heat[...]
    total = jnp.sum(row, axis=1, keepdims=True) * float(NDIR)
    cols[0] = column(speed[...], 0, nb)
    cols[1] = column(row / total, lax.axis_index("band") * nb, nb)
    for m in range(table.shape[0]):
        cols[2 + m] = column(table[m : m + 1], 0, nb)


def rate_tile(cols, density, material, hs):
    return base_tile(cols, material, hs) * (0.2 + 0.8 * density)


def base_tile(cols, material, hs):
    base = jnp.broadcast_to(cols[2, hs], (SUB, LANES))
    for m in range(1, cols.shape[0] - 2):
        base = jnp.where(material == m, cols[2 + m, hs], base)
    return base


def halves(nb):
    return [slice(h * SUB, (h + 1) * SUB) for h in range(nb // SUB)]


def tiles(plane):
    return [slice(j * LANES, (j + 1) * LANES) for j in range(plane // LANES)]


def sub_sum(t):
    return jnp.sum(t, axis=0, keepdims=True)


def add_terms(terms):
    terms = [t for t in terms if t is not None]
    total = terms[0]
    for t in terms[1:]:
        total = total + t
    return total


def times(a, b):
    return None if b is None else a * b


def cosines(dirs, d):
    at = 3 * d
    return dirs[at], dirs[at + 1], dirs[at + 2]


def is_even():
    return lax.axis_index("space") % 2 == 0


def faces_kernel(
    heat_in, speed_in, table_in, density_in, material_in, objective_in, start,
    out_a, out_b, cols, density, material, objective,
    heat, speed, table, others, sems,
):
    half, nb, plane = others.shape[1:]
    last = density.shape[0] - 1
    even = is_even()
    copies = []
    for n, (src, dst) in enumerate(
        (
            (heat_in, heat), (speed_in, speed), (table_in, table),
            (density_in, density), (material_in, material), (objective_in, objective),
        )
    ):
        copies.append(pltpu.make_async_copy(src, dst, sems.at[n]))
    for side, out in enumerate((out_a, out_b)):
        upper = even if side == 0 else jnp.logical_not(even)
        first, second, x = jnp.where(upper, half, 0), jnp.where(upper, 0, half), jnp.where(upper, last, 0)
        at = 6 + side * (half + 1)
        for d in range(half):
            copies.append(
                pltpu.make_async_copy(start.at[first + d, x], out.at[pl.ds(d * nb, nb)], sems.at[at + d])
            )
        copies.append(pltpu.make_async_copy(start.at[pl.ds(second, half), x], others.at[side], sems.at[at + half]))
    for copy in copies:
        copy.start()
    for copy in copies:
        copy.wait()
    fill_columns(cols, heat, speed, table)
    for side, out in enumerate((out_a, out_b)):
        upper = even if side == 0 else jnp.logical_not(even)
        row = lambda ref, cs: jnp.where(upper, ref[last : last + 1, cs], ref[0:1, cs])
        base = half * nb
        for cs in tiles(plane):
            dens, mat = row(density, cs), row(material, cs)
            share = 0.0
            for h, hs in enumerate(halves(nb)):
                total = others[side, 0, hs, cs]
                for d in range(1, half):
                    total = total + others[side, d, hs, cs]
                for d in range(half):
                    total = total + out[d * nb + h * SUB : d * nb + (h + 1) * SUB, cs]
                share = share + rate_tile(cols, dens, mat, hs) * total
            out[base : base + 1, cs] = sub_sum(share)
            out[base + 1 : base + 2, cs] = dens
            out[base + 2 : base + 3, cs] = mat.astype(jnp.float32)
            out[base + 3 : base + 4, cs] = row(objective, cs)
            out[base + 4 : base + 8, cs] = jnp.zeros((4, LANES), jnp.float32)


def first_kernel(
    dirs, cols, density, material, start, excess_in, flow, excess, face_a, face_b, sums, field, rate, acc, sems
):
    count, nx, nb, plane = field.shape
    half = count // 2
    per = math.gcd(FIRST_GROUP, half)
    groups = count // per
    cuts, bands = tiles(plane), halves(nb)
    n = len(cuts)

    def fetch(x, which):
        src, dst = ((start, field), (excess_in, excess))[which]
        return pltpu.make_async_copy(src.at[:, x], dst.at[:, x], sems.at[which, x])

    for x, which in ((0, 0), (1, 0), (0, 1), (2, 0), (1, 1)):
        if x < nx:
            fetch(x, which).start()
    for x in range(nx):
        for cs in cuts:
            for hs in bands:
                rate[x, hs, cs] = rate_tile(cols, density[x : x + 1, cs], material[x : x + 1, cs], hs)
    acc[...] = jnp.zeros_like(acc)
    block = lax.axis_index("dir")
    lane = lane_ids()
    fetch(0, 0).wait()

    def layer(x, _):
        pl.when(x + 3 < nx)(lambda: fetch(x + 3, 0).start())
        pl.when(x + 2 < nx)(lambda: fetch(x + 2, 1).start())
        pl.when(x + 1 < nx)(lambda: fetch(x + 1, 0).wait())
        fetch(x, 1).wait()

        def group(k, _):
            first = k * per
            ahead = first < half
            edge = jnp.where(ahead, x == nx - 1, x == 0)
            beside = jnp.where(edge, x, jnp.where(ahead, x + 1, x - 1))

            def run(rising):
                for hs in bands:
                    pace = cols[0, hs]
                    ways = []
                    for dd in range(per):
                        ax, ay, az = [jnp.abs(a) for a in cosines(dirs, block * count + first + dd)]
                        v = lazily(lambda j, dd=dd: field[first + dd, x, hs, cuts[j]])
                        speeds = (pace * jnp.where(edge, 0.0, ax), pace * ay, pace * az, pace * (ax + ay + az))
                        ways.append((v, shift_y(v, n, rising, lane), shift_z(v, n, dd % 2 == 0, lane), speeds))
                    for j, cs in enumerate(cuts):
                        r = rate[x, hs, cs]
                        kept = []
                        for dd, (v, along_y, along_z, (cx, cy, cz, speeds)) in enumerate(ways):
                            d = first + dd
                            inv = inverse(speeds + r)
                            a = inv * add_terms(
                                [times(cx, field[d, beside, hs, cs]), times(cy, along_y(j)), times(cz, along_z(j))]
                            )
                            flow[d, x, hs, cs] = a
                            kept.append((v(j), excess[d, x, hs, cs], a, inv))
                        for f in range(4):
                            acc[f, x, hs, cs] += add_terms([k[f] for k in kept])

            rises = cosines(dirs, block * count + first)[1] > 0
            pl.when(rises)(lambda: run(True))
            pl.when(jnp.logical_not(rises))(lambda: run(False))
            return 0

        lax.fori_loop(0, groups, group, 0)
        return 0

    lax.fori_loop(0, nx, layer, 0)
    even = is_even()
    for face, upper in ((face_a, even), (face_b, jnp.logical_not(even))):
        first, x = jnp.where(upper, half, 0), jnp.where(upper, nx - 1, 0)
        for d in range(half):
            face[d * nb : (d + 1) * nb] = flow[first + d, x]
    for x in range(nx):
        for cs in cuts:
            totals = [0.0] * 4
            for hs in bands:
                r, w = rate[x, hs, cs], cols[1, hs]
                for f, scale in enumerate((r, w, r, r * w)):
                    totals[f] = totals[f] + scale * acc[f, x, hs, cs]
            for f in range(4):
                sums[f * nx + x : f * nx + x + 1, cs] = sub_sum(totals[f])
    sums[4 * nx :] = jnp.zeros((sums.shape[0] - 4 * nx, plane), jnp.float32)


def edges_kernel(dirs, cols, density, material, halo_a, halo_b, sums, out):
    nx, plane = density.shape
    nb = cols.shape[1]
    half = (halo_a.shape[0] - SUB) // nb
    count = 2 * half
    block = lax.axis_index("dir")
    even = is_even()
    out[...] = sums[...]
    cuts = tiles(plane)
    gains = []
    for side, halo in enumerate((halo_a, halo_b)):
        ahead = even if side == 0 else jnp.logical_not(even)
        rates = []
        for hs in halves(nb):
            rates.append([])
            for cs in cuts:
                mat = jnp.where(ahead, material[nx - 1 : nx, cs], material[0:1, cs])
                dens = jnp.where(ahead, density[nx - 1 : nx, cs], density[0:1, cs])
                rates[-1].append(rate_tile(cols, dens, mat, hs))
        first = block * count + jnp.where(ahead, 0, half)

        def add(d, totals):
            ax, ay, az = [jnp.abs(a) for a in cosines(dirs, first + d)]
            new = list(totals)
            for h, hs in enumerate(halves(nb)):
                pace = cols[0, hs]
                cx, speeds = pace * ax, pace * (ax + ay + az)
                rows = halo.at[pl.ds(pl.multiple_of(d * nb + h * SUB, SUB), SUB)]
                for j, cs in enumerate(cuts):
                    r = rates[h][j]
                    new[j] = new[j] + (cx * rows[:, cs]) * (r * inverse(speeds + r))
            return tuple(new)

        totals = lax.fori_loop(0, half, add, tuple(jnp.zeros((SUB, LANES), jnp.float32) for _ in cuts))
        gains.append([sub_sum(t) for t in totals])
    base = half * nb
    for side, x in enumerate((nx - 1, 0)):
        near, far = (0, 1) if side == 0 else (1, 0)
        row = 2 * nx + x
        for j, cs in enumerate(cuts):
            out[row : row + 1, cs] = out[row : row + 1, cs] + jnp.where(even, gains[near][j], gains[far][j])
            a, b = halo_a[base : base + 1, cs], halo_b[base : base + 1, cs]
            out[4 * nx + side : 4 * nx + side + 1, cs] = jnp.where(even, a, b) if side == 0 else jnp.where(even, b, a)


def second_kernel(
    dirs, cols, density, material, objective, sum0, sum1, sum2, sum3, halo0_a, halo0_b, flow, excess,
    dual, edge_dual, known, gradient,
    rate, source0, source1, warm, prev, seed, acc,
):
    g = pl.program_id(0)
    steps = pl.num_programs(0)
    count, nx, nb, plane = flow.shape
    per = count // steps
    cuts, bands = tiles(plane), halves(nb)
    n = len(cuts)
    scale = float(NDIR * NB)
    edge = halo0_a.shape[0] - SUB

    @pl.when(g == 0)
    def _():
        total = (sum0[...] + sum1[...]) + (sum2[...] + sum3[...])
        for x in range(nx):
            warm[x] = jnp.broadcast_to(total[nx + x : nx + x + 1], (SUB, plane))
        known[0:1] = total[2 * nx - 1 : 2 * nx]
        known[1:2] = total[nx : nx + 1]
        for side in range(2):
            from_a = is_even() if side == 0 else jnp.logical_not(is_even())
            aim = jnp.where(from_a, halo0_a[edge + 3 : edge + 4], halo0_b[edge + 3 : edge + 4])
            known[2 + side : 3 + side] = total[4 * nx + side : 4 * nx + side + 1] + scale * aim
        known[4:8] = jnp.zeros((4, plane), jnp.float32)
        for x in range(nx):
            for cs in cuts:
                drive = total[x : x + 1, cs] + scale * objective[x : x + 1, cs]
                again = (
                    total[2 * nx + x : 2 * nx + x + 1, cs]
                    + drive * total[3 * nx + x : 3 * nx + x + 1, cs]
                    + scale * objective[x : x + 1, cs]
                )
                for hs in bands:
                    w = cols[1, hs]
                    rate[x, hs, cs] = rate_tile(cols, density[x : x + 1, cs], material[x : x + 1, cs], hs)
                    source0[x, hs, cs] = w * drive
                    source1[x, hs, cs] = w * again
        acc[...] = jnp.zeros_like(acc)

    block = lax.axis_index("dir")
    first = block * count + g * per
    ahead = g < steps // 2
    lane = lane_ids()

    def enter(halo0):
        skip = jnp.where(ahead, 0, steps // 2)
        for dd in range(per):
            ax = jnp.abs(cosines(dirs, first + dd)[0])
            for h, hs in enumerate(bands):
                cx = cols[0, hs] * ax
                rows = pl.ds(pl.multiple_of(((g - skip) * per + dd) * nb + h * SUB, SUB), SUB)
                for cs in cuts:
                    seed[dd, hs, cs] = cx * halo0[rows, cs]

    pl.when(ahead == is_even())(lambda: enter(halo0_a))
    pl.when(ahead != is_even())(lambda: enter(halo0_b))

    def run(rising):
        def layer(i, at_edge):
            x = jnp.where(ahead, nx - 1 - i, i)
            for hs in bands:
                pace = cols[0, hs]
                rates = lazily(lambda j: rate[x, hs, cuts[j]])
                sources = lazily(lambda j: source0[x, hs, cuts[j]])
                ways = []
                for dd in range(per):
                    ax, ay, az = [jnp.abs(a) for a in cosines(dirs, first + dd)]
                    speeds = pace * (ax + ay + az)
                    inv = lazily(lambda j, speeds=speeds: inverse(speeds + rates(j)))

                    def fresh(j, dd=dd, inv=inv):
                        s = sources(j)
                        if at_edge:
                            s = s + seed[dd, hs, cuts[j]]
                        return flow[g * per + dd, x, hs, cuts[j]] + s * inv(j)

                    v = lazily(fresh)
                    shifts = (shift_y(v, n, rising, lane), shift_z(v, n, dd % 2 == 0, lane))
                    ways.append((v, inv, *shifts, (pace * ax, pace * ay, pace * az)))
                for j, cs in enumerate(cuts):
                    kept = []
                    again, level = source1[x, hs, cs], warm[x, :, cs]
                    for dd, (v, inv, along_y, along_z, (cx, cy, cz)) in enumerate(ways):
                        beside = None if at_edge else cx * prev[dd, hs, cs]
                        new = inv(j) * add_terms([beside, times(cy, along_y(j)), times(cz, along_z(j)), again])
                        prev[dd, hs, cs] = v(j)
                        dual[dd, x, hs, cs] = new
                        if at_edge:
                            edge_dual[g * per + dd, hs, cs] = new
                        kept.append((v(j) + new) * (excess[g * per + dd, x, hs, cs] - level))
                    acc[x, hs, cs] += add_terms(kept)

        layer(0, True)

        def later(i, _):
            layer(i, False)
            return 0

        lax.fori_loop(1, nx, later, 0)

    rises = cosines(dirs, first)[1] > 0
    pl.when(rises)(lambda: run(True))
    pl.when(jnp.logical_not(rises))(lambda: run(False))

    @pl.when(g == steps - 1)
    def _():
        for x in range(nx):
            for cs in cuts:
                total = 0.0
                for hs in bands:
                    total = total + base_tile(cols, material[x : x + 1, cs], hs) * acc[x, hs, cs]
                gradient[x : x + 1, cs] = sub_sum(total) * 0.8


def last_kernel(
    dirs, cols, density, material, halo0_a, halo0_b, halo1_a, halo1_b, excess, edge_dual, known, gradient, dual_in,
    dual, out, done, sems,
):
    nx, plane = density.shape
    count, nb = edge_dual.shape[:2]
    half = count // 2
    cuts, bands = tiles(plane), halves(nb)
    params = halo0_a.shape[0] - SUB
    block = lax.axis_index("dir")
    even = is_even()
    copies = []
    gains = []
    for part, (halo0, halo1) in enumerate(((halo0_a, halo1_a), (halo0_b, halo1_b))):
        ahead = even if part == 0 else jnp.logical_not(even)
        first, x = jnp.where(ahead, 0, half), jnp.where(ahead, nx - 1, 0)

        def pick(ref, i, k, cs):
            return jnp.where(ahead, ref[i : i + 1, cs], ref[k : k + 1, cs])

        sums = []
        for cs in cuts:
            dens, mat = pick(density, nx - 1, 0, cs), pick(material, nx - 1, 0, cs)
            beyond = halo0[params + 1 : params + 2, cs]
            beyond_mat = halo0[params + 2 : params + 3, cs].astype(jnp.int32)
            level, drive = pick(known, 0, 1, cs), pick(known, 2, 3, cs)
            share = 0.0
            for h, hs in enumerate(bands):
                pace, base = cols[0, hs], base_tile(cols, mat, hs)
                r, r_beyond = base * (0.2 + 0.8 * dens), rate_tile(cols, beyond, beyond_mat, hs)
                source = cols[1, hs] * drive

                def add(d, total):
                    ax, ay, az = [jnp.abs(a) for a in cosines(dirs, block * count + first + d)]
                    speeds, cx = pace * (ax + ay + az), pace * ax
                    rows = pl.ds(pl.multiple_of(d * nb + h * SUB, SUB), SUB)
                    v = halo1[rows, cs] + source * inverse(speeds + r_beyond)
                    new = (cx * v) * inverse(speeds + r)
                    done[first + d, hs, cs] = edge_dual[first + d, hs, cs] + new
                    return total + new * (excess[first + d, x, hs, cs] - level)

                total = lax.fori_loop(0, half, add, jnp.zeros((SUB, LANES), jnp.float32), unroll=True)
                share = share + base * total
            sums.append(sub_sum(share) * 0.8)
        gains.append(sums)
        copy = pltpu.make_async_copy(done.at[pl.ds(first, half)], dual.at[pl.ds(first, half), x], sems.at[part])
        copy.start()
        copies.append(copy)
    out[...] = gradient[...]
    for j, cs in enumerate(cuts):
        out[nx - 1 : nx, cs] = out[nx - 1 : nx, cs] + jnp.where(even, gains[0][j], gains[1][j])
        out[0:1, cs] = out[0:1, cs] + jnp.where(even, gains[1][j], gains[0][j])
    for copy in copies:
        copy.wait()


def swapped(value, start):
    count = lax.axis_size("space")
    pairs = [(s, s + 1) for s in range(start, count - 1, 2)]
    return lax.ppermute(value, "space", pairs + [(b, a) for a, b in pairs])


def shares(partial):
    size = lax.axis_size("band")
    total = partial
    for k in range(1, size):
        total = total + lax.ppermute(partial, "band", [(s, (s + k) % size) for s in range(size)])
    count = lax.axis_size("dir")
    pairs = count & (count - 1) == 0
    hops = [[(s, s ^ k if pairs else (s + k) % count) for s in range(count)] for k in range(1, count)]
    return [total] + [lax.ppermute(total, "dir", hop) for hop in hops]


def whole(array):
    return pl.BlockSpec(array.shape, lambda *g: (0,) * array.ndim)


def on_device(
    adjoint_start, primal_deviations, density, material, rate_table, group_speed, heat_capacity, objective_weight
):
    count, nb, nx, plane = adjoint_start.shape
    half = count // 2
    first_steps = count // math.gcd(FIRST_GROUP, half)
    second_steps = count // math.gcd(SECOND_GROUP, half)
    nmat = rate_table.shape[0]
    start = adjoint_start.transpose(0, 2, 1, 3)
    excess = primal_deviations.transpose(0, 2, 1, 3)
    f32 = jnp.float32
    vmem = pl.BlockSpec(memory_space=pltpu.VMEM)
    smem = pl.BlockSpec(memory_space=pltpu.SMEM)
    vmem = pl.BlockSpec(memory_space=pltpu.VMEM)
    hbm = pl.BlockSpec(memory_space=pltpu.HBM)
    dirs = jnp.asarray(direction_table(count))
    params = pltpu.CompilerParams(vmem_limit_bytes=VMEM_LIMIT)
    size = count * nb * nx * plane

    def stay(*arrays):
        return [pltpu.with_memory_space_constraint(a, pltpu.HBM) for a in arrays]

    def like(*shape):
        return jax.ShapeDtypeStruct(shape, f32)

    def cost(work, moved):
        return pl.CostEstimate(flops=int(size * work), bytes_accessed=int(size * moved), transcendentals=0)

    small = (heat_capacity.reshape(1, -1), group_speed.reshape(1, -1), rate_table)
    cells = (density, material, objective_weight)
    face_a, face_b, cols, density, material, objective = pl.pallas_call(
        faces_kernel,
        out_shape=(
            like(half * nb + SUB, plane), like(half * nb + SUB, plane), like(2 + nmat, nb, LANES),
            *(jax.ShapeDtypeStruct(a.shape, a.dtype) for a in cells),
        ),
        in_specs=[hbm] * 7,
        out_specs=[vmem] * 6,
        scratch_shapes=[pltpu.VMEM(a.shape, a.dtype) for a in small]
        + [pltpu.VMEM((2, half, nb, plane), f32), pltpu.SemaphoreType.DMA((6 + 2 * (half + 1),))],
        compiler_params=params,
        cost_estimate=cost(0.3, 2),
        name="faces",
    )(*stay(*small, *cells, start))
    halo0_a, halo0_b = swapped(face_a, 0), swapped(face_b, 1)

    sum_rows = -(-(4 * nx + 2) // SUB) * SUB
    flow, excess, face_a, face_b, sums = pl.pallas_call(
        first_kernel,
        out_shape=(
            like(*start.shape), like(*start.shape), like(half * nb, plane), like(half * nb, plane), like(sum_rows, plane)
        ),
        in_specs=[smem] + [vmem] * 3 + [hbm] * 2,
        out_specs=[vmem] * 5,
        scratch_shapes=[
            pltpu.VMEM(start.shape, f32), pltpu.VMEM((nx, nb, plane), f32), pltpu.VMEM((4, nx, nb, plane), f32),
            pltpu.SemaphoreType.DMA((2, nx)),
        ],
        compiler_params=params,
        cost_estimate=cost(20, 12),
        name="first",
    )(dirs, cols, density, material, *stay(start, excess))
    halo1_a, halo1_b = swapped(face_a, 0), swapped(face_b, 1)

    sums = pl.pallas_call(
        edges_kernel,
        out_shape=like(sum_rows, plane),
        in_specs=[smem] + [vmem] * 6,
        out_specs=vmem,
        compiler_params=params,
        cost_estimate=cost(1, 1),
        name="edges",
    )(dirs, cols, density, material, halo0_a, halo0_b, sums)
    parts = shares(sums)
    parts = parts + [jnp.zeros_like(sums)] * (4 - len(parts))
    parts = parts[:3] + [sum(parts[4:], parts[3])]

    second_steps = count // math.gcd(SECOND_GROUP, half)
    per = count // second_steps
    layer = pltpu.VMEM((nx, nb, plane), f32)
    dual, edge_dual, known, gradient = pl.pallas_call(
        second_kernel,
        grid=(second_steps,),
        out_shape=(like(*start.shape), like(count, nb, plane), like(SUB, plane), like(nx, plane)),
        in_specs=[smem] + [vmem] * 12,
        out_specs=[pl.BlockSpec((per, nx, nb, plane), lambda g: (g, 0, 0, 0))] + [vmem] * 3,
        scratch_shapes=[
            layer, layer, layer, pltpu.VMEM((nx, SUB, plane), f32),
            pltpu.VMEM((per, nb, plane), f32), pltpu.VMEM((per, nb, plane), f32), layer,
        ],
        compiler_params=params,
        cost_estimate=cost(30, 12),
        name="second",
    )(dirs, cols, density, material, objective, *parts, halo0_a, halo0_b, flow, excess)

    dual, gradient = pl.pallas_call(
        last_kernel,
        out_shape=(like(*start.shape), like(nx, plane)),
        in_specs=[smem] + [vmem] * 11 + [hbm],
        out_specs=[hbm, vmem],
        scratch_shapes=[pltpu.VMEM((count, nb, plane), f32), pltpu.SemaphoreType.DMA((2,))],
        input_output_aliases={12: 0},
        compiler_params=params,
        cost_estimate=cost(1, 1),
        name="last",
    )(dirs, cols, density, material, halo0_a, halo0_b, halo1_a, halo1_b, excess, edge_dual, known, gradient, dual)
    gradient = sum(shares(gradient)) * (-0.125 / ITERS)
    return (dual.transpose(0, 2, 1, 3), gradient)


def solution(mesh):
    placed = (
        P("dir", "band", "space", None),
        P("dir", "band", "space", None),
        P("space", None),
        P("space", None),
        P(None, "band"),
        P("band"),
        P(),
        P("space", None),
    )
    return jax.shard_map(
        on_device,
        mesh=mesh,
        in_specs=placed,
        out_specs=(P("dir", "band", "space", None), P("space", None)),
        check_vma=False,
    )
```

time: 61.3 us -> 56.9 us (0.928)
  local copies, waits for them, and re-layouts: 9.42 us -> 0.01 us
  Pallas kernels: 19.8 us -> 23.4 us
  waiting for transfers between devices: 15.8 us -> 17.1 us
    unnamed x22 -> x2, local copies, waits for them, and re-layouts: 9.42 us -> 0.01 us
    ppermute x6, waiting for transfers between devices: 5.26 us -> 9.99 us  [shares(): return [total] + [lax.ppermute(total, 'dir', hop) for hop in hops]]
    pallas_call x4 -> x5, Pallas kernels: 19.8 us -> 23.4 us  [the longest x1 8.98 us: on_device(): pl.pallas_call(second_kernel, grid=(second_steps,), out_shape=(like(*star...]
    ppermute x4, waiting for transfers between devices: 7.94 us -> 4.59 us  [swapped(): return lax.ppermute(value, 'space', pairs + [(b, a) for a, b in pairs])]
  transfers between devices with their start and end apart: 12 -> 12, of which waited for: 10 -> 10; matrix products, arithmetic and copies ran while one was open for 0% -> 0% of each run, Pallas kernels for 13% -> 33%
where the time goes in v3:
time: 56.9 us; the launch traced here: 56.7 us
  Pallas kernels  23.4 us (41%)
  waiting for transfers between devices  17.1 us (30%)
  starting transfers between devices  14.7 us (26%)
  between operations  0.73 us (1%)
  other arithmetic  0.65 us (1%)
    ppermute x6, waiting for transfers between devices, shares(): return [total] + [lax.ppermute(total, 'dir', hop) for hop in hops]  9.99 us
    pallas_call x1, Pallas kernels, on_device(): pl.pallas_call(second_kernel, grid=(second_steps,), out_shape=(like(*star...  8.98 us
    pallas_call x1, Pallas kernels, on_device(): pl.pallas_call(first_kernel, out_shape=(like(*start.shape), like(*start.s...  8.4 us
    ppermute x4, starting transfers between devices, swapped(): return lax.ppermute(value, 'space', pairs + [(b, a) for a, b in pairs])  7.54 us
    ppermute x6, starting transfers between devices, shares(): return [total] + [lax.ppermute(total, 'dir', hop) for hop in hops]  7.04 us
    ppermute x4, waiting for transfers between devices, swapped(): return lax.ppermute(value, 'space', pairs + [(b, a) for a, b in pairs])  4.59 us
    ppermute x2, waiting for transfers between devices, shares(): lax.ppermute(partial, 'band', [(s, (s + k) % size) for s in range(size)])  2.56 us
    pallas_call x1, Pallas kernels, on_device(): pl.pallas_call(last_kernel, out_shape=(like(*start.shape), like(nx, plane...  2.46 us
  transfers between devices with their start and end apart: 12, of which 10 were waited for; matrix products, arithmetic and copies ran while one was open for 0% of the time, Pallas kernels for 33%

profile of v3, /device:TPU:16, one launch (start us, length us, event | category | flops | bytes accessed | tf_op | source)
XLA Modules:
  0.0 56.7 jit_solution(6819019843703463841)
XLA Ops:
  0.6 2.3 %faces.1 = (f32[136,1152]{1,0:T(8,128)S(1)}, f32[136,1152]{1,0:T(8,128)S(1)}, f32[6,16,128]{2,1,0:T(8,128)S(1)}, f32[6,1152]{1,0:T(8,128)S(1)}, s32[6,1152]{1,0:T(8,128)S(1)}, /*index=5*/f32[6,1152]{1,0:T(8,128)S(1)}) custom-call(f32[1,32]{1,0:T(1,128)} %bitcast.9, f32[1,16]{1,0:T(1,128)} %bitcast.10, f32[4,16]{1,0:T(4,128)} %table_in.1, ...), custom_call_target="tpu_custom_call" | custom-call | flops 530841 | bytes 3538944 | tf_op jit(solution)/shard_map/faces/pallas_call | solution.py:557
  2.9 1.6 %collective-permute-start = (f32[136,1152]{1,0:T(8,128)S(1)}, f32[136,1152]{1,0:T(8,128)S(1)}, u32[]{:S(2)}, u32[]{:S(2)}) collective-permute-start(f32[136,1152]{1,0:T(8,128)S(1)} %get-tuple-element.22), channel_id=1, source_target_pairs={{0,8},{16,24},{8,0},{24,16},{1,9},{17,25},{9,1},{25,17},{2,10},{18... | collective-permute-start | bytes 1880072 | tf_op jit(solution)/shard_map/ppermute | solution.py:509
  4.6 1.9 %collective-permute-start.1 = (f32[136,1152]{1,0:T(8,128)S(1)}, f32[136,1152]{1,0:T(8,128)S(1)}, u32[]{:S(2)}, u32[]{:S(2)}) collective-permute-start(f32[136,1152]{1,0:T(8,128)S(1)} %get-tuple-element.23), channel_id=1, source_target_pairs={{8,16},{16,8},{9,17},{17,9},{10,18},{18,10},{11,19},{19,11},{12,20... | collective-permute-start | bytes 1880072 | tf_op jit(solution)/shard_map/ppermute | solution.py:509
  6.5 8.4 %first.1 = (f32[16,6,16,1152]{3,2,1,0:T(8,128)S(1)}, f32[16,6,16,1152]{3,2,1,0:T(8,128)S(1)}, f32[128,1152]{1,0:T(8,128)S(1)}, f32[128,1152]{1,0:T(8,128)S(1)}, f32[32,1152]{1,0:T(8,128)S(1)}) custom-call(f32[192]{0:T(256)S(1)} %copy-done, f32[6,16,128]{2,1,0:T(8,128)S(1)} %get-tuple-element.19.cols, f32[6,1152]{1,0:T(8,128)S(1)} %get-tuple-element.20.density, ...), custom_call_target="tpu_custom_call" | custom-call | flops 35389440 | bytes 21233664 | tf_op jit(solution)/shard_map/first/pallas_call | solution.py:574
  15.0 3.9 %collective-permute-start.3 = (f32[128,1152]{1,0:T(8,128)S(1)}, f32[128,1152]{1,0:T(8,128)S(1)}, u32[]{:S(2)}, u32[]{:S(2)}) collective-permute-start(f32[128,1152]{1,0:T(8,128)S(1)} %get-tuple-element.25), channel_id=1, source_target_pairs={{8,16},{16,8},{9,17},{17,9},{10,18},{18,10},{11,19},{19,11},{12,20... | collective-permute-start | bytes 1769480 | tf_op jit(solution)/shard_map/ppermute | solution.py:509
  18.9 1.1 %collective-permute-done.halo_a.halo0_a = f32[136,1152]{1,0:T(8,128)S(1)} collective-permute-done((f32[136,1152]{1,0:T(8,128)S(1)}, f32[136,1152]{1,0:T(8,128)S(1)}, u32[]{:S(2)}, u32[]{:S(2)}) %collective-permute-start) | collective-permute-done | bytes 626720 | tf_op jit(solution)/shard_map/ppermute | solution.py:509
  20.0 3.5 %collective-permute-done.1.halo_b.halo0_b = f32[136,1152]{1,0:T(8,128)S(1)} collective-permute-done((f32[136,1152]{1,0:T(8,128)S(1)}, f32[136,1152]{1,0:T(8,128)S(1)}, u32[]{:S(2)}, u32[]{:S(2)}) %collective-permute-start.1) | collective-permute-done | bytes 626720 | tf_op jit(solution)/shard_map/ppermute | solution.py:509
  23.5 1.3 %edges.1 = f32[32,1152]{1,0:T(8,128)S(1)} custom-call(f32[192]{0:T(256)S(1)} %copy-done, f32[6,16,128]{2,1,0:T(8,128)S(1)} %get-tuple-element.19.cols, f32[6,1152]{1,0:T(8,128)S(1)} %get-tuple-element.20.density, s32[6,1152]{1,0:T(8,128)S(1)} %get-tuple-element.21.material, f32[136,1152]{1,0:T(8,128)S(1)} %collective-permute-done.halo_a.halo0_a, ...), custom_call_target="tpu_custom_call" | custom-call | flops 1769472 | bytes 1769472 | tf_op jit(solution)/shard_map/edges/pallas_call | solution.py:591
  24.9 1.4 %collective-permute-done.4 = f32[32,1152]{1,0:T(8,128)S(1)} collective-permute-done((f32[32,1152]{1,0:T(8,128)S(1)}, f32[32,1152]{1,0:T(8,128)S(1)}, u32[]{:S(2)}, u32[]{:S(2)}) %collective-permute-start.4) | collective-permute-done | bytes 147488 | tf_op jit(solution)/shard_map/ppermute | solution.py:516
  26.3 2.5 %collective-permute-start.7 = (f32[32,1152]{1,0:T(8,128)S(1)}, f32[32,1152]{1,0:T(8,128)S(1)}, u32[]{:S(2)}, u32[]{:S(2)}) collective-permute-start(f32[32,1152]{1,0:T(8,128)S(1)} %add.15.sum0), channel_id=1, source_target_pairs={{0,6},{2,4},{4,2},{6,0},{1,7},{3,5},{5,3},{7,1},{8,14},{10,12},{12... | collective-permute-start | bytes 442376 | tf_op jit(solution)/shard_map/ppermute | solution.py:520
  28.8 0.5 collective-permute-start.6
  29.3 0.5 collective-permute-start.5
  29.8 4.0 %collective-permute-done.7.sum3 = f32[32,1152]{1,0:T(8,128)S(1)} collective-permute-done((f32[32,1152]{1,0:T(8,128)S(1)}, f32[32,1152]{1,0:T(8,128)S(1)}, u32[]{:S(2)}, u32[]{:S(2)}) %collective-permute-start.7) | collective-permute-done | bytes 147488 | tf_op jit(solution)/shard_map/ppermute | solution.py:520
  33.8 2.5 %collective-permute-done.6.sum2 = f32[32,1152]{1,0:T(8,128)S(1)} collective-permute-done((f32[32,1152]{1,0:T(8,128)S(1)}, f32[32,1152]{1,0:T(8,128)S(1)}, u32[]{:S(2)}, u32[]{:S(2)}) %collective-permute-start.6) | collective-permute-done | bytes 147488 | tf_op jit(solution)/shard_map/ppermute | solution.py:520
  36.4 9.0 %second.1 = (f32[16,6,16,1152]{3,2,1,0:T(8,128)}, f32[16,16,1152]{2,1,0:T(8,128)S(1)}, f32[8,1152]{1,0:T(8,128)S(1)}, f32[6,1152]{1,0:T(8,128)S(1)}) custom-call(f32[192]{0:T(256)S(1)} %copy-done, f32[6,16,128]{2,1,0:T(8,128)S(1)} %get-tuple-element.19.cols, f32[6,1152]{1,0:T(8,128)S(1)} %get-tuple-element.20.density, ...), custom_call_target="tpu_custom_call" | custom-call | flops 53084160 | bytes 21233664 | tf_op jit(solution)/shard_map/second/pallas_call | solution.py:607
  45.4 2.5 %last.1 = (f32[16,6,16,1152]{3,2,1,0:T(8,128)}, f32[6,1152]{1,0:T(8,128)S(1)}) custom-call(f32[192]{0:T(256)S(1)} %copy-done, f32[6,16,128]{2,1,0:T(8,128)S(1)} %get-tuple-element.19.cols, f32[6,1152]{1,0:T(8,128)S(1)} %get-tuple-element.20.density, s32[6,1152]{1,0:T(8,128)S(1)} %get-tuple-element.21.material, ...), custom_call_target="tpu_custom_call", output_to_operand_aliasing={{0}: (12, {})} | custom-call | flops 1769472 | bytes 1769472 | tf_op jit(solution)/shard_map/last/pallas_call | solution.py:622
  47.9 1.2 %collective-permute-done.8 = f32[6,1152]{1,0:T(8,128)S(1)} collective-permute-done((f32[6,1152]{1,0:T(8,128)S(1)}, f32[6,1152]{1,0:T(8,128)S(1)}, u32[]{:S(2)}, u32[]{:S(2)}) %collective-permute-start.8) | collective-permute-done | bytes 27680 | tf_op jit(solution)/shard_map/ppermute | solution.py:516
  49.1 1.7 %collective-permute-start.11 = (f32[6,1152]{1,0:T(8,128)S(1)}, f32[6,1152]{1,0:T(8,128)S(1)}, u32[]{:S(2)}, u32[]{:S(2)}) collective-permute-start(f32[6,1152]{1,0:T(8,128)S(1)} %add.16), channel_id=1, source_target_pairs={{0,6},{2,4},{4,2},{6,0},{1,7},{3,5},{5,3},{7,1},{8,14},{10,12},{12... | collective-permute-start | bytes 82952 | tf_op jit(solution)/shard_map/ppermute | solution.py:520
  50.8 1.3 %collective-permute-start.10 = (f32[6,1152]{1,0:T(8,128)S(1)}, f32[6,1152]{1,0:T(8,128)S(1)}, u32[]{:S(2)}, u32[]{:S(2)}) collective-permute-start(f32[6,1152]{1,0:T(8,128)S(1)} %add.16), channel_id=1, source_target_pairs={{0,4},{2,6},{4,0},{6,2},{1,5},{3,7},{5,1},{7,3},{8,12},{10,14},{12... | collective-permute-start | bytes 82952 | tf_op jit(solution)/shard_map/ppermute | solution.py:520
  52.1 0.5 collective-permute-start.9
  52.6 1.4 %collective-permute-done.11 = f32[6,1152]{1,0:T(8,128)S(1)} collective-permute-done((f32[6,1152]{1,0:T(8,128)S(1)}, f32[6,1152]{1,0:T(8,128)S(1)}, u32[]{:S(2)}, u32[]{:S(2)}) %collective-permute-start.11) | collective-permute-done | bytes 27680 | tf_op jit(solution)/shard_map/ppermute | solution.py:520
  54.1 0.7 %collective-permute-done.10 = f32[6,1152]{1,0:T(8,128)S(1)} collective-permute-done((f32[6,1152]{1,0:T(8,128)S(1)}, f32[6,1152]{1,0:T(8,128)S(1)}, u32[]{:S(2)}, u32[]{:S(2)}) %collective-permute-start.10) | collective-permute-done | bytes 27680 | tf_op jit(solution)/shard_map/ppermute | solution.py:520
  54.8 1.3 %collective-permute-done.9 = f32[6,1152]{1,0:T(8,128)S(1)} collective-permute-done((f32[6,1152]{1,0:T(8,128)S(1)}, f32[6,1152]{1,0:T(8,128)S(1)}, u32[]{:S(2)}, u32[]{:S(2)}) %collective-permute-start.9) | collective-permute-done | bytes 27680 | tf_op jit(solution)/shard_map/ppermute | solution.py:520
  56.0 0.6 %add_multiply_fusion = f32[6,1152]{1,0:T(8,128)} fusion(f32[6,1152]{1,0:T(8,128)S(1)} %collective-permute-done.11, f32[6,1152]{1,0:T(8,128)S(1)} %collective-permute-done.10, f32[6,1152]{1,0:T(8,128)S(1)} %add.16, f32[6,1152]{1,0:T(8,128)S(1)} %collective-permute-done.9), kind=kLoop, calls=%fused_computation | loop fusion | flops 27648 | bytes 138240 | tf_op jit(solution)/shard_map/mul | solution.py:633
  (10 shorter events, 0.4 us)
Async XLA Ops:
  0.6 5.9 %copy-start = (f32[192]{0:T(256)S(1)}, f32[192]{0:T(256)}, u32[]{:S(2)}) copy-start(f32[192]{0:T(256)} %constant.4.clone.dirs) | copy-start | bytes 2308
  2.9 17.1 %collective-permute-start = (f32[136,1152]{1,0:T(8,128)S(1)}, f32[136,1152]{1,0:T(8,128)S(1)}, u32[]{:S(2)}, u32[]{:S(2)}) collective-permute-start(f32[136,1152]{1,0:T(8,128)S(1)} %get-tuple-element.22), channel_id=1, source_target_pairs={{0,8},{16,24},{8,0},{24,16},{1,9},{17,25},{9,1},{25,17},{2,10},{18... | collective-permute-start | bytes 1880072 | tf_op jit(solution)/shard_map/ppermute | solution.py:509
  4.6 18.9 %collective-permute-start.1 = (f32[136,1152]{1,0:T(8,128)S(1)}, f32[136,1152]{1,0:T(8,128)S(1)}, u32[]{:S(2)}, u32[]{:S(2)}) collective-permute-start(f32[136,1152]{1,0:T(8,128)S(1)} %get-tuple-element.23), channel_id=1, source_target_pairs={{8,16},{16,8},{9,17},{17,9},{10,18},{18,10},{11,19},{19,11},{12,20... | collective-permute-start | bytes 1880072 | tf_op jit(solution)/shard_map/ppermute | solution.py:509
  14.9 30.5 %collective-permute-start.2 = (f32[128,1152]{1,0:T(8,128)S(1)}, f32[128,1152]{1,0:T(8,128)S(1)}, u32[]{:S(2)}, u32[]{:S(2)}) collective-permute-start(f32[128,1152]{1,0:T(8,128)S(1)} %get-tuple-element.24), channel_id=1, source_target_pairs={{0,8},{16,24},{8,0},{24,16},{1,9},{17,25},{9,1},{25,17},{2,10},{18... | collective-permute-start | bytes 1769480 | tf_op jit(solution)/shard_map/ppermute | solution.py:509
  15.0 30.4 %collective-permute-start.3 = (f32[128,1152]{1,0:T(8,128)S(1)}, f32[128,1152]{1,0:T(8,128)S(1)}, u32[]{:S(2)}, u32[]{:S(2)}) collective-permute-start(f32[128,1152]{1,0:T(8,128)S(1)} %get-tuple-element.25), channel_id=1, source_target_pairs={{8,16},{16,8},{9,17},{17,9},{10,18},{18,10},{11,19},{19,11},{12,20... | collective-permute-start | bytes 1769480 | tf_op jit(solution)/shard_map/ppermute | solution.py:509
  24.8 1.4 %collective-permute-start.4 = (f32[32,1152]{1,0:T(8,128)S(1)}, f32[32,1152]{1,0:T(8,128)S(1)}, u32[]{:S(2)}, u32[]{:S(2)}) collective-permute-start(f32[32,1152]{1,0:T(8,128)S(1)} %edges.1), channel_id=1, source_target_pairs={{0,1},{1,0},{2,3},{3,2},{4,5},{5,4},{6,7},{7,6},{8,9},{9,8},{10,11... | collective-permute-start | bytes 442376 | tf_op jit(solution)/shard_map/ppermute | solution.py:516
  26.3 7.5 %collective-permute-start.7 = (f32[32,1152]{1,0:T(8,128)S(1)}, f32[32,1152]{1,0:T(8,128)S(1)}, u32[]{:S(2)}, u32[]{:S(2)}) collective-permute-start(f32[32,1152]{1,0:T(8,128)S(1)} %add.15.sum0), channel_id=1, source_target_pairs={{0,6},{2,4},{4,2},{6,0},{1,7},{3,5},{5,3},{7,1},{8,14},{10,12},{12... | collective-permute-start | bytes 442376 | tf_op jit(solution)/shard_map/ppermute | solution.py:520
  28.8 7.5 %collective-permute-start.6 = (f32[32,1152]{1,0:T(8,128)S(1)}, f32[32,1152]{1,0:T(8,128)S(1)}, u32[]{:S(2)}, u32[]{:S(2)}) collective-permute-start(f32[32,1152]{1,0:T(8,128)S(1)} %add.15.sum0), channel_id=1, source_target_pairs={{0,4},{2,6},{4,0},{6,2},{1,5},{3,7},{5,1},{7,3},{8,12},{10,14},{12... | collective-permute-start | bytes 442376 | tf_op jit(solution)/shard_map/ppermute | solution.py:520
  29.3 7.1 %collective-permute-start.5 = (f32[32,1152]{1,0:T(8,128)S(1)}, f32[32,1152]{1,0:T(8,128)S(1)}, u32[]{:S(2)}, u32[]{:S(2)}) collective-permute-start(f32[32,1152]{1,0:T(8,128)S(1)} %add.15.sum0), channel_id=1, source_target_pairs={{0,2},{2,0},{4,6},{6,4},{1,3},{3,1},{5,7},{7,5},{8,10},{10,8},{12,... | collective-permute-start | bytes 442376 | tf_op jit(solution)/shard_map/ppermute | solution.py:520
  47.8 1.3 %collective-permute-start.8 = (f32[6,1152]{1,0:T(8,128)S(1)}, f32[6,1152]{1,0:T(8,128)S(1)}, u32[]{:S(2)}, u32[]{:S(2)}) collective-permute-start(f32[6,1152]{1,0:T(8,128)S(1)} %get-tuple-element.35), channel_id=1, source_target_pairs={{0,1},{1,0},{2,3},{3,2},{4,5},{5,4},{6,7},{7,6},{8,9},{9,8},{10,11... | collective-permute-start | bytes 82952 | tf_op jit(solution)/shard_map/ppermute | solution.py:516
  49.1 4.9 %collective-permute-start.11 = (f32[6,1152]{1,0:T(8,128)S(1)}, f32[6,1152]{1,0:T(8,128)S(1)}, u32[]{:S(2)}, u32[]{:S(2)}) collective-permute-start(f32[6,1152]{1,0:T(8,128)S(1)} %add.16), channel_id=1, source_target_pairs={{0,6},{2,4},{4,2},{6,0},{1,7},{3,5},{5,3},{7,1},{8,14},{10,12},{12... | collective-permute-start | bytes 82952 | tf_op jit(solution)/shard_map/ppermute | solution.py:520
  50.8 4.0 %collective-permute-start.10 = (f32[6,1152]{1,0:T(8,128)S(1)}, f32[6,1152]{1,0:T(8,128)S(1)}, u32[]{:S(2)}, u32[]{:S(2)}) collective-permute-start(f32[6,1152]{1,0:T(8,128)S(1)} %add.16), channel_id=1, source_target_pairs={{0,4},{2,6},{4,0},{6,2},{1,5},{3,7},{5,1},{7,3},{8,12},{10,14},{12... | collective-permute-start | bytes 82952 | tf_op jit(solution)/shard_map/ppermute | solution.py:520
  52.1 4.0 %collective-permute-start.9 = (f32[6,1152]{1,0:T(8,128)S(1)}, f32[6,1152]{1,0:T(8,128)S(1)}, u32[]{:S(2)}, u32[]{:S(2)}) collective-permute-start(f32[6,1152]{1,0:T(8,128)S(1)} %add.16), channel_id=1, source_target_pairs={{0,2},{2,0},{4,6},{6,4},{1,3},{3,1},{5,7},{7,5},{8,10},{10,8},{12,... | collective-permute-start | bytes 82952 | tf_op jit(solution)/shard_map/ppermute | solution.py:520

commit v4 on v3

--- a/solution.py
+++ b/solution.py
@@ -15,8 +15,9 @@
 LANES = 128
 SUB = 8
 FIRST_GROUP = 8
-SECOND_GROUP = 4
-VMEM_LIMIT = 16 * 1024 * 1024
+SECOND_GROUP = 8
+SLOTS = 5
+VMEM_LIMIT = 18 * 1024 * 1024
 
 
 def direction_table(count):
@@ -283,17 +284,15 @@
                     totals[f] = totals[f] + scale * acc[f, x, hs, cs]
             for f in range(4):
                 sums[f * nx + x : f * nx + x + 1, cs] = sub_sum(totals[f])
-    sums[4 * nx :] = jnp.zeros((sums.shape[0] - 4 * nx, plane), jnp.float32)
-
-
-def edges_kernel(dirs, cols, density, material, halo_a, halo_b, sums, out):
+
+
+def edges_kernel(dirs, cols, density, material, halo_a, halo_b, out):
     nx, plane = density.shape
     nb = cols.shape[1]
     half = (halo_a.shape[0] - SUB) // nb
     count = 2 * half
     block = lax.axis_index("dir")
     even = is_even()
-    out[...] = sums[...]
     cuts = tiles(plane)
     gains = []
     for side, halo in enumerate((halo_a, halo_b)):
@@ -322,129 +321,147 @@
         totals = lax.fori_loop(0, half, add, tuple(jnp.zeros((SUB, LANES), jnp.float32) for _ in cuts))
         gains.append([sub_sum(t) for t in totals])
     base = half * nb
-    for side, x in enumerate((nx - 1, 0)):
+    for side in range(2):
         near, far = (0, 1) if side == 0 else (1, 0)
-        row = 2 * nx + x
         for j, cs in enumerate(cuts):
-            out[row : row + 1, cs] = out[row : row + 1, cs] + jnp.where(even, gains[near][j], gains[far][j])
+            out[side : side + 1, cs] = jnp.where(even, gains[near][j], gains[far][j])
             a, b = halo_a[base : base + 1, cs], halo_b[base : base + 1, cs]
-            out[4 * nx + side : 4 * nx + side + 1, cs] = jnp.where(even, a, b) if side == 0 else jnp.where(even, b, a)
+            out[2 + side : 3 + side, cs] = jnp.where(even, a, b) if side == 0 else jnp.where(even, b, a)
+    out[4:] = jnp.zeros((out.shape[0] - 4, plane), jnp.float32)
 
 
 def second_kernel(
-    dirs, cols, density, material, objective, sum0, sum1, sum2, sum3, halo0_a, halo0_b, flow, excess,
+    dirs, cols, density, material, objective, sum0, sum1, sum2, sum3, add0, add1, add2, add3, halo0_a, halo0_b, flow, excess,
     dual, edge_dual, known, gradient,
-    rate, source0, source1, warm, prev, seed, acc,
+    rate, source0, source1, warm, prev, seed, acc, stage, sems,
 ):
-    g = pl.program_id(0)
-    steps = pl.num_programs(0)
     count, nx, nb, plane = flow.shape
-    per = count // steps
+    half = count // 2
+    per = prev.shape[0]
+    slots = stage.shape[0]
     cuts, bands = tiles(plane), halves(nb)
     n = len(cuts)
     scale = float(NDIR * NB)
     edge = halo0_a.shape[0] - SUB
-
-    @pl.when(g == 0)
-    def _():
-        total = (sum0[...] + sum1[...]) + (sum2[...] + sum3[...])
-        for x in range(nx):
-            warm[x] = jnp.broadcast_to(total[nx + x : nx + x + 1], (SUB, plane))
-        known[0:1] = total[2 * nx - 1 : 2 * nx]
-        known[1:2] = total[nx : nx + 1]
-        for side in range(2):
-            from_a = is_even() if side == 0 else jnp.logical_not(is_even())
-            aim = jnp.where(from_a, halo0_a[edge + 3 : edge + 4], halo0_b[edge + 3 : edge + 4])
-            known[2 + side : 3 + side] = total[4 * nx + side : 4 * nx + side + 1] + scale * aim
-        known[4:8] = jnp.zeros((4, plane), jnp.float32)
-        for x in range(nx):
-            for cs in cuts:
-                drive = total[x : x + 1, cs] + scale * objective[x : x + 1, cs]
-                again = (
-                    total[2 * nx + x : 2 * nx + x + 1, cs]
-                    + drive * total[3 * nx + x : 3 * nx + x + 1, cs]
-                    + scale * objective[x : x + 1, cs]
-                )
+    even = is_even()
+
+    total = (sum0[...] + sum1[...]) + (sum2[...] + sum3[...])
+    more = (add0[...] + add1[...]) + (add2[...] + add3[...])
+    for x in range(nx):
+        warm[x] = jnp.broadcast_to(total[nx + x : nx + x + 1], (SUB, plane))
+    known[0:1] = total[2 * nx - 1 : 2 * nx]
+    known[1:2] = total[nx : nx + 1]
+    for side in range(2):
+        from_a = even if side == 0 else jnp.logical_not(even)
+        aim = jnp.where(from_a, halo0_a[edge + 3 : edge + 4], halo0_b[edge + 3 : edge + 4])
+        known[2 + side : 3 + side] = more[2 + side : 3 + side] + scale * aim
+    known[4:8] = jnp.zeros((4, plane), jnp.float32)
+    for x in range(nx):
+        for cs in cuts:
+            drive = total[x : x + 1, cs] + scale * objective[x : x + 1, cs]
+            again = (
+                total[2 * nx + x : 2 * nx + x + 1, cs]
+                + drive * total[3 * nx + x : 3 * nx + x + 1, cs]
+                + scale * objective[x : x + 1, cs]
+            )
+            if x == nx - 1:
+                again = again + more[0:1, cs]
+            if x == 0:
+                again = again + more[1:2, cs]
+            for hs in bands:
+                w = cols[1, hs]
+                rate[x, hs, cs] = rate_tile(cols, density[x : x + 1, cs], material[x : x + 1, cs], hs)
+                source0[x, hs, cs] = w * drive
+                source1[x, hs, cs] = w * again
+    acc[...] = jnp.zeros_like(acc)
+    block = lax.axis_index("dir")
+    lane = lane_ids()
+
+    def sent(first, x, slot):
+        return pltpu.make_async_copy(stage.at[slot], dual.at[pl.ds(first, per), x], sems.at[slot])
+
+    def group(k, _):
+        first = k * per
+        ahead = first < half
+
+        def enter(halo0):
+            skip = jnp.where(ahead, 0, half)
+            for dd in range(per):
+                ax = jnp.abs(cosines(dirs, block * count + first + dd)[0])
+                for h, hs in enumerate(bands):
+                    cx = cols[0, hs] * ax
+                    rows = pl.ds(pl.multiple_of((first - skip + dd) * nb + h * SUB, SUB), SUB)
+                    for cs in cuts:
+                        seed[dd, hs, cs] = cx * halo0[rows, cs]
+
+        pl.when(ahead == even)(lambda: enter(halo0_a))
+        pl.when(ahead != even)(lambda: enter(halo0_b))
+
+        def run(rising):
+            def layer(i, at_edge):
+                x = jnp.where(ahead, nx - 1 - i, i)
+                turn = k * (nx - 1) + i - 1
+                slot = turn % slots
+                if not at_edge:
+                    pl.when(turn >= slots)(lambda: sent(first, x, slot).wait())
                 for hs in bands:
-                    w = cols[1, hs]
-                    rate[x, hs, cs] = rate_tile(cols, density[x : x + 1, cs], material[x : x + 1, cs], hs)
-                    source0[x, hs, cs] = w * drive
-                    source1[x, hs, cs] = w * again
-        acc[...] = jnp.zeros_like(acc)
-
-    block = lax.axis_index("dir")
-    first = block * count + g * per
-    ahead = g < steps // 2
-    lane = lane_ids()
-
-    def enter(halo0):
-        skip = jnp.where(ahead, 0, steps // 2)
-        for dd in range(per):
-            ax = jnp.abs(cosines(dirs, first + dd)[0])
-            for h, hs in enumerate(bands):
-                cx = cols[0, hs] * ax
-                rows = pl.ds(pl.multiple_of(((g - skip) * per + dd) * nb + h * SUB, SUB), SUB)
-                for cs in cuts:
-                    seed[dd, hs, cs] = cx * halo0[rows, cs]
-
-    pl.when(ahead == is_even())(lambda: enter(halo0_a))
-    pl.when(ahead != is_even())(lambda: enter(halo0_b))
-
-    def run(rising):
-        def layer(i, at_edge):
-            x = jnp.where(ahead, nx - 1 - i, i)
+                    pace = cols[0, hs]
+                    rates = lazily(lambda j: rate[x, hs, cuts[j]])
+                    sources = lazily(lambda j: source0[x, hs, cuts[j]])
+                    ways = []
+                    for dd in range(per):
+                        ax, ay, az = [jnp.abs(a) for a in cosines(dirs, block * count + first + dd)]
+                        speeds = pace * (ax + ay + az)
+                        inv = lazily(lambda j, speeds=speeds: inverse(speeds + rates(j)))
+
+                        def fresh(j, dd=dd, inv=inv):
+                            s = sources(j)
+                            if at_edge:
+                                s = s + seed[dd, hs, cuts[j]]
+                            return flow[first + dd, x, hs, cuts[j]] + s * inv(j)
+
+                        v = lazily(fresh)
+                        shifts = (shift_y(v, n, rising, lane), shift_z(v, n, dd % 2 == 0, lane))
+                        ways.append((v, inv, *shifts, (pace * ax, pace * ay, pace * az)))
+                    for j, cs in enumerate(cuts):
+                        kept = []
+                        again, level = source1[x, hs, cs], warm[x, :, cs]
+                        for dd, (v, inv, along_y, along_z, (cx, cy, cz)) in enumerate(ways):
+                            beside = None if at_edge else cx * prev[dd, hs, cs]
+                            new = inv(j) * add_terms([beside, times(cy, along_y(j)), times(cz, along_z(j)), again])
+                            prev[dd, hs, cs] = v(j)
+                            if at_edge:
+                                edge_dual[first + dd, hs, cs] = new
+                            else:
+                                stage[slot, dd, hs, cs] = new
+                            kept.append((v(j) + new) * (excess[first + dd, x, hs, cs] - level))
+                        acc[x, hs, cs] += add_terms(kept)
+                if not at_edge:
+                    sent(first, x, slot).start()
+
+            layer(0, True)
+
+            def later(i, _):
+                layer(i, False)
+                return 0
+
+            lax.fori_loop(1, nx, later, 0)
+
+        rises = cosines(dirs, block * count + first)[1] > 0
+        pl.when(rises)(lambda: run(True))
+        pl.when(jnp.logical_not(rises))(lambda: run(False))
+        return 0
+
+    groups = count // per
+    lax.fori_loop(0, groups, group, 0)
+    for x in range(nx):
+        for cs in cuts:
+            total = 0.0
             for hs in bands:
-                pace = cols[0, hs]
-                rates = lazily(lambda j: rate[x, hs, cuts[j]])
-                sources = lazily(lambda j: source0[x, hs, cuts[j]])
-                ways = []
-                for dd in range(per):
-                    ax, ay, az = [jnp.abs(a) for a in cosines(dirs, first + dd)]
-                    speeds = pace * (ax + ay + az)
-                    inv = lazily(lambda j, speeds=speeds: inverse(speeds + rates(j)))
-
-                    def fresh(j, dd=dd, inv=inv):
-                        s = sources(j)
-                        if at_edge:
-                            s = s + seed[dd, hs, cuts[j]]
-                        return flow[g * per + dd, x, hs, cuts[j]] + s * inv(j)
-
-                    v = lazily(fresh)
-                    shifts = (shift_y(v, n, rising, lane), shift_z(v, n, dd % 2 == 0, lane))
-                    ways.append((v, inv, *shifts, (pace * ax, pace * ay, pace * az)))
-                for j, cs in enumerate(cuts):
-                    kept = []
-                    again, level = source1[x, hs, cs], warm[x, :, cs]
-                    for dd, (v, inv, along_y, along_z, (cx, cy, cz)) in enumerate(ways):
-                        beside = None if at_edge else cx * prev[dd, hs, cs]
-                        new = inv(j) * add_terms([beside, times(cy, along_y(j)), times(cz, along_z(j)), again])
-                        prev[dd, hs, cs] = v(j)
-                        dual[dd, x, hs, cs] = new
-                        if at_edge:
-                            edge_dual[g * per + dd, hs, cs] = new
-                        kept.append((v(j) + new) * (excess[g * per + dd, x, hs, cs] - level))
-                    acc[x, hs, cs] += add_terms(kept)
-
-        layer(0, True)
-
-        def later(i, _):
-            layer(i, False)
-            return 0
-
-        lax.fori_loop(1, nx, later, 0)
-
-    rises = cosines(dirs, first)[1] > 0
-    pl.when(rises)(lambda: run(True))
-    pl.when(jnp.logical_not(rises))(lambda: run(False))
-
-    @pl.when(g == steps - 1)
-    def _():
-        for x in range(nx):
-            for cs in cuts:
-                total = 0.0
-                for hs in bands:
-                    total = total + base_tile(cols, material[x : x + 1, cs], hs) * acc[x, hs, cs]
-                gradient[x : x + 1, cs] = sub_sum(total) * 0.8
+                total = total + base_tile(cols, material[x : x + 1, cs], hs) * acc[x, hs, cs]
+            gradient[x : x + 1, cs] = sub_sum(total) * 0.8
+    for turn in range(groups * (nx - 1))[-slots:]:
+        sent(0, 0, turn % slots).wait()
 
 
 def last_kernel(
@@ -509,19 +526,21 @@
     return lax.ppermute(value, "space", pairs + [(b, a) for a, b in pairs])
 
 
-def shares(partial):
-    size = lax.axis_size("band")
-    total = partial
-    for k in range(1, size):
-        total = total + lax.ppermute(partial, "band", [(s, (s + k) % size) for s in range(size)])
-    count = lax.axis_size("dir")
+def others(value, axis):
+    count = lax.axis_size(axis)
     pairs = count & (count - 1) == 0
     hops = [[(s, s ^ k if pairs else (s + k) % count) for s in range(count)] for k in range(1, count)]
-    return [total] + [lax.ppermute(total, "dir", hop) for hop in hops]
-
-
-def whole(array):
-    return pl.BlockSpec(array.shape, lambda *g: (0,) * array.ndim)
+    return [lax.ppermute(value, axis, hop) for hop in hops]
+
+
+def shares(partial, first, then):
+    total = sum(others(partial, first), partial)
+    return [total] + others(total, then)
+
+
+def packed(parts, count):
+    parts = parts + [jnp.zeros_like(parts[0])] * (count - len(parts))
+    return parts[: count - 1] + [sum(parts[count:], parts[count - 1])]
 
 
 def on_device(
@@ -570,11 +589,10 @@
     )(*stay(*small, *cells, start))
     halo0_a, halo0_b = swapped(face_a, 0), swapped(face_b, 1)
 
-    sum_rows = -(-(4 * nx + 2) // SUB) * SUB
     flow, excess, face_a, face_b, sums = pl.pallas_call(
         first_kernel,
         out_shape=(
-            like(*start.shape), like(*start.shape), like(half * nb, plane), like(half * nb, plane), like(sum_rows, plane)
+            like(*start.shape), like(*start.shape), like(half * nb, plane), like(half * nb, plane), like(4 * nx, plane)
         ),
         in_specs=[smem] + [vmem] * 3 + [hbm] * 2,
         out_specs=[vmem] * 5,
@@ -588,36 +606,35 @@
     )(dirs, cols, density, material, *stay(start, excess))
     halo1_a, halo1_b = swapped(face_a, 0), swapped(face_b, 1)
 
-    sums = pl.pallas_call(
+    parts = packed(shares(sums, "band", "dir"), 4)
+
+    extra = pl.pallas_call(
         edges_kernel,
-        out_shape=like(sum_rows, plane),
-        in_specs=[smem] + [vmem] * 6,
+        out_shape=like(SUB, plane),
+        in_specs=[smem] + [vmem] * 5,
         out_specs=vmem,
         compiler_params=params,
         cost_estimate=cost(1, 1),
         name="edges",
-    )(dirs, cols, density, material, halo0_a, halo0_b, sums)
-    parts = shares(sums)
-    parts = parts + [jnp.zeros_like(sums)] * (4 - len(parts))
-    parts = parts[:3] + [sum(parts[4:], parts[3])]
-
-    second_steps = count // math.gcd(SECOND_GROUP, half)
-    per = count // second_steps
+    )(dirs, cols, density, material, halo0_a, halo0_b)
+    extras = packed(shares(extra, "band", "dir"), 4)
+
+    per = math.gcd(SECOND_GROUP, half)
     layer = pltpu.VMEM((nx, nb, plane), f32)
+    rows = pltpu.VMEM((per, nb, plane), f32)
     dual, edge_dual, known, gradient = pl.pallas_call(
         second_kernel,
-        grid=(second_steps,),
-        out_shape=(like(*start.shape), like(count, nb, plane), like(SUB, plane), like(nx, plane)),
-        in_specs=[smem] + [vmem] * 12,
-        out_specs=[pl.BlockSpec((per, nx, nb, plane), lambda g: (g, 0, 0, 0))] + [vmem] * 3,
+        out_shape=(pltpu.HBM(start.shape, f32), like(count, nb, plane), like(SUB, plane), like(nx, plane)),
+        in_specs=[smem] + [vmem] * 16,
+        out_specs=[hbm] + [vmem] * 3,
         scratch_shapes=[
-            layer, layer, layer, pltpu.VMEM((nx, SUB, plane), f32),
-            pltpu.VMEM((per, nb, plane), f32), pltpu.VMEM((per, nb, plane), f32), layer,
+            layer, layer, layer, pltpu.VMEM((nx, SUB, plane), f32), rows, rows, layer,
+            pltpu.VMEM((SLOTS, per, nb, plane), f32), pltpu.SemaphoreType.DMA((SLOTS,)),
         ],
         compiler_params=params,
         cost_estimate=cost(30, 12),
         name="second",
-    )(dirs, cols, density, material, objective, *parts, halo0_a, halo0_b, flow, excess)
+    )(dirs, cols, density, material, objective, *parts, *extras, halo0_a, halo0_b, flow, excess)
 
     dual, gradient = pl.pallas_call(
         last_kernel,
@@ -630,7 +647,7 @@
         cost_estimate=cost(1, 1),
         name="last",
     )(dirs, cols, density, material, halo0_a, halo0_b, halo1_a, halo1_b, excess, edge_dual, known, gradient, dual)
-    gradient = sum(shares(gradient)) * (-0.125 / ITERS)
+    gradient = sum(shares(gradient, "band", "dir")) * (-0.125 / ITERS)
     return (dual.transpose(0, 2, 1, 3), gradient)
 
 

time: 56.9 us -> 58 us (1.019)
  starting transfers between devices: 14.7 us -> 19.4 us
  waiting for transfers between devices: 17.1 us -> 14.6 us
  Pallas kernels: 23.4 us -> 22.4 us
    ppermute x8 -> x12, starting transfers between devices: 7.18 us -> 11.8 us  [others(): return [lax.ppermute(value, axis, hop) for hop in hops]]
    ppermute x8 -> x12, waiting for transfers between devices: 12.5 us -> 10 us  [others(): return [lax.ppermute(value, axis, hop) for hop in hops]]
    pallas_call x2, Pallas kernels: 10.3 us -> 9.28 us  [the longest x1 7.97 us: on_device(): pl.pallas_call(second_kernel, out_shape=(pltpu.HBM(start.shape, f32), lik...]
  transfers between devices with their start and end apart: 12 -> 16, of which waited for: 10 -> 10; matrix products, arithmetic and copies ran while one was open for 0% -> 0% of each run, Pallas kernels for 33% -> 31%
where the time goes in v4:
time: 58 us; the launch traced here: 57.8 us
  Pallas kernels  22.4 us (39%)
  starting transfers between devices  19.4 us (33%)
  waiting for transfers between devices  14.6 us (25%)
  between operations  0.78 us (1%)
  other arithmetic  0.66 us (1%)
    ppermute x12, starting transfers between devices, others(): return [lax.ppermute(value, axis, hop) for hop in hops]  11.8 us
    ppermute x12, waiting for transfers between devices, others(): return [lax.ppermute(value, axis, hop) for hop in hops]  10 us
    pallas_call x1, Pallas kernels, on_device(): pl.pallas_call(first_kernel, out_shape=(like(*start.shape), like(*start.s...  8.39 us
    pallas_call x1, Pallas kernels, on_device(): pl.pallas_call(second_kernel, out_shape=(pltpu.HBM(start.shape, f32), lik...  7.97 us
    ppermute x4, starting transfers between devices, swapped(): return lax.ppermute(value, 'space', pairs + [(b, a) for a, b in pairs])  7.55 us
    ppermute x4, waiting for transfers between devices, swapped(): return lax.ppermute(value, 'space', pairs + [(b, a) for a, b in pairs])  4.51 us
    pallas_call x1, Pallas kernels, on_device(): pl.pallas_call(last_kernel, out_shape=(like(*start.shape), like(nx, plane...  2.49 us
    pallas_call x1, Pallas kernels, on_device(): pl.pallas_call(faces_kernel, out_shape=(like(half * nb + SUB, plane), lik...  2.28 us
  transfers between devices with their start and end apart: 16, of which 10 were waited for; matrix products, arithmetic and copies ran while one was open for 0% of the time, Pallas kernels for 31%

profile of v4, /device:TPU:16, one launch (start us, length us, event | category | flops | bytes accessed | tf_op | source)
XLA Modules:
  0.0 57.8 jit_solution(4063285462077422187)
XLA Ops:
  0.6 2.3 %faces.1 = (f32[136,1152]{1,0:T(8,128)S(1)}, f32[136,1152]{1,0:T(8,128)S(1)}, f32[6,16,128]{2,1,0:T(8,128)S(1)}, f32[6,1152]{1,0:T(8,128)S(1)}, s32[6,1152]{1,0:T(8,128)S(1)}, /*index=5*/f32[6,1152]{1,0:T(8,128)S(1)}) custom-call(f32[1,32]{1,0:T(1,128)} %bitcast.9, f32[1,16]{1,0:T(1,128)} %bitcast.10, f32[4,16]{1,0:T(4,128)} %table_in.1, ...), custom_call_target="tpu_custom_call" | custom-call | flops 530841 | bytes 3538944 | tf_op jit(solution)/shard_map/faces/pallas_call | solution.py:576
  2.9 1.6 %collective-permute-start = (f32[136,1152]{1,0:T(8,128)S(1)}, f32[136,1152]{1,0:T(8,128)S(1)}, u32[]{:S(2)}, u32[]{:S(2)}) collective-permute-start(f32[136,1152]{1,0:T(8,128)S(1)} %get-tuple-element.22), channel_id=1, source_target_pairs={{0,8},{16,24},{8,0},{24,16},{1,9},{17,25},{9,1},{25,17},{2,10},{18... | collective-permute-start | bytes 1880072 | tf_op jit(solution)/shard_map/ppermute | solution.py:526
  4.6 1.9 %collective-permute-start.1 = (f32[136,1152]{1,0:T(8,128)S(1)}, f32[136,1152]{1,0:T(8,128)S(1)}, u32[]{:S(2)}, u32[]{:S(2)}) collective-permute-start(f32[136,1152]{1,0:T(8,128)S(1)} %get-tuple-element.23), channel_id=1, source_target_pairs={{8,16},{16,8},{9,17},{17,9},{10,18},{18,10},{11,19},{19,11},{12,20... | collective-permute-start | bytes 1880072 | tf_op jit(solution)/shard_map/ppermute | solution.py:526
  6.5 8.4 %first.1 = (f32[16,6,16,1152]{3,2,1,0:T(8,128)S(1)}, f32[16,6,16,1152]{3,2,1,0:T(8,128)S(1)}, f32[128,1152]{1,0:T(8,128)S(1)}, f32[128,1152]{1,0:T(8,128)S(1)}, f32[24,1152]{1,0:T(8,128)S(1)}) custom-call(f32[192]{0:T(256)S(1)} %copy-done, f32[6,16,128]{2,1,0:T(8,128)S(1)} %get-tuple-element.19.cols, f32[6,1152]{1,0:T(8,128)S(1)} %get-tuple-element.20.density, ...), custom_call_target="tpu_custom_call" | custom-call | flops 35389440 | bytes 21233664 | tf_op jit(solution)/shard_map/first/pallas_call | solution.py:592
  15.0 3.9 %collective-permute-start.3 = (f32[128,1152]{1,0:T(8,128)S(1)}, f32[128,1152]{1,0:T(8,128)S(1)}, u32[]{:S(2)}, u32[]{:S(2)}) collective-permute-start(f32[128,1152]{1,0:T(8,128)S(1)} %get-tuple-element.25), channel_id=1, source_target_pairs={{8,16},{16,8},{9,17},{17,9},{10,18},{18,10},{11,19},{19,11},{12,20... | collective-permute-start | bytes 1769480 | tf_op jit(solution)/shard_map/ppermute | solution.py:526
  19.0 1.0 %collective-permute-done.halo_a.halo0_a = f32[136,1152]{1,0:T(8,128)S(1)} collective-permute-done((f32[136,1152]{1,0:T(8,128)S(1)}, f32[136,1152]{1,0:T(8,128)S(1)}, u32[]{:S(2)}, u32[]{:S(2)}) %collective-permute-start) | collective-permute-done | bytes 626720 | tf_op jit(solution)/shard_map/ppermute | solution.py:526
  20.0 3.5 %collective-permute-done.1.halo_b.halo0_b = f32[136,1152]{1,0:T(8,128)S(1)} collective-permute-done((f32[136,1152]{1,0:T(8,128)S(1)}, f32[136,1152]{1,0:T(8,128)S(1)}, u32[]{:S(2)}, u32[]{:S(2)}) %collective-permute-start.1) | collective-permute-done | bytes 626720 | tf_op jit(solution)/shard_map/ppermute | solution.py:526
  23.5 1.3 %edges.1 = f32[8,1152]{1,0:T(8,128)S(1)} custom-call(f32[192]{0:T(256)S(1)} %copy-done, f32[6,16,128]{2,1,0:T(8,128)S(1)} %get-tuple-element.19.cols, f32[6,1152]{1,0:T(8,128)S(1)} %get-tuple-element.20.density, s32[6,1152]{1,0:T(8,128)S(1)} %get-tuple-element.21.material, f32[136,1152]{1,0:T(8,128)S(1)} %collective-permute-done.halo_a.halo0_a, ...), custom_call_target="tpu_custom_call" | custom-call | flops 1769472 | bytes 1769472 | tf_op jit(solution)/shard_map/edges/pallas_call | solution.py:611
  24.9 2.5 %collective-permute-start.7 = (f32[24,1152]{1,0:T(8,128)S(1)}, f32[24,1152]{1,0:T(8,128)S(1)}, u32[]{:S(2)}, u32[]{:S(2)}) collective-permute-start(f32[24,1152]{1,0:T(8,128)S(1)} %add.18.sum0), channel_id=1, source_target_pairs={{0,6},{2,4},{4,2},{6,0},{1,7},{3,5},{5,3},{7,1},{8,14},{10,12},{12... | collective-permute-start | bytes 331784 | tf_op jit(solution)/shard_map/ppermute | solution.py:533
  28.5 3.0 %collective-permute-done.7.sum3 = f32[24,1152]{1,0:T(8,128)S(1)} collective-permute-done((f32[24,1152]{1,0:T(8,128)S(1)}, f32[24,1152]{1,0:T(8,128)S(1)}, u32[]{:S(2)}, u32[]{:S(2)}) %collective-permute-start.7) | collective-permute-done | bytes 110624 | tf_op jit(solution)/shard_map/ppermute | solution.py:533
  31.4 2.8 %collective-permute-start.11 = (f32[8,1152]{1,0:T(8,128)S(1)}, f32[8,1152]{1,0:T(8,128)S(1)}, u32[]{:S(2)}, u32[]{:S(2)}) collective-permute-start(f32[8,1152]{1,0:T(8,128)S(1)} %add.19.add0), channel_id=1, source_target_pairs={{0,6},{2,4},{4,2},{6,0},{1,7},{3,5},{5,3},{7,1},{8,14},{10,12},{12... | collective-permute-start | bytes 110600 | tf_op jit(solution)/shard_map/ppermute | solution.py:533
  34.2 1.0 %collective-permute-start.10 = (f32[8,1152]{1,0:T(8,128)S(1)}, f32[8,1152]{1,0:T(8,128)S(1)}, u32[]{:S(2)}, u32[]{:S(2)}) collective-permute-start(f32[8,1152]{1,0:T(8,128)S(1)} %add.19.add0), channel_id=1, source_target_pairs={{0,4},{2,6},{4,0},{6,2},{1,5},{3,7},{5,1},{7,3},{8,12},{10,14},{12... | collective-permute-start | bytes 110600 | tf_op jit(solution)/shard_map/ppermute | solution.py:533
  35.2 0.8 %collective-permute-start.9 = (f32[8,1152]{1,0:T(8,128)S(1)}, f32[8,1152]{1,0:T(8,128)S(1)}, u32[]{:S(2)}, u32[]{:S(2)}) collective-permute-start(f32[8,1152]{1,0:T(8,128)S(1)} %add.19.add0), channel_id=1, source_target_pairs={{0,2},{2,0},{4,6},{6,4},{1,3},{3,1},{5,7},{7,5},{8,10},{10,8},{12,... | collective-permute-start | bytes 110600 | tf_op jit(solution)/shard_map/ppermute | solution.py:533
  36.3 1.9 %collective-permute-done.10.add2 = f32[8,1152]{1,0:T(8,128)S(1)} collective-permute-done((f32[8,1152]{1,0:T(8,128)S(1)}, f32[8,1152]{1,0:T(8,128)S(1)}, u32[]{:S(2)}, u32[]{:S(2)}) %collective-permute-start.10) | collective-permute-done | bytes 36896 | tf_op jit(solution)/shard_map/ppermute | solution.py:533
  38.2 1.0 %collective-permute-done.9.add1 = f32[8,1152]{1,0:T(8,128)S(1)} collective-permute-done((f32[8,1152]{1,0:T(8,128)S(1)}, f32[8,1152]{1,0:T(8,128)S(1)}, u32[]{:S(2)}, u32[]{:S(2)}) %collective-permute-start.9) | collective-permute-done | bytes 36896 | tf_op jit(solution)/shard_map/ppermute | solution.py:533
  39.2 8.0 %second.1 = (f32[16,6,16,1152]{3,2,1,0:T(8,128)}, f32[16,16,1152]{2,1,0:T(8,128)S(1)}, f32[8,1152]{1,0:T(8,128)S(1)}, f32[6,1152]{1,0:T(8,128)S(1)}) custom-call(f32[192]{0:T(256)S(1)} %copy-done, f32[6,16,128]{2,1,0:T(8,128)S(1)} %get-tuple-element.19.cols, f32[6,1152]{1,0:T(8,128)S(1)} %get-tuple-element.20.density, ...), custom_call_target="tpu_custom_call" | custom-call | flops 53084160 | bytes 21233664 | tf_op jit(solution)/shard_map/second/pallas_call | solution.py:625
  47.2 2.5 %last.1 = (f32[16,6,16,1152]{3,2,1,0:T(8,128)}, f32[6,1152]{1,0:T(8,128)S(1)}) custom-call(f32[192]{0:T(256)S(1)} %copy-done, f32[6,16,128]{2,1,0:T(8,128)S(1)} %get-tuple-element.19.cols, f32[6,1152]{1,0:T(8,128)S(1)} %get-tuple-element.20.density, s32[6,1152]{1,0:T(8,128)S(1)} %get-tuple-element.21.material, ...), custom_call_target="tpu_custom_call", output_to_operand_aliasing={{0}: (12, {})} | custom-call | flops 1769472 | bytes 1769472 | tf_op jit(solution)/shard_map/last/pallas_call | solution.py:639
  49.8 1.2 %collective-permute-done.12 = f32[6,1152]{1,0:T(8,128)S(1)} collective-permute-done((f32[6,1152]{1,0:T(8,128)S(1)}, f32[6,1152]{1,0:T(8,128)S(1)}, u32[]{:S(2)}, u32[]{:S(2)}) %collective-permute-start.12) | collective-permute-done | bytes 27680 | tf_op jit(solution)/shard_map/ppermute | solution.py:533
  51.0 1.4 %collective-permute-start.15 = (f32[6,1152]{1,0:T(8,128)S(1)}, f32[6,1152]{1,0:T(8,128)S(1)}, u32[]{:S(2)}, u32[]{:S(2)}) collective-permute-start(f32[6,1152]{1,0:T(8,128)S(1)} %add.20), channel_id=1, source_target_pairs={{0,6},{2,4},{4,2},{6,0},{1,7},{3,5},{5,3},{7,1},{8,14},{10,12},{12... | collective-permute-start | bytes 82952 | tf_op jit(solution)/shard_map/ppermute | solution.py:533
  52.3 0.9 %collective-permute-start.14 = (f32[6,1152]{1,0:T(8,128)S(1)}, f32[6,1152]{1,0:T(8,128)S(1)}, u32[]{:S(2)}, u32[]{:S(2)}) collective-permute-start(f32[6,1152]{1,0:T(8,128)S(1)} %add.20), channel_id=1, source_target_pairs={{0,4},{2,6},{4,0},{6,2},{1,5},{3,7},{5,1},{7,3},{8,12},{10,14},{12... | collective-permute-start | bytes 82952 | tf_op jit(solution)/shard_map/ppermute | solution.py:533
  53.2 1.2 %collective-permute-start.13 = (f32[6,1152]{1,0:T(8,128)S(1)}, f32[6,1152]{1,0:T(8,128)S(1)}, u32[]{:S(2)}, u32[]{:S(2)}) collective-permute-start(f32[6,1152]{1,0:T(8,128)S(1)} %add.20), channel_id=1, source_target_pairs={{0,2},{2,0},{4,6},{6,4},{1,3},{3,1},{5,7},{7,5},{8,10},{10,8},{12,... | collective-permute-start | bytes 82952 | tf_op jit(solution)/shard_map/ppermute | solution.py:533
  54.5 1.4 %collective-permute-done.15 = f32[6,1152]{1,0:T(8,128)S(1)} collective-permute-done((f32[6,1152]{1,0:T(8,128)S(1)}, f32[6,1152]{1,0:T(8,128)S(1)}, u32[]{:S(2)}, u32[]{:S(2)}) %collective-permute-start.15) | collective-permute-done | bytes 27680 | tf_op jit(solution)/shard_map/ppermute | solution.py:533
  56.3 0.9 %collective-permute-done.13 = f32[6,1152]{1,0:T(8,128)S(1)} collective-permute-done((f32[6,1152]{1,0:T(8,128)S(1)}, f32[6,1152]{1,0:T(8,128)S(1)}, u32[]{:S(2)}, u32[]{:S(2)}) %collective-permute-start.13) | collective-permute-done | bytes 27680 | tf_op jit(solution)/shard_map/ppermute | solution.py:533
  57.2 0.6 %add_multiply_fusion = f32[6,1152]{1,0:T(8,128)} fusion(f32[6,1152]{1,0:T(8,128)S(1)} %collective-permute-done.15, f32[6,1152]{1,0:T(8,128)S(1)} %collective-permute-done.14, f32[6,1152]{1,0:T(8,128)S(1)} %add.20, f32[6,1152]{1,0:T(8,128)S(1)} %collective-permute-done.13), kind=kLoop, calls=%fused_computation | loop fusion | flops 27648 | bytes 138240 | tf_op jit(solution)/shard_map/mul | solution.py:650
  (19 shorter events, 2.1 us)
Async XLA Ops:
  0.6 5.9 %copy-start = (f32[192]{0:T(256)S(1)}, f32[192]{0:T(256)}, u32[]{:S(2)}) copy-start(f32[192]{0:T(256)} %constant.4.clone.dirs) | copy-start | bytes 2308
  2.9 17.1 %collective-permute-start = (f32[136,1152]{1,0:T(8,128)S(1)}, f32[136,1152]{1,0:T(8,128)S(1)}, u32[]{:S(2)}, u32[]{:S(2)}) collective-permute-start(f32[136,1152]{1,0:T(8,128)S(1)} %get-tuple-element.22), channel_id=1, source_target_pairs={{0,8},{16,24},{8,0},{24,16},{1,9},{17,25},{9,1},{25,17},{2,10},{18... | collective-permute-start | bytes 1880072 | tf_op jit(solution)/shard_map/ppermute | solution.py:526
  4.6 18.9 %collective-permute-start.1 = (f32[136,1152]{1,0:T(8,128)S(1)}, f32[136,1152]{1,0:T(8,128)S(1)}, u32[]{:S(2)}, u32[]{:S(2)}) collective-permute-start(f32[136,1152]{1,0:T(8,128)S(1)} %get-tuple-element.23), channel_id=1, source_target_pairs={{8,16},{16,8},{9,17},{17,9},{10,18},{18,10},{11,19},{19,11},{12,20... | collective-permute-start | bytes 1880072 | tf_op jit(solution)/shard_map/ppermute | solution.py:526
  14.9 32.3 %collective-permute-start.2 = (f32[128,1152]{1,0:T(8,128)S(1)}, f32[128,1152]{1,0:T(8,128)S(1)}, u32[]{:S(2)}, u32[]{:S(2)}) collective-permute-start(f32[128,1152]{1,0:T(8,128)S(1)} %get-tuple-element.24), channel_id=1, source_target_pairs={{0,8},{16,24},{8,0},{24,16},{1,9},{17,25},{9,1},{25,17},{2,10},{18... | collective-permute-start | bytes 1769480 | tf_op jit(solution)/shard_map/ppermute | solution.py:526
  15.0 32.2 %collective-permute-start.3 = (f32[128,1152]{1,0:T(8,128)S(1)}, f32[128,1152]{1,0:T(8,128)S(1)}, u32[]{:S(2)}, u32[]{:S(2)}) collective-permute-start(f32[128,1152]{1,0:T(8,128)S(1)} %get-tuple-element.25), channel_id=1, source_target_pairs={{8,16},{16,8},{9,17},{17,9},{10,18},{18,10},{11,19},{19,11},{12,20... | collective-permute-start | bytes 1769480 | tf_op jit(solution)/shard_map/ppermute | solution.py:526
  18.9 6.0 %collective-permute-start.4 = (f32[24,1152]{1,0:T(8,128)S(1)}, f32[24,1152]{1,0:T(8,128)S(1)}, u32[]{:S(2)}, u32[]{:S(2)}) collective-permute-start(f32[24,1152]{1,0:T(8,128)S(1)} %get-tuple-element.28), channel_id=1, source_target_pairs={{0,1},{1,0},{2,3},{3,2},{4,5},{5,4},{6,7},{7,6},{8,9},{9,8},{10,11... | collective-permute-start | bytes 331784 | tf_op jit(solution)/shard_map/ppermute | solution.py:533
  24.8 3.1 %collective-permute-start.8 = (f32[8,1152]{1,0:T(8,128)S(1)}, f32[8,1152]{1,0:T(8,128)S(1)}, u32[]{:S(2)}, u32[]{:S(2)}) collective-permute-start(f32[8,1152]{1,0:T(8,128)S(1)} %edges.1), channel_id=1, source_target_pairs={{0,1},{1,0},{2,3},{3,2},{4,5},{5,4},{6,7},{7,6},{8,9},{9,8},{10,11... | collective-permute-start | bytes 110600 | tf_op jit(solution)/shard_map/ppermute | solution.py:533
  24.9 6.5 %collective-permute-start.7 = (f32[24,1152]{1,0:T(8,128)S(1)}, f32[24,1152]{1,0:T(8,128)S(1)}, u32[]{:S(2)}, u32[]{:S(2)}) collective-permute-start(f32[24,1152]{1,0:T(8,128)S(1)} %add.18.sum0), channel_id=1, source_target_pairs={{0,6},{2,4},{4,2},{6,0},{1,7},{3,5},{5,3},{7,1},{8,14},{10,12},{12... | collective-permute-start | bytes 331784 | tf_op jit(solution)/shard_map/ppermute | solution.py:533
  27.4 6.8 %collective-permute-start.6 = (f32[24,1152]{1,0:T(8,128)S(1)}, f32[24,1152]{1,0:T(8,128)S(1)}, u32[]{:S(2)}, u32[]{:S(2)}) collective-permute-start(f32[24,1152]{1,0:T(8,128)S(1)} %add.18.sum0), channel_id=1, source_target_pairs={{0,4},{2,6},{4,0},{6,2},{1,5},{3,7},{5,1},{7,3},{8,12},{10,14},{12... | collective-permute-start | bytes 331784 | tf_op jit(solution)/shard_map/ppermute | solution.py:533
  27.9 7.3 %collective-permute-start.5 = (f32[24,1152]{1,0:T(8,128)S(1)}, f32[24,1152]{1,0:T(8,128)S(1)}, u32[]{:S(2)}, u32[]{:S(2)}) collective-permute-start(f32[24,1152]{1,0:T(8,128)S(1)} %add.18.sum0), channel_id=1, source_target_pairs={{0,2},{2,0},{4,6},{6,4},{1,3},{3,1},{5,7},{7,5},{8,10},{10,8},{12,... | collective-permute-start | bytes 331784 | tf_op jit(solution)/shard_map/ppermute | solution.py:533
  31.4 4.9 %collective-permute-start.11 = (f32[8,1152]{1,0:T(8,128)S(1)}, f32[8,1152]{1,0:T(8,128)S(1)}, u32[]{:S(2)}, u32[]{:S(2)}) collective-permute-start(f32[8,1152]{1,0:T(8,128)S(1)} %add.19.add0), channel_id=1, source_target_pairs={{0,6},{2,4},{4,2},{6,0},{1,7},{3,5},{5,3},{7,1},{8,14},{10,12},{12... | collective-permute-start | bytes 110600 | tf_op jit(solution)/shard_map/ppermute | solution.py:533
  34.2 4.0 %collective-permute-start.10 = (f32[8,1152]{1,0:T(8,128)S(1)}, f32[8,1152]{1,0:T(8,128)S(1)}, u32[]{:S(2)}, u32[]{:S(2)}) collective-permute-start(f32[8,1152]{1,0:T(8,128)S(1)} %add.19.add0), channel_id=1, source_target_pairs={{0,4},{2,6},{4,0},{6,2},{1,5},{3,7},{5,1},{7,3},{8,12},{10,14},{12... | collective-permute-start | bytes 110600 | tf_op jit(solution)/shard_map/ppermute | solution.py:533
  35.2 4.0 %collective-permute-start.9 = (f32[8,1152]{1,0:T(8,128)S(1)}, f32[8,1152]{1,0:T(8,128)S(1)}, u32[]{:S(2)}, u32[]{:S(2)}) collective-permute-start(f32[8,1152]{1,0:T(8,128)S(1)} %add.19.add0), channel_id=1, source_target_pairs={{0,2},{2,0},{4,6},{6,4},{1,3},{3,1},{5,7},{7,5},{8,10},{10,8},{12,... | collective-permute-start | bytes 110600 | tf_op jit(solution)/shard_map/ppermute | solution.py:533
  49.7 1.3 %collective-permute-start.12 = (f32[6,1152]{1,0:T(8,128)S(1)}, f32[6,1152]{1,0:T(8,128)S(1)}, u32[]{:S(2)}, u32[]{:S(2)}) collective-permute-start(f32[6,1152]{1,0:T(8,128)S(1)} %get-tuple-element.35), channel_id=1, source_target_pairs={{0,1},{1,0},{2,3},{3,2},{4,5},{5,4},{6,7},{7,6},{8,9},{9,8},{10,11... | collective-permute-start | bytes 82952 | tf_op jit(solution)/shard_map/ppermute | solution.py:533
  51.0 4.9 %collective-permute-start.15 = (f32[6,1152]{1,0:T(8,128)S(1)}, f32[6,1152]{1,0:T(8,128)S(1)}, u32[]{:S(2)}, u32[]{:S(2)}) collective-permute-start(f32[6,1152]{1,0:T(8,128)S(1)} %add.20), channel_id=1, source_target_pairs={{0,6},{2,4},{4,2},{6,0},{1,7},{3,5},{5,3},{7,1},{8,14},{10,12},{12... | collective-permute-start | bytes 82952 | tf_op jit(solution)/shard_map/ppermute | solution.py:533
  52.3 4.0 %collective-permute-start.14 = (f32[6,1152]{1,0:T(8,128)S(1)}, f32[6,1152]{1,0:T(8,128)S(1)}, u32[]{:S(2)}, u32[]{:S(2)}) collective-permute-start(f32[6,1152]{1,0:T(8,128)S(1)} %add.20), channel_id=1, source_target_pairs={{0,4},{2,6},{4,0},{6,2},{1,5},{3,7},{5,1},{7,3},{8,12},{10,14},{12... | collective-permute-start | bytes 82952 | tf_op jit(solution)/shard_map/ppermute | solution.py:533
  53.2 4.0 %collective-permute-start.13 = (f32[6,1152]{1,0:T(8,128)S(1)}, f32[6,1152]{1,0:T(8,128)S(1)}, u32[]{:S(2)}, u32[]{:S(2)}) collective-permute-start(f32[6,1152]{1,0:T(8,128)S(1)} %add.20), channel_id=1, source_target_pairs={{0,2},{2,0},{4,6},{6,4},{1,3},{3,1},{5,7},{7,5},{8,10},{10,8},{12,... | collective-permute-start | bytes 82952 | tf_op jit(solution)/shard_map/ppermute | solution.py:533

commit v5 on v4

--- a/solution.py
+++ b/solution.py
@@ -143,6 +143,10 @@
 def cosines(dirs, d):
     at = 3 * d
     return dirs[at], dirs[at + 1], dirs[at + 2]
+
+
+def has_low():
+    return lax.axis_index("band") % 2 == 0
 
 
 def is_even():
@@ -201,7 +205,7 @@
 
 
 def first_kernel(
-    dirs, cols, density, material, start, excess_in, flow, excess, face_a, face_b, sums, field, rate, acc, sems
+    dirs, cols, density, material, start, excess_in, flow, excess, face_a, face_b, keep, give, field, rate, acc, sums, sems
 ):
     count, nx, nb, plane = field.shape
     half = count // 2
@@ -284,9 +288,18 @@
                     totals[f] = totals[f] + scale * acc[f, x, hs, cs]
             for f in range(4):
                 sums[f * nx + x : f * nx + x + 1, cs] = sub_sum(totals[f])
-
-
-def edges_kernel(dirs, cols, density, material, halo_a, halo_b, out):
+    mid = 2 * nx
+
+    def deal(low, high):
+        for k, part in enumerate((low, high)):
+            part[:mid] = sums[k * mid : (k + 1) * mid]
+            part[mid:] = jnp.zeros((part.shape[0] - mid, plane), jnp.float32)
+
+    pl.when(has_low())(lambda: deal(keep, give))
+    pl.when(jnp.logical_not(has_low()))(lambda: deal(give, keep))
+
+
+def edges_kernel(dirs, cols, density, material, halo_a, halo_b, sums, out):
     nx, plane = density.shape
     nb = cols.shape[1]
     half = (halo_a.shape[0] - SUB) // nb
@@ -321,19 +334,20 @@
         totals = lax.fori_loop(0, half, add, tuple(jnp.zeros((SUB, LANES), jnp.float32) for _ in cuts))
         gains.append([sub_sum(t) for t in totals])
     base = half * nb
+    row = 2 * nx
+    out[...] = sums[...]
     for side in range(2):
         near, far = (0, 1) if side == 0 else (1, 0)
         for j, cs in enumerate(cuts):
-            out[side : side + 1, cs] = jnp.where(even, gains[near][j], gains[far][j])
+            out[row + side : row + side + 1, cs] = jnp.where(even, gains[near][j], gains[far][j])
             a, b = halo_a[base : base + 1, cs], halo_b[base : base + 1, cs]
-            out[2 + side : 3 + side, cs] = jnp.where(even, a, b) if side == 0 else jnp.where(even, b, a)
-    out[4:] = jnp.zeros((out.shape[0] - 4, plane), jnp.float32)
+            out[row + 2 + side : row + 3 + side, cs] = jnp.where(even, a, b) if side == 0 else jnp.where(even, b, a)
 
 
 def second_kernel(
-    dirs, cols, density, material, objective, sum0, sum1, sum2, sum3, add0, add1, add2, add3, halo0_a, halo0_b, flow, excess,
+    dirs, cols, density, material, objective, mine, theirs, halo0_a, halo0_b, flow, excess,
     dual, edge_dual, known, gradient,
-    rate, source0, source1, warm, prev, seed, acc, stage, sems,
+    rate, source0, source1, warm, prev, seed, acc, stage, full, sems,
 ):
     count, nx, nb, plane = flow.shape
     half = count // 2
@@ -345,8 +359,16 @@
     edge = halo0_a.shape[0] - SUB
     even = is_even()
 
-    total = (sum0[...] + sum1[...]) + (sum2[...] + sum3[...])
-    more = (add0[...] + add1[...]) + (add2[...] + add3[...])
+    mid = 2 * nx
+
+    def join(low, high):
+        full[:mid] = low[:mid]
+        full[mid : 2 * mid] = high[:mid]
+        full[2 * mid : 2 * mid + 4] = low[mid : mid + 4] + high[mid : mid + 4]
+
+    pl.when(has_low())(lambda: join(mine, theirs))
+    pl.when(jnp.logical_not(has_low()))(lambda: join(theirs, mine))
+    total = full[...]
     for x in range(nx):
         warm[x] = jnp.broadcast_to(total[nx + x : nx + x + 1], (SUB, plane))
     known[0:1] = total[2 * nx - 1 : 2 * nx]
@@ -354,7 +376,7 @@
     for side in range(2):
         from_a = even if side == 0 else jnp.logical_not(even)
         aim = jnp.where(from_a, halo0_a[edge + 3 : edge + 4], halo0_b[edge + 3 : edge + 4])
-        known[2 + side : 3 + side] = more[2 + side : 3 + side] + scale * aim
+        known[2 + side : 3 + side] = total[4 * nx + 2 + side : 4 * nx + 3 + side] + scale * aim
     known[4:8] = jnp.zeros((4, plane), jnp.float32)
     for x in range(nx):
         for cs in cuts:
@@ -364,10 +386,9 @@
                 + drive * total[3 * nx + x : 3 * nx + x + 1, cs]
                 + scale * objective[x : x + 1, cs]
             )
-            if x == nx - 1:
-                again = again + more[0:1, cs]
-            if x == 0:
-                again = again + more[1:2, cs]
+            for side, outer in enumerate((nx - 1, 0)):
+                if x == outer:
+                    again = again + total[4 * nx + side : 4 * nx + side + 1, cs]
             for hs in bands:
                 w = cols[1, hs]
                 rate[x, hs, cs] = rate_tile(cols, density[x : x + 1, cs], material[x : x + 1, cs], hs)
@@ -466,7 +487,7 @@
 
 def last_kernel(
     dirs, cols, density, material, halo0_a, halo0_b, halo1_a, halo1_b, excess, edge_dual, known, gradient, dual_in,
-    dual, out, done, sems,
+    dual, out, done, gained, sems,
 ):
     nx, plane = density.shape
     count, nb = edge_dual.shape[:2]
@@ -477,41 +498,48 @@
     even = is_even()
     copies = []
     gains = []
-    for part, (halo0, halo1) in enumerate(((halo0_a, halo1_a), (halo0_b, halo1_b))):
-        ahead = even if part == 0 else jnp.logical_not(even)
-        first, x = jnp.where(ahead, 0, half), jnp.where(ahead, nx - 1, 0)
-
-        def pick(ref, i, k, cs):
-            return jnp.where(ahead, ref[i : i + 1, cs], ref[k : k + 1, cs])
-
-        sums = []
+    parts = ((halo0_a, halo1_a, even), (halo0_b, halo1_b, jnp.logical_not(even)))
+
+    def places(ahead):
+        return jnp.where(ahead, 0, half), jnp.where(ahead, nx - 1, 0)
+
+    def pick(ahead, ref, i, k, cs):
+        return jnp.where(ahead, ref[i : i + 1, cs], ref[k : k + 1, cs])
+
+    for part, (halo0, halo1, ahead) in enumerate(parts):
+        first, x = places(ahead)
         for cs in cuts:
-            dens, mat = pick(density, nx - 1, 0, cs), pick(material, nx - 1, 0, cs)
+            dens, mat = pick(ahead, density, nx - 1, 0, cs), pick(ahead, material, nx - 1, 0, cs)
             beyond = halo0[params + 1 : params + 2, cs]
             beyond_mat = halo0[params + 2 : params + 3, cs].astype(jnp.int32)
-            level, drive = pick(known, 0, 1, cs), pick(known, 2, 3, cs)
-            share = 0.0
+            drive = pick(ahead, known, 2, 3, cs)
             for h, hs in enumerate(bands):
-                pace, base = cols[0, hs], base_tile(cols, mat, hs)
-                r, r_beyond = base * (0.2 + 0.8 * dens), rate_tile(cols, beyond, beyond_mat, hs)
+                pace = cols[0, hs]
+                r, r_beyond = rate_tile(cols, dens, mat, hs), rate_tile(cols, beyond, beyond_mat, hs)
                 source = cols[1, hs] * drive
-
-                def add(d, total):
+                for d in range(half):
                     ax, ay, az = [jnp.abs(a) for a in cosines(dirs, block * count + first + d)]
-                    speeds, cx = pace * (ax + ay + az), pace * ax
-                    rows = pl.ds(pl.multiple_of(d * nb + h * SUB, SUB), SUB)
-                    v = halo1[rows, cs] + source * inverse(speeds + r_beyond)
-                    new = (cx * v) * inverse(speeds + r)
-                    done[first + d, hs, cs] = edge_dual[first + d, hs, cs] + new
-                    return total + new * (excess[first + d, x, hs, cs] - level)
-
-                total = lax.fori_loop(0, half, add, jnp.zeros((SUB, LANES), jnp.float32), unroll=True)
-                share = share + base * total
-            sums.append(sub_sum(share) * 0.8)
-        gains.append(sums)
+                    speeds = pace * (ax + ay + az)
+                    v = halo1[d * nb + h * SUB : d * nb + (h + 1) * SUB, cs] + source * inverse(speeds + r_beyond)
+                    gain = (pace * ax * v) * inverse(speeds + r)
+                    gained[first + d, hs, cs] = gain
+                    done[first + d, hs, cs] = edge_dual[first + d, hs, cs] + gain
         copy = pltpu.make_async_copy(done.at[pl.ds(first, half)], dual.at[pl.ds(first, half), x], sems.at[part])
         copy.start()
         copies.append(copy)
+    for _, _, ahead in parts:
+        first, x = places(ahead)
+        sums = []
+        for cs in cuts:
+            mat, level = pick(ahead, material, nx - 1, 0, cs), pick(ahead, known, 0, 1, cs)
+            share = 0.0
+            for hs in bands:
+                total = add_terms(
+                    [gained[first + d, hs, cs] * (excess[first + d, x, hs, cs] - level) for d in range(half)]
+                )
+                share = share + base_tile(cols, mat, hs) * total
+            sums.append(sub_sum(share) * 0.8)
+        gains.append(sums)
     out[...] = gradient[...]
     for j, cs in enumerate(cuts):
         out[nx - 1 : nx, cs] = out[nx - 1 : nx, cs] + jnp.where(even, gains[0][j], gains[1][j])
@@ -533,14 +561,8 @@
     return [lax.ppermute(value, axis, hop) for hop in hops]
 
 
-def shares(partial, first, then):
-    total = sum(others(partial, first), partial)
-    return [total] + others(total, then)
-
-
-def packed(parts, count):
-    parts = parts + [jnp.zeros_like(parts[0])] * (count - len(parts))
-    return parts[: count - 1] + [sum(parts[count:], parts[count - 1])]
+def shares(value, axis):
+    return [value] + others(value, axis)
 
 
 def on_device(
@@ -589,16 +611,18 @@
     )(*stay(*small, *cells, start))
     halo0_a, halo0_b = swapped(face_a, 0), swapped(face_b, 1)
 
-    flow, excess, face_a, face_b, sums = pl.pallas_call(
+    mid = -(-(2 * nx + 4) // SUB) * SUB
+    flow, excess, face_a, face_b, keep, give = pl.pallas_call(
         first_kernel,
         out_shape=(
-            like(*start.shape), like(*start.shape), like(half * nb, plane), like(half * nb, plane), like(4 * nx, plane)
+            like(*start.shape), like(*start.shape), like(half * nb, plane), like(half * nb, plane),
+            like(mid, plane), like(mid, plane),
         ),
         in_specs=[smem] + [vmem] * 3 + [hbm] * 2,
-        out_specs=[vmem] * 5,
+        out_specs=[vmem] * 6,
         scratch_shapes=[
             pltpu.VMEM(start.shape, f32), pltpu.VMEM((nx, nb, plane), f32), pltpu.VMEM((4, nx, nb, plane), f32),
-            pltpu.SemaphoreType.DMA((2, nx)),
+            pltpu.VMEM((4 * nx, plane), f32), pltpu.SemaphoreType.DMA((2, nx)),
         ],
         compiler_params=params,
         cost_estimate=cost(20, 12),
@@ -606,18 +630,17 @@
     )(dirs, cols, density, material, *stay(start, excess))
     halo1_a, halo1_b = swapped(face_a, 0), swapped(face_b, 1)
 
-    parts = packed(shares(sums, "band", "dir"), 4)
-
-    extra = pl.pallas_call(
+    sums = pl.pallas_call(
         edges_kernel,
-        out_shape=like(SUB, plane),
-        in_specs=[smem] + [vmem] * 5,
+        out_shape=like(mid, plane),
+        in_specs=[smem] + [vmem] * 6,
         out_specs=vmem,
         compiler_params=params,
         cost_estimate=cost(1, 1),
         name="edges",
-    )(dirs, cols, density, material, halo0_a, halo0_b)
-    extras = packed(shares(extra, "band", "dir"), 4)
+    )(dirs, cols, density, material, halo0_a, halo0_b, keep + others(give, "band")[0])
+    mine = sum(shares(sums, "dir"))
+    theirs = others(mine, "band")[0]
 
     per = math.gcd(SECOND_GROUP, half)
     layer = pltpu.VMEM((nx, nb, plane), f32)
@@ -625,29 +648,30 @@
     dual, edge_dual, known, gradient = pl.pallas_call(
         second_kernel,
         out_shape=(pltpu.HBM(start.shape, f32), like(count, nb, plane), like(SUB, plane), like(nx, plane)),
-        in_specs=[smem] + [vmem] * 16,
+        in_specs=[smem] + [vmem] * 10,
         out_specs=[hbm] + [vmem] * 3,
         scratch_shapes=[
             layer, layer, layer, pltpu.VMEM((nx, SUB, plane), f32), rows, rows, layer,
-            pltpu.VMEM((SLOTS, per, nb, plane), f32), pltpu.SemaphoreType.DMA((SLOTS,)),
+            pltpu.VMEM((SLOTS, per, nb, plane), f32), pltpu.VMEM((4 * nx + SUB, plane), f32),
+            pltpu.SemaphoreType.DMA((SLOTS,)),
         ],
         compiler_params=params,
         cost_estimate=cost(30, 12),
         name="second",
-    )(dirs, cols, density, material, objective, *parts, *extras, halo0_a, halo0_b, flow, excess)
+    )(dirs, cols, density, material, objective, mine, theirs, halo0_a, halo0_b, flow, excess)
 
     dual, gradient = pl.pallas_call(
         last_kernel,
         out_shape=(like(*start.shape), like(nx, plane)),
         in_specs=[smem] + [vmem] * 11 + [hbm],
         out_specs=[hbm, vmem],
-        scratch_shapes=[pltpu.VMEM((count, nb, plane), f32), pltpu.SemaphoreType.DMA((2,))],
+        scratch_shapes=[pltpu.VMEM((count, nb, plane), f32)] * 2 + [pltpu.SemaphoreType.DMA((2,))],
         input_output_aliases={12: 0},
         compiler_params=params,
         cost_estimate=cost(1, 1),
         name="last",
     )(dirs, cols, density, material, halo0_a, halo0_b, halo1_a, halo1_b, excess, edge_dual, known, gradient, dual)
-    gradient = sum(shares(gradient, "band", "dir")) * (-0.125 / ITERS)
+    gradient = sum(shares(sum(shares(gradient, "band")), "dir")) * (-0.125 / ITERS)
     return (dual.transpose(0, 2, 1, 3), gradient)
 
 

time: 58 us -> 53.4 us (0.921)
  starting transfers between devices: 19.4 us -> 13 us
  waiting for transfers between devices: 14.6 us -> 16.2 us
    ppermute x12 -> x9, starting transfers between devices: 11.8 us -> 7.25 us  [others(): return [lax.ppermute(value, axis, hop) for hop in hops]]
    ppermute x4, waiting for transfers between devices: 4.51 us -> 7.48 us  [swapped(): return lax.ppermute(value, 'space', pairs + [(b, a) for a, b in pairs])]
    ppermute x4, starting transfers between devices: 7.55 us -> 5.74 us  [swapped(): return lax.ppermute(value, 'space', pairs + [(b, a) for a, b in pairs])]
    ppermute x12 -> x9, waiting for transfers between devices: 10 us -> 8.74 us  [others(): return [lax.ppermute(value, axis, hop) for hop in hops]]
  transfers between devices with their start and end apart: 16 -> 13, of which waited for: 10 -> 12; matrix products, arithmetic and copies ran while one was open for 0% -> 0% of each run, Pallas kernels for 31% -> 31%
where the time goes in v5:
time: 53.4 us; the launch traced here: 53.1 us
  Pallas kernels  22.5 us (42%)
  waiting for transfers between devices  16.2 us (30%)
  starting transfers between devices  13 us (24%)
  between operations  0.75 us (1%)
  other arithmetic  0.67 us (1%)
    ppermute x9, waiting for transfers between devices, others(): return [lax.ppermute(value, axis, hop) for hop in hops]  8.74 us
    pallas_call x1, Pallas kernels, on_device(): pl.pallas_call(first_kernel, out_shape=(like(*start.shape), like(*start.s...  8.42 us
    pallas_call x1, Pallas kernels, on_device(): pl.pallas_call(second_kernel, out_shape=(pltpu.HBM(start.shape, f32), lik...  8.01 us
    ppermute x4, waiting for transfers between devices, swapped(): return lax.ppermute(value, 'space', pairs + [(b, a) for a, b in pairs])  7.48 us
    ppermute x9, starting transfers between devices, others(): return [lax.ppermute(value, axis, hop) for hop in hops]  7.25 us
    ppermute x4, starting transfers between devices, swapped(): return lax.ppermute(value, 'space', pairs + [(b, a) for a, b in pairs])  5.74 us
    pallas_call x1, Pallas kernels, on_device(): pl.pallas_call(last_kernel, out_shape=(like(*start.shape), like(nx, plane...  2.44 us
    pallas_call x1, Pallas kernels, on_device(): pl.pallas_call(faces_kernel, out_shape=(like(half * nb + SUB, plane), lik...  2.27 us
  transfers between devices with their start and end apart: 13, of which 12 were waited for; matrix products, arithmetic and copies ran while one was open for 0% of the time, Pallas kernels for 31%

profile of v5, /device:TPU:16, one launch (start us, length us, event | category | flops | bytes accessed | tf_op | source)
XLA Modules:
  0.0 53.1 jit_solution(4399596180689249591)
XLA Ops:
  0.6 2.3 %faces.1 = (f32[136,1152]{1,0:T(8,128)S(1)}, f32[136,1152]{1,0:T(8,128)S(1)}, f32[6,16,128]{2,1,0:T(8,128)S(1)}, f32[6,1152]{1,0:T(8,128)S(1)}, s32[6,1152]{1,0:T(8,128)S(1)}, /*index=5*/f32[6,1152]{1,0:T(8,128)S(1)}) custom-call(f32[1,32]{1,0:T(1,128)} %bitcast.9, f32[1,16]{1,0:T(1,128)} %bitcast.10, f32[4,16]{1,0:T(4,128)} %table_in.1, ...), custom_call_target="tpu_custom_call" | custom-call | flops 530841 | bytes 3538944 | tf_op jit(solution)/shard_map/faces/pallas_call | solution.py:598
  2.9 1.6 %collective-permute-start = (f32[136,1152]{1,0:T(8,128)S(1)}, f32[136,1152]{1,0:T(8,128)S(1)}, u32[]{:S(2)}, u32[]{:S(2)}) collective-permute-start(f32[136,1152]{1,0:T(8,128)S(1)} %get-tuple-element.23), channel_id=1, source_target_pairs={{0,8},{16,24},{8,0},{24,16},{1,9},{17,25},{9,1},{25,17},{2,10},{18... | collective-permute-start | bytes 1880072 | tf_op jit(solution)/shard_map/ppermute | solution.py:554
  4.6 1.9 %collective-permute-start.1 = (f32[136,1152]{1,0:T(8,128)S(1)}, f32[136,1152]{1,0:T(8,128)S(1)}, u32[]{:S(2)}, u32[]{:S(2)}) collective-permute-start(f32[136,1152]{1,0:T(8,128)S(1)} %get-tuple-element.24), channel_id=1, source_target_pairs={{8,16},{16,8},{9,17},{17,9},{10,18},{18,10},{11,19},{19,11},{12,20... | collective-permute-start | bytes 1880072 | tf_op jit(solution)/shard_map/ppermute | solution.py:554
  6.5 8.4 %first.1 = (f32[16,6,16,1152]{3,2,1,0:T(8,128)S(1)}, f32[16,6,16,1152]{3,2,1,0:T(8,128)S(1)}, f32[128,1152]{1,0:T(8,128)S(1)}, f32[128,1152]{1,0:T(8,128)S(1)}, ...) custom-call(f32[192]{0:T(256)S(1)} %copy-done, f32[6,16,128]{2,1,0:T(8,128)S(1)} %get-tuple-element.20.cols, ...), custom_call_target="tpu_custom_call" | custom-call | flops 35389440 | bytes 21233664 | tf_op jit(solution)/shard_map/first/pallas_call | solution.py:615
  15.0 1.3 %collective-permute-done.4 = f32[16,1152]{1,0:T(8,128)S(1)} collective-permute-done((f32[16,1152]{1,0:T(8,128)S(1)}, f32[16,1152]{1,0:T(8,128)S(1)}, u32[]{:S(2)}, u32[]{:S(2)}) %collective-permute-start.4) | collective-permute-done | bytes 73760 | tf_op jit(solution)/shard_map/ppermute | solution.py:561
  16.3 2.6 %collective-permute-done.halo_a.halo0_a = f32[136,1152]{1,0:T(8,128)S(1)} collective-permute-done((f32[136,1152]{1,0:T(8,128)S(1)}, f32[136,1152]{1,0:T(8,128)S(1)}, u32[]{:S(2)}, u32[]{:S(2)}) %collective-permute-start) | collective-permute-done | bytes 626720 | tf_op jit(solution)/shard_map/ppermute | solution.py:554
  18.8 3.2 %collective-permute-done.1.halo_b.halo0_b = f32[136,1152]{1,0:T(8,128)S(1)} collective-permute-done((f32[136,1152]{1,0:T(8,128)S(1)}, f32[136,1152]{1,0:T(8,128)S(1)}, u32[]{:S(2)}, u32[]{:S(2)}) %collective-permute-start.1) | collective-permute-done | bytes 626720 | tf_op jit(solution)/shard_map/ppermute | solution.py:554
  22.0 1.3 %edges.1 = f32[16,1152]{1,0:T(8,128)S(1)} custom-call(f32[192]{0:T(256)S(1)} %copy-done, f32[6,16,128]{2,1,0:T(8,128)S(1)} %get-tuple-element.20.cols, f32[6,1152]{1,0:T(8,128)S(1)} %get-tuple-element.21.density, s32[6,1152]{1,0:T(8,128)S(1)} %get-tuple-element.22.material, f32[136,1152]{1,0:T(8,128)S(1)} %collective-permute-done.halo_a.halo0_a, ...), custom_call_target="tpu_custom_call" | custom-call | flops 1769472 | bytes 1769472 | tf_op jit(solution)/shard_map/edges/pallas_call | solution.py:633
  23.3 2.5 %collective-permute-start.7 = (f32[16,1152]{1,0:T(8,128)S(1)}, f32[16,1152]{1,0:T(8,128)S(1)}, u32[]{:S(2)}, u32[]{:S(2)}) collective-permute-start(f32[16,1152]{1,0:T(8,128)S(1)} %edges.1), channel_id=1, source_target_pairs={{0,6},{2,4},{4,2},{6,0},{1,7},{3,5},{5,3},{7,1},{8,14},{10,12},{12... | collective-permute-start | bytes 221192 | tf_op jit(solution)/shard_map/ppermute | solution.py:561
  25.8 0.5 collective-permute-start.6
  26.4 0.5 %collective-permute-start.5 = (f32[16,1152]{1,0:T(8,128)S(1)}, f32[16,1152]{1,0:T(8,128)S(1)}, u32[]{:S(2)}, u32[]{:S(2)}) collective-permute-start(f32[16,1152]{1,0:T(8,128)S(1)} %edges.1), channel_id=1, source_target_pairs={{0,2},{2,0},{4,6},{6,4},{1,3},{3,1},{5,7},{7,5},{8,10},{10,8},{12,... | collective-permute-start | bytes 221192 | tf_op jit(solution)/shard_map/ppermute | solution.py:561
  26.9 2.2 %collective-permute-start.3 = (f32[128,1152]{1,0:T(8,128)S(1)}, f32[128,1152]{1,0:T(8,128)S(1)}, u32[]{:S(2)}, u32[]{:S(2)}) collective-permute-start(f32[128,1152]{1,0:T(8,128)S(1)} %get-tuple-element.26), channel_id=1, source_target_pairs={{8,16},{16,8},{9,17},{17,9},{10,18},{18,10},{11,19},{19,11},{12,20... | collective-permute-start | bytes 1769480 | tf_op jit(solution)/shard_map/ppermute | solution.py:554
  29.3 0.9 %collective-permute-done.6 = f32[16,1152]{1,0:T(8,128)S(1)} collective-permute-done((f32[16,1152]{1,0:T(8,128)S(1)}, f32[16,1152]{1,0:T(8,128)S(1)}, u32[]{:S(2)}, u32[]{:S(2)}) %collective-permute-start.6) | collective-permute-done | bytes 73760 | tf_op jit(solution)/shard_map/ppermute | solution.py:561
  30.8 1.3 %collective-permute-done.8.theirs = f32[16,1152]{1,0:T(8,128)S(1)} collective-permute-done((f32[16,1152]{1,0:T(8,128)S(1)}, f32[16,1152]{1,0:T(8,128)S(1)}, u32[]{:S(2)}, u32[]{:S(2)}) %collective-permute-start.8) | collective-permute-done | bytes 73760 | tf_op jit(solution)/shard_map/ppermute | solution.py:561
  32.1 8.0 %second.1 = (f32[16,6,16,1152]{3,2,1,0:T(8,128)}, f32[16,16,1152]{2,1,0:T(8,128)S(1)}, f32[8,1152]{1,0:T(8,128)S(1)}, f32[6,1152]{1,0:T(8,128)S(1)}) custom-call(f32[192]{0:T(256)S(1)} %copy-done, f32[6,16,128]{2,1,0:T(8,128)S(1)} %get-tuple-element.20.cols, f32[6,1152]{1,0:T(8,128)S(1)} %get-tuple-element.21.density, ...), custom_call_target="tpu_custom_call" | custom-call | flops 53084160 | bytes 21233664 | tf_op jit(solution)/shard_map/second/pallas_call | solution.py:648
  40.1 1.7 %collective-permute-done.3.halo1_b = f32[128,1152]{1,0:T(8,128)S(1)} collective-permute-done((f32[128,1152]{1,0:T(8,128)S(1)}, f32[128,1152]{1,0:T(8,128)S(1)}, u32[]{:S(2)}, u32[]{:S(2)}) %collective-permute-start.3) | collective-permute-done | bytes 589856 | tf_op jit(solution)/shard_map/ppermute | solution.py:554
  41.8 2.4 %last.1 = (f32[16,6,16,1152]{3,2,1,0:T(8,128)}, f32[6,1152]{1,0:T(8,128)S(1)}) custom-call(f32[192]{0:T(256)S(1)} %copy-done, f32[6,16,128]{2,1,0:T(8,128)S(1)} %get-tuple-element.20.cols, f32[6,1152]{1,0:T(8,128)S(1)} %get-tuple-element.21.density, s32[6,1152]{1,0:T(8,128)S(1)} %get-tuple-element.22.material, ...), custom_call_target="tpu_custom_call", output_to_operand_aliasing={{0}: (12, {})} | custom-call | flops 1769472 | bytes 1769472 | tf_op jit(solution)/shard_map/last/pallas_call | solution.py:663
  44.3 1.2 %collective-permute-done.9 = f32[6,1152]{1,0:T(8,128)S(1)} collective-permute-done((f32[6,1152]{1,0:T(8,128)S(1)}, f32[6,1152]{1,0:T(8,128)S(1)}, u32[]{:S(2)}, u32[]{:S(2)}) %collective-permute-start.9) | collective-permute-done | bytes 27680 | tf_op jit(solution)/shard_map/ppermute | solution.py:561
  45.5 2.4 %collective-permute-start.12 = (f32[6,1152]{1,0:T(8,128)S(1)}, f32[6,1152]{1,0:T(8,128)S(1)}, u32[]{:S(2)}, u32[]{:S(2)}) collective-permute-start(f32[6,1152]{1,0:T(8,128)S(1)} %add.28), channel_id=1, source_target_pairs={{0,6},{2,4},{4,2},{6,0},{1,7},{3,5},{5,3},{7,1},{8,14},{10,12},{12... | collective-permute-start | bytes 82952 | tf_op jit(solution)/shard_map/ppermute | solution.py:561
  48.0 0.5 collective-permute-start.11
  48.5 0.5 %collective-permute-start.10 = (f32[6,1152]{1,0:T(8,128)S(1)}, f32[6,1152]{1,0:T(8,128)S(1)}, u32[]{:S(2)}, u32[]{:S(2)}) collective-permute-start(f32[6,1152]{1,0:T(8,128)S(1)} %add.28), channel_id=1, source_target_pairs={{0,2},{2,0},{4,6},{6,4},{1,3},{3,1},{5,7},{7,5},{8,10},{10,8},{12,... | collective-permute-start | bytes 82952 | tf_op jit(solution)/shard_map/ppermute | solution.py:561
  49.0 1.4 %collective-permute-done.12 = f32[6,1152]{1,0:T(8,128)S(1)} collective-permute-done((f32[6,1152]{1,0:T(8,128)S(1)}, f32[6,1152]{1,0:T(8,128)S(1)}, u32[]{:S(2)}, u32[]{:S(2)}) %collective-permute-start.12) | collective-permute-done | bytes 27680 | tf_op jit(solution)/shard_map/ppermute | solution.py:561
  50.4 1.5 %collective-permute-done.11 = f32[6,1152]{1,0:T(8,128)S(1)} collective-permute-done((f32[6,1152]{1,0:T(8,128)S(1)}, f32[6,1152]{1,0:T(8,128)S(1)}, u32[]{:S(2)}, u32[]{:S(2)}) %collective-permute-start.11) | collective-permute-done | bytes 27680 | tf_op jit(solution)/shard_map/ppermute | solution.py:561
  52.5 0.6 %add_multiply_fusion = f32[6,1152]{1,0:T(8,128)} fusion(f32[6,1152]{1,0:T(8,128)S(1)} %collective-permute-done.12, f32[6,1152]{1,0:T(8,128)S(1)} %collective-permute-done.11, f32[6,1152]{1,0:T(8,128)S(1)} %add.28, f32[6,1152]{1,0:T(8,128)S(1)} %collective-permute-done.10), kind=kLoop, calls=%fused_computation.1 | loop fusion | flops 27648 | bytes 138240 | tf_op jit(solution)/shard_map/mul | solution.py:674
  (13 shorter events, 1.5 us)
Async XLA Ops:
  0.6 5.8 %copy-start = (f32[192]{0:T(256)S(1)}, f32[192]{0:T(256)}, u32[]{:S(2)}) copy-start(f32[192]{0:T(256)} %constant.4.clone.dirs) | copy-start | bytes 2308
  2.9 15.9 %collective-permute-start = (f32[136,1152]{1,0:T(8,128)S(1)}, f32[136,1152]{1,0:T(8,128)S(1)}, u32[]{:S(2)}, u32[]{:S(2)}) collective-permute-start(f32[136,1152]{1,0:T(8,128)S(1)} %get-tuple-element.23), channel_id=1, source_target_pairs={{0,8},{16,24},{8,0},{24,16},{1,9},{17,25},{9,1},{25,17},{2,10},{18... | collective-permute-start | bytes 1880072 | tf_op jit(solution)/shard_map/ppermute | solution.py:554
  4.6 17.5 %collective-permute-start.1 = (f32[136,1152]{1,0:T(8,128)S(1)}, f32[136,1152]{1,0:T(8,128)S(1)}, u32[]{:S(2)}, u32[]{:S(2)}) collective-permute-start(f32[136,1152]{1,0:T(8,128)S(1)} %get-tuple-element.24), channel_id=1, source_target_pairs={{8,16},{16,8},{9,17},{17,9},{10,18},{18,10},{11,19},{19,11},{12,20... | collective-permute-start | bytes 1880072 | tf_op jit(solution)/shard_map/ppermute | solution.py:554
  14.9 1.3 %collective-permute-start.4 = (f32[16,1152]{1,0:T(8,128)S(1)}, f32[16,1152]{1,0:T(8,128)S(1)}, u32[]{:S(2)}, u32[]{:S(2)}) collective-permute-start(f32[16,1152]{1,0:T(8,128)S(1)} %get-tuple-element.30), channel_id=1, source_target_pairs={{0,1},{1,0},{2,3},{3,2},{4,5},{5,4},{6,7},{7,6},{8,9},{9,8},{10,11... | collective-permute-start | bytes 221192 | tf_op jit(solution)/shard_map/ppermute | solution.py:561
  23.3 6.0 %collective-permute-start.7 = (f32[16,1152]{1,0:T(8,128)S(1)}, f32[16,1152]{1,0:T(8,128)S(1)}, u32[]{:S(2)}, u32[]{:S(2)}) collective-permute-start(f32[16,1152]{1,0:T(8,128)S(1)} %edges.1), channel_id=1, source_target_pairs={{0,6},{2,4},{4,2},{6,0},{1,7},{3,5},{5,3},{7,1},{8,14},{10,12},{12... | collective-permute-start | bytes 221192 | tf_op jit(solution)/shard_map/ppermute | solution.py:561
  25.8 4.4 %collective-permute-start.6 = (f32[16,1152]{1,0:T(8,128)S(1)}, f32[16,1152]{1,0:T(8,128)S(1)}, u32[]{:S(2)}, u32[]{:S(2)}) collective-permute-start(f32[16,1152]{1,0:T(8,128)S(1)} %edges.1), channel_id=1, source_target_pairs={{0,4},{2,6},{4,0},{6,2},{1,5},{3,7},{5,1},{7,3},{8,12},{10,14},{12... | collective-permute-start | bytes 221192 | tf_op jit(solution)/shard_map/ppermute | solution.py:561
  26.4 4.4 %collective-permute-start.5 = (f32[16,1152]{1,0:T(8,128)S(1)}, f32[16,1152]{1,0:T(8,128)S(1)}, u32[]{:S(2)}, u32[]{:S(2)}) collective-permute-start(f32[16,1152]{1,0:T(8,128)S(1)} %edges.1), channel_id=1, source_target_pairs={{0,2},{2,0},{4,6},{6,4},{1,3},{3,1},{5,7},{7,5},{8,10},{10,8},{12,... | collective-permute-start | bytes 221192 | tf_op jit(solution)/shard_map/ppermute | solution.py:561
  26.9 13.2 %collective-permute-start.2 = (f32[128,1152]{1,0:T(8,128)S(1)}, f32[128,1152]{1,0:T(8,128)S(1)}, u32[]{:S(2)}, u32[]{:S(2)}) collective-permute-start(f32[128,1152]{1,0:T(8,128)S(1)} %get-tuple-element.25), channel_id=1, source_target_pairs={{0,8},{16,24},{8,0},{24,16},{1,9},{17,25},{9,1},{25,17},{2,10},{18... | collective-permute-start | bytes 1769480 | tf_op jit(solution)/shard_map/ppermute | solution.py:554
  26.9 14.9 %collective-permute-start.3 = (f32[128,1152]{1,0:T(8,128)S(1)}, f32[128,1152]{1,0:T(8,128)S(1)}, u32[]{:S(2)}, u32[]{:S(2)}) collective-permute-start(f32[128,1152]{1,0:T(8,128)S(1)} %get-tuple-element.26), channel_id=1, source_target_pairs={{8,16},{16,8},{9,17},{17,9},{10,18},{18,10},{11,19},{19,11},{12,20... | collective-permute-start | bytes 1769480 | tf_op jit(solution)/shard_map/ppermute | solution.py:554
  30.7 1.3 %collective-permute-start.8 = (f32[16,1152]{1,0:T(8,128)S(1)}, f32[16,1152]{1,0:T(8,128)S(1)}, u32[]{:S(2)}, u32[]{:S(2)}) collective-permute-start(f32[16,1152]{1,0:T(8,128)S(1)} %add_add_fusion.mine), channel_id=1, source_target_pairs={{0,1},{1,0},{2,3},{3,2},{4,5},{5,4},{6,7},{7,6},{8,9},{9,8},{10,11... | collective-permute-start | bytes 221192 | tf_op jit(solution)/shard_map/ppermute | solution.py:561
  44.3 1.3 %collective-permute-start.9 = (f32[6,1152]{1,0:T(8,128)S(1)}, f32[6,1152]{1,0:T(8,128)S(1)}, u32[]{:S(2)}, u32[]{:S(2)}) collective-permute-start(f32[6,1152]{1,0:T(8,128)S(1)} %get-tuple-element.37), channel_id=1, source_target_pairs={{0,1},{1,0},{2,3},{3,2},{4,5},{5,4},{6,7},{7,6},{8,9},{9,8},{10,11... | collective-permute-start | bytes 82952 | tf_op jit(solution)/shard_map/ppermute | solution.py:561
  45.5 4.9 %collective-permute-start.12 = (f32[6,1152]{1,0:T(8,128)S(1)}, f32[6,1152]{1,0:T(8,128)S(1)}, u32[]{:S(2)}, u32[]{:S(2)}) collective-permute-start(f32[6,1152]{1,0:T(8,128)S(1)} %add.28), channel_id=1, source_target_pairs={{0,6},{2,4},{4,2},{6,0},{1,7},{3,5},{5,3},{7,1},{8,14},{10,12},{12... | collective-permute-start | bytes 82952 | tf_op jit(solution)/shard_map/ppermute | solution.py:561
  48.0 4.0 %collective-permute-start.11 = (f32[6,1152]{1,0:T(8,128)S(1)}, f32[6,1152]{1,0:T(8,128)S(1)}, u32[]{:S(2)}, u32[]{:S(2)}) collective-permute-start(f32[6,1152]{1,0:T(8,128)S(1)} %add.28), channel_id=1, source_target_pairs={{0,4},{2,6},{4,0},{6,2},{1,5},{3,7},{5,1},{7,3},{8,12},{10,14},{12... | collective-permute-start | bytes 82952 | tf_op jit(solution)/shard_map/ppermute | solution.py:561
  48.5 4.0 %collective-permute-start.10 = (f32[6,1152]{1,0:T(8,128)S(1)}, f32[6,1152]{1,0:T(8,128)S(1)}, u32[]{:S(2)}, u32[]{:S(2)}) collective-permute-start(f32[6,1152]{1,0:T(8,128)S(1)} %add.28), channel_id=1, source_target_pairs={{0,2},{2,0},{4,6},{6,4},{1,3},{3,1},{5,7},{7,5},{8,10},{10,8},{12,... | collective-permute-start | bytes 82952 | tf_op jit(solution)/shard_map/ppermute | solution.py:561

commit v6 on v5

--- a/solution.py
+++ b/solution.py
@@ -180,13 +180,15 @@
         copies.append(pltpu.make_async_copy(start.at[pl.ds(second, half), x], others.at[side], sems.at[at + half]))
     for copy in copies:
         copy.start()
-    for copy in copies:
+    for copy in copies[:6]:
         copy.wait()
     fill_columns(cols, heat, speed, table)
     for side, out in enumerate((out_a, out_b)):
         upper = even if side == 0 else jnp.logical_not(even)
         row = lambda ref, cs: jnp.where(upper, ref[last : last + 1, cs], ref[0:1, cs])
         base = half * nb
+        for copy in copies[6 + side * (half + 1) : 6 + (side + 1) * (half + 1)]:
+            copy.wait()
         for cs in tiles(plane):
             dens, mat = row(density, cs), row(material, cs)
             share = 0.0
@@ -486,8 +488,8 @@
 
 
 def last_kernel(
-    dirs, cols, density, material, halo0_a, halo0_b, halo1_a, halo1_b, excess, edge_dual, known, gradient, dual_in,
-    dual, out, done, gained, sems,
+    dirs, cols, density, material, halo0_a, halo0_b, halo1_a, halo1_b, excess, edge_dual, known, gradient,
+    out, done, gained,
 ):
     nx, plane = density.shape
     count, nb = edge_dual.shape[:2]
@@ -496,7 +498,6 @@
     params = halo0_a.shape[0] - SUB
     block = lax.axis_index("dir")
     even = is_even()
-    copies = []
     gains = []
     parts = ((halo0_a, halo1_a, even), (halo0_b, halo1_b, jnp.logical_not(even)))
 
@@ -524,9 +525,6 @@
                     gain = (pace * ax * v) * inverse(speeds + r)
                     gained[first + d, hs, cs] = gain
                     done[first + d, hs, cs] = edge_dual[first + d, hs, cs] + gain
-        copy = pltpu.make_async_copy(done.at[pl.ds(first, half)], dual.at[pl.ds(first, half), x], sems.at[part])
-        copy.start()
-        copies.append(copy)
     for _, _, ahead in parts:
         first, x = places(ahead)
         sums = []
@@ -544,6 +542,18 @@
     for j, cs in enumerate(cuts):
         out[nx - 1 : nx, cs] = out[nx - 1 : nx, cs] + jnp.where(even, gains[0][j], gains[1][j])
         out[0:1, cs] = out[0:1, cs] + jnp.where(even, gains[1][j], gains[0][j])
+
+
+def place_kernel(done, dual_in, dual, sems):
+    half = done.shape[0] // 2
+    copies = [
+        pltpu.make_async_copy(
+            done.at[pl.ds(side * half, half)], dual.at[pl.ds(side * half, half), x], sems.at[side]
+        )
+        for side, x in enumerate((dual.shape[1] - 1, 0))
+    ]
+    for copy in copies:
+        copy.start()
     for copy in copies:
         copy.wait()
 
@@ -660,18 +670,28 @@
         name="second",
     )(dirs, cols, density, material, objective, mine, theirs, halo0_a, halo0_b, flow, excess)
 
-    dual, gradient = pl.pallas_call(
+    gradient, done = pl.pallas_call(
         last_kernel,
-        out_shape=(like(*start.shape), like(nx, plane)),
-        in_specs=[smem] + [vmem] * 11 + [hbm],
-        out_specs=[hbm, vmem],
-        scratch_shapes=[pltpu.VMEM((count, nb, plane), f32)] * 2 + [pltpu.SemaphoreType.DMA((2,))],
-        input_output_aliases={12: 0},
+        out_shape=(like(nx, plane), like(count, nb, plane)),
+        in_specs=[smem] + [vmem] * 11,
+        out_specs=[vmem] * 2,
+        scratch_shapes=[pltpu.VMEM((count, nb, plane), f32)],
         compiler_params=params,
         cost_estimate=cost(1, 1),
         name="last",
-    )(dirs, cols, density, material, halo0_a, halo0_b, halo1_a, halo1_b, excess, edge_dual, known, gradient, dual)
+    )(dirs, cols, density, material, halo0_a, halo0_b, halo1_a, halo1_b, excess, edge_dual, known, gradient)
     gradient = sum(shares(sum(shares(gradient, "band")), "dir")) * (-0.125 / ITERS)
+    dual = pl.pallas_call(
+        place_kernel,
+        out_shape=like(*start.shape),
+        in_specs=[vmem, hbm],
+        out_specs=hbm,
+        scratch_shapes=[pltpu.SemaphoreType.DMA((2,))],
+        input_output_aliases={1: 0},
+        compiler_params=params,
+        cost_estimate=cost(0, 2),
+        name="place",
+    )(done, dual)
     return (dual.transpose(0, 2, 1, 3), gradient)
 
 

time: 53.4 us -> 52.7 us (0.987)
  waiting for transfers between devices: 16.2 us -> 15.2 us
    ppermute x9, waiting for transfers between devices: 8.74 us -> 7.71 us  [others(): return [lax.ppermute(value, axis, hop) for hop in hops]]
    pallas_call x1 -> x2, Pallas kernels: 2.44 us -> 2.85 us  [the longest x1 1.83 us: on_device(): pl.pallas_call(last_kernel, out_shape=(like(nx, plane), like(count, nb, p...]
  transfers between devices with their start and end apart: 13 -> 13, of which waited for: 12 -> 12; matrix products, arithmetic and copies ran while one was open for 0% -> 0% of each run, Pallas kernels for 31% -> 33%
where the time goes in v6:
time: 52.7 us; the launch traced here: 52.3 us
  Pallas kernels  22.7 us (43%)
  waiting for transfers between devices  15.2 us (29%)
  starting transfers between devices  13 us (25%)
  between operations  0.75 us (1%)
  other arithmetic  0.67 us (1%)
    pallas_call x1, Pallas kernels, on_device(): pl.pallas_call(first_kernel, out_shape=(like(*start.shape), like(*start.s...  8.42 us
    pallas_call x1, Pallas kernels, on_device(): pl.pallas_call(second_kernel, out_shape=(pltpu.HBM(start.shape, f32), lik...  8.01 us
    ppermute x9, waiting for transfers between devices, others(): return [lax.ppermute(value, axis, hop) for hop in hops]  7.71 us
    ppermute x4, waiting for transfers between devices, swapped(): return lax.ppermute(value, 'space', pairs + [(b, a) for a, b in pairs])  7.48 us
    ppermute x9, starting transfers between devices, others(): return [lax.ppermute(value, axis, hop) for hop in hops]  7.25 us
    ppermute x4, starting transfers between devices, swapped(): return lax.ppermute(value, 'space', pairs + [(b, a) for a, b in pairs])  5.74 us
    pallas_call x1, Pallas kernels, on_device(): pl.pallas_call(faces_kernel, out_shape=(like(half * nb + SUB, plane), lik...  2.12 us
    pallas_call x1, Pallas kernels, on_device(): pl.pallas_call(last_kernel, out_shape=(like(nx, plane), like(count, nb, p...  1.83 us
  transfers between devices with their start and end apart: 13, of which 12 were waited for; matrix products, arithmetic and copies ran while one was open for 0% of the time, Pallas kernels for 33%

profile of v6, /device:TPU:16, one launch (start us, length us, event | category | flops | bytes accessed | tf_op | source)
XLA Modules:
  0.0 52.3 jit_solution(263388364652326877)
XLA Ops:
  0.6 2.1 %faces.1 = (f32[136,1152]{1,0:T(8,128)S(1)}, f32[136,1152]{1,0:T(8,128)S(1)}, f32[6,16,128]{2,1,0:T(8,128)S(1)}, f32[6,1152]{1,0:T(8,128)S(1)}, s32[6,1152]{1,0:T(8,128)S(1)}, /*index=5*/f32[6,1152]{1,0:T(8,128)S(1)}) custom-call(f32[1,32]{1,0:T(1,128)} %bitcast.9, f32[1,16]{1,0:T(1,128)} %bitcast.10, f32[4,16]{1,0:T(4,128)} %table_in.1, ...), custom_call_target="tpu_custom_call" | custom-call | flops 530841 | bytes 3538944 | tf_op jit(solution)/shard_map/faces/pallas_call | solution.py:608
  2.8 1.6 %collective-permute-start = (f32[136,1152]{1,0:T(8,128)S(1)}, f32[136,1152]{1,0:T(8,128)S(1)}, u32[]{:S(2)}, u32[]{:S(2)}) collective-permute-start(f32[136,1152]{1,0:T(8,128)S(1)} %get-tuple-element.23), channel_id=1, source_target_pairs={{0,8},{16,24},{8,0},{24,16},{1,9},{17,25},{9,1},{25,17},{2,10},{18... | collective-permute-start | bytes 1880072 | tf_op jit(solution)/shard_map/ppermute | solution.py:564
  4.4 1.9 %collective-permute-start.1 = (f32[136,1152]{1,0:T(8,128)S(1)}, f32[136,1152]{1,0:T(8,128)S(1)}, u32[]{:S(2)}, u32[]{:S(2)}) collective-permute-start(f32[136,1152]{1,0:T(8,128)S(1)} %get-tuple-element.24), channel_id=1, source_target_pairs={{8,16},{16,8},{9,17},{17,9},{10,18},{18,10},{11,19},{19,11},{12,20... | collective-permute-start | bytes 1880072 | tf_op jit(solution)/shard_map/ppermute | solution.py:564
  6.3 8.4 %first.1 = (f32[16,6,16,1152]{3,2,1,0:T(8,128)S(1)}, f32[16,6,16,1152]{3,2,1,0:T(8,128)S(1)}, f32[128,1152]{1,0:T(8,128)S(1)}, f32[128,1152]{1,0:T(8,128)S(1)}, ...) custom-call(f32[192]{0:T(256)S(1)} %copy-done, f32[6,16,128]{2,1,0:T(8,128)S(1)} %get-tuple-element.20.cols, ...), custom_call_target="tpu_custom_call" | custom-call | flops 35389440 | bytes 21233664 | tf_op jit(solution)/shard_map/first/pallas_call | solution.py:625
  14.9 1.3 %collective-permute-done.4 = f32[16,1152]{1,0:T(8,128)S(1)} collective-permute-done((f32[16,1152]{1,0:T(8,128)S(1)}, f32[16,1152]{1,0:T(8,128)S(1)}, u32[]{:S(2)}, u32[]{:S(2)}) %collective-permute-start.4) | collective-permute-done | bytes 73760 | tf_op jit(solution)/shard_map/ppermute | solution.py:571
  16.1 2.6 %collective-permute-done.halo_a.halo0_a = f32[136,1152]{1,0:T(8,128)S(1)} collective-permute-done((f32[136,1152]{1,0:T(8,128)S(1)}, f32[136,1152]{1,0:T(8,128)S(1)}, u32[]{:S(2)}, u32[]{:S(2)}) %collective-permute-start) | collective-permute-done | bytes 626720 | tf_op jit(solution)/shard_map/ppermute | solution.py:564
  18.7 3.2 %collective-permute-done.1.halo_b.halo0_b = f32[136,1152]{1,0:T(8,128)S(1)} collective-permute-done((f32[136,1152]{1,0:T(8,128)S(1)}, f32[136,1152]{1,0:T(8,128)S(1)}, u32[]{:S(2)}, u32[]{:S(2)}) %collective-permute-start.1) | collective-permute-done | bytes 626720 | tf_op jit(solution)/shard_map/ppermute | solution.py:564
  21.9 1.3 %edges.1 = f32[16,1152]{1,0:T(8,128)S(1)} custom-call(f32[192]{0:T(256)S(1)} %copy-done, f32[6,16,128]{2,1,0:T(8,128)S(1)} %get-tuple-element.20.cols, f32[6,1152]{1,0:T(8,128)S(1)} %get-tuple-element.21.density, s32[6,1152]{1,0:T(8,128)S(1)} %get-tuple-element.22.material, f32[136,1152]{1,0:T(8,128)S(1)} %collective-permute-done.halo_a.halo0_a, ...), custom_call_target="tpu_custom_call" | custom-call | flops 1769472 | bytes 1769472 | tf_op jit(solution)/shard_map/edges/pallas_call | solution.py:643
  23.2 2.5 %collective-permute-start.7 = (f32[16,1152]{1,0:T(8,128)S(1)}, f32[16,1152]{1,0:T(8,128)S(1)}, u32[]{:S(2)}, u32[]{:S(2)}) collective-permute-start(f32[16,1152]{1,0:T(8,128)S(1)} %edges.1), channel_id=1, source_target_pairs={{0,6},{2,4},{4,2},{6,0},{1,7},{3,5},{5,3},{7,1},{8,14},{10,12},{12... | collective-permute-start | bytes 221192 | tf_op jit(solution)/shard_map/ppermute | solution.py:571
  26.2 0.5 %collective-permute-start.5 = (f32[16,1152]{1,0:T(8,128)S(1)}, f32[16,1152]{1,0:T(8,128)S(1)}, u32[]{:S(2)}, u32[]{:S(2)}) collective-permute-start(f32[16,1152]{1,0:T(8,128)S(1)} %edges.1), channel_id=1, source_target_pairs={{0,2},{2,0},{4,6},{6,4},{1,3},{3,1},{5,7},{7,5},{8,10},{10,8},{12,... | collective-permute-start | bytes 221192 | tf_op jit(solution)/shard_map/ppermute | solution.py:571
  26.7 2.2 %collective-permute-start.3 = (f32[128,1152]{1,0:T(8,128)S(1)}, f32[128,1152]{1,0:T(8,128)S(1)}, u32[]{:S(2)}, u32[]{:S(2)}) collective-permute-start(f32[128,1152]{1,0:T(8,128)S(1)} %get-tuple-element.26), channel_id=1, source_target_pairs={{8,16},{16,8},{9,17},{17,9},{10,18},{18,10},{11,19},{19,11},{12,20... | collective-permute-start | bytes 1769480 | tf_op jit(solution)/shard_map/ppermute | solution.py:564
  29.2 0.9 %collective-permute-done.6 = f32[16,1152]{1,0:T(8,128)S(1)} collective-permute-done((f32[16,1152]{1,0:T(8,128)S(1)}, f32[16,1152]{1,0:T(8,128)S(1)}, u32[]{:S(2)}, u32[]{:S(2)}) %collective-permute-start.6) | collective-permute-done | bytes 73760 | tf_op jit(solution)/shard_map/ppermute | solution.py:571
  30.1 0.5 collective-permute-done.5
  30.7 1.3 %collective-permute-done.8.theirs = f32[16,1152]{1,0:T(8,128)S(1)} collective-permute-done((f32[16,1152]{1,0:T(8,128)S(1)}, f32[16,1152]{1,0:T(8,128)S(1)}, u32[]{:S(2)}, u32[]{:S(2)}) %collective-permute-start.8) | collective-permute-done | bytes 73760 | tf_op jit(solution)/shard_map/ppermute | solution.py:571
  31.9 8.0 %second.1 = (f32[16,6,16,1152]{3,2,1,0:T(8,128)}, f32[16,16,1152]{2,1,0:T(8,128)S(1)}, f32[8,1152]{1,0:T(8,128)S(1)}, f32[6,1152]{1,0:T(8,128)S(1)}) custom-call(f32[192]{0:T(256)S(1)} %copy-done, f32[6,16,128]{2,1,0:T(8,128)S(1)} %get-tuple-element.20.cols, f32[6,1152]{1,0:T(8,128)S(1)} %get-tuple-element.21.density, ...), custom_call_target="tpu_custom_call" | custom-call | flops 53084160 | bytes 21233664 | tf_op jit(solution)/shard_map/second/pallas_call | solution.py:658
  39.9 1.7 %collective-permute-done.3.halo1_b = f32[128,1152]{1,0:T(8,128)S(1)} collective-permute-done((f32[128,1152]{1,0:T(8,128)S(1)}, f32[128,1152]{1,0:T(8,128)S(1)}, u32[]{:S(2)}, u32[]{:S(2)}) %collective-permute-start.3) | collective-permute-done | bytes 589856 | tf_op jit(solution)/shard_map/ppermute | solution.py:564
  41.7 1.8 %last.1 = (f32[6,1152]{1,0:T(8,128)S(1)}, f32[16,16,1152]{2,1,0:T(8,128)S(1)}) custom-call(f32[192]{0:T(256)S(1)} %copy-done, f32[6,16,128]{2,1,0:T(8,128)S(1)} %get-tuple-element.20.cols, f32[6,1152]{1,0:T(8,128)S(1)} %get-tuple-element.21.density, s32[6,1152]{1,0:T(8,128)S(1)} %get-tuple-element.22.material, ...), custom_call_target="tpu_custom_call" | custom-call | flops 1769472 | bytes 1769472 | tf_op jit(solution)/shard_map/last/pallas_call | solution.py:673
  43.6 1.2 %collective-permute-done.9 = f32[6,1152]{1,0:T(8,128)S(1)} collective-permute-done((f32[6,1152]{1,0:T(8,128)S(1)}, f32[6,1152]{1,0:T(8,128)S(1)}, u32[]{:S(2)}, u32[]{:S(2)}) %collective-permute-start.9) | collective-permute-done | bytes 27680 | tf_op jit(solution)/shard_map/ppermute | solution.py:571
  44.8 2.4 %collective-permute-start.12 = (f32[6,1152]{1,0:T(8,128)S(1)}, f32[6,1152]{1,0:T(8,128)S(1)}, u32[]{:S(2)}, u32[]{:S(2)}) collective-permute-start(f32[6,1152]{1,0:T(8,128)S(1)} %add.28), channel_id=1, source_target_pairs={{0,6},{2,4},{4,2},{6,0},{1,7},{3,5},{5,3},{7,1},{8,14},{10,12},{12... | collective-permute-start | bytes 82952 | tf_op jit(solution)/shard_map/ppermute | solution.py:571
  47.7 0.5 %collective-permute-start.10 = (f32[6,1152]{1,0:T(8,128)S(1)}, f32[6,1152]{1,0:T(8,128)S(1)}, u32[]{:S(2)}, u32[]{:S(2)}) collective-permute-start(f32[6,1152]{1,0:T(8,128)S(1)} %add.28), channel_id=1, source_target_pairs={{0,2},{2,0},{4,6},{6,4},{1,3},{3,1},{5,7},{7,5},{8,10},{10,8},{12,... | collective-permute-start | bytes 82952 | tf_op jit(solution)/shard_map/ppermute | solution.py:571
  48.3 1.0 %place.1 = f32[16,6,16,1152]{3,2,1,0:T(8,128)} custom-call(f32[16,16,1152]{2,1,0:T(8,128)S(1)} %get-tuple-element.35.done, f32[16,6,16,1152]{3,2,1,0:T(8,128)} %get-tuple-element.36.dual_in), custom_call_target="tpu_custom_call", output_to_operand_aliasing={{}: (1, {})} | custom-call | bytes 3538944 | tf_op jit(solution)/shard_map/place/pallas_call | solution.py:684
  49.6 1.5 %collective-permute-done.11 = f32[6,1152]{1,0:T(8,128)S(1)} collective-permute-done((f32[6,1152]{1,0:T(8,128)S(1)}, f32[6,1152]{1,0:T(8,128)S(1)}, u32[]{:S(2)}, u32[]{:S(2)}) %collective-permute-start.11) | collective-permute-done | bytes 27680 | tf_op jit(solution)/shard_map/ppermute | solution.py:571
  51.2 0.5 collective-permute-done.10
  51.7 0.6 %add_multiply_fusion = f32[6,1152]{1,0:T(8,128)} fusion(f32[6,1152]{1,0:T(8,128)S(1)} %collective-permute-done.12, f32[6,1152]{1,0:T(8,128)S(1)} %collective-permute-done.11, f32[6,1152]{1,0:T(8,128)S(1)} %add.28, f32[6,1152]{1,0:T(8,128)S(1)} %collective-permute-done.10), kind=kLoop, calls=%fused_computation.1 | loop fusion | flops 27648 | bytes 138240 | tf_op jit(solution)/shard_map/mul | solution.py:683
  (14 shorter events, 1.8 us)
Async XLA Ops:
  0.6 5.7 %copy-start = (f32[192]{0:T(256)S(1)}, f32[192]{0:T(256)}, u32[]{:S(2)}) copy-start(f32[192]{0:T(256)} %constant.4.clone.dirs) | copy-start | bytes 2308
  2.8 15.9 %collective-permute-start = (f32[136,1152]{1,0:T(8,128)S(1)}, f32[136,1152]{1,0:T(8,128)S(1)}, u32[]{:S(2)}, u32[]{:S(2)}) collective-permute-start(f32[136,1152]{1,0:T(8,128)S(1)} %get-tuple-element.23), channel_id=1, source_target_pairs={{0,8},{16,24},{8,0},{24,16},{1,9},{17,25},{9,1},{25,17},{2,10},{18... | collective-permute-start | bytes 1880072 | tf_op jit(solution)/shard_map/ppermute | solution.py:564
  4.4 17.5 %collective-permute-start.1 = (f32[136,1152]{1,0:T(8,128)S(1)}, f32[136,1152]{1,0:T(8,128)S(1)}, u32[]{:S(2)}, u32[]{:S(2)}) collective-permute-start(f32[136,1152]{1,0:T(8,128)S(1)} %get-tuple-element.24), channel_id=1, source_target_pairs={{8,16},{16,8},{9,17},{17,9},{10,18},{18,10},{11,19},{19,11},{12,20... | collective-permute-start | bytes 1880072 | tf_op jit(solution)/shard_map/ppermute | solution.py:564
  14.8 1.3 %collective-permute-start.4 = (f32[16,1152]{1,0:T(8,128)S(1)}, f32[16,1152]{1,0:T(8,128)S(1)}, u32[]{:S(2)}, u32[]{:S(2)}) collective-permute-start(f32[16,1152]{1,0:T(8,128)S(1)} %get-tuple-element.30), channel_id=1, source_target_pairs={{0,1},{1,0},{2,3},{3,2},{4,5},{5,4},{6,7},{7,6},{8,9},{9,8},{10,11... | collective-permute-start | bytes 221192 | tf_op jit(solution)/shard_map/ppermute | solution.py:571
  23.2 6.0 %collective-permute-start.7 = (f32[16,1152]{1,0:T(8,128)S(1)}, f32[16,1152]{1,0:T(8,128)S(1)}, u32[]{:S(2)}, u32[]{:S(2)}) collective-permute-start(f32[16,1152]{1,0:T(8,128)S(1)} %edges.1), channel_id=1, source_target_pairs={{0,6},{2,4},{4,2},{6,0},{1,7},{3,5},{5,3},{7,1},{8,14},{10,12},{12... | collective-permute-start | bytes 221192 | tf_op jit(solution)/shard_map/ppermute | solution.py:571
  25.7 4.4 %collective-permute-start.6 = (f32[16,1152]{1,0:T(8,128)S(1)}, f32[16,1152]{1,0:T(8,128)S(1)}, u32[]{:S(2)}, u32[]{:S(2)}) collective-permute-start(f32[16,1152]{1,0:T(8,128)S(1)} %edges.1), channel_id=1, source_target_pairs={{0,4},{2,6},{4,0},{6,2},{1,5},{3,7},{5,1},{7,3},{8,12},{10,14},{12... | collective-permute-start | bytes 221192 | tf_op jit(solution)/shard_map/ppermute | solution.py:571
  26.2 4.4 %collective-permute-start.5 = (f32[16,1152]{1,0:T(8,128)S(1)}, f32[16,1152]{1,0:T(8,128)S(1)}, u32[]{:S(2)}, u32[]{:S(2)}) collective-permute-start(f32[16,1152]{1,0:T(8,128)S(1)} %edges.1), channel_id=1, source_target_pairs={{0,2},{2,0},{4,6},{6,4},{1,3},{3,1},{5,7},{7,5},{8,10},{10,8},{12,... | collective-permute-start | bytes 221192 | tf_op jit(solution)/shard_map/ppermute | solution.py:571
  26.7 13.2 %collective-permute-start.2 = (f32[128,1152]{1,0:T(8,128)S(1)}, f32[128,1152]{1,0:T(8,128)S(1)}, u32[]{:S(2)}, u32[]{:S(2)}) collective-permute-start(f32[128,1152]{1,0:T(8,128)S(1)} %get-tuple-element.25), channel_id=1, source_target_pairs={{0,8},{16,24},{8,0},{24,16},{1,9},{17,25},{9,1},{25,17},{2,10},{18... | collective-permute-start | bytes 1769480 | tf_op jit(solution)/shard_map/ppermute | solution.py:564
  26.7 14.9 %collective-permute-start.3 = (f32[128,1152]{1,0:T(8,128)S(1)}, f32[128,1152]{1,0:T(8,128)S(1)}, u32[]{:S(2)}, u32[]{:S(2)}) collective-permute-start(f32[128,1152]{1,0:T(8,128)S(1)} %get-tuple-element.26), channel_id=1, source_target_pairs={{8,16},{16,8},{9,17},{17,9},{10,18},{18,10},{11,19},{19,11},{12,20... | collective-permute-start | bytes 1769480 | tf_op jit(solution)/shard_map/ppermute | solution.py:564
  30.6 1.3 %collective-permute-start.8 = (f32[16,1152]{1,0:T(8,128)S(1)}, f32[16,1152]{1,0:T(8,128)S(1)}, u32[]{:S(2)}, u32[]{:S(2)}) collective-permute-start(f32[16,1152]{1,0:T(8,128)S(1)} %add_add_fusion.mine), channel_id=1, source_target_pairs={{0,1},{1,0},{2,3},{3,2},{4,5},{5,4},{6,7},{7,6},{8,9},{9,8},{10,11... | collective-permute-start | bytes 221192 | tf_op jit(solution)/shard_map/ppermute | solution.py:571
  43.5 1.3 %collective-permute-start.9 = (f32[6,1152]{1,0:T(8,128)S(1)}, f32[6,1152]{1,0:T(8,128)S(1)}, u32[]{:S(2)}, u32[]{:S(2)}) collective-permute-start(f32[6,1152]{1,0:T(8,128)S(1)} %get-tuple-element.37), channel_id=1, source_target_pairs={{0,1},{1,0},{2,3},{3,2},{4,5},{5,4},{6,7},{7,6},{8,9},{9,8},{10,11... | collective-permute-start | bytes 82952 | tf_op jit(solution)/shard_map/ppermute | solution.py:571
  44.8 4.9 %collective-permute-start.12 = (f32[6,1152]{1,0:T(8,128)S(1)}, f32[6,1152]{1,0:T(8,128)S(1)}, u32[]{:S(2)}, u32[]{:S(2)}) collective-permute-start(f32[6,1152]{1,0:T(8,128)S(1)} %add.28), channel_id=1, source_target_pairs={{0,6},{2,4},{4,2},{6,0},{1,7},{3,5},{5,3},{7,1},{8,14},{10,12},{12... | collective-permute-start | bytes 82952 | tf_op jit(solution)/shard_map/ppermute | solution.py:571
  47.2 4.0 %collective-permute-start.11 = (f32[6,1152]{1,0:T(8,128)S(1)}, f32[6,1152]{1,0:T(8,128)S(1)}, u32[]{:S(2)}, u32[]{:S(2)}) collective-permute-start(f32[6,1152]{1,0:T(8,128)S(1)} %add.28), channel_id=1, source_target_pairs={{0,4},{2,6},{4,0},{6,2},{1,5},{3,7},{5,1},{7,3},{8,12},{10,14},{12... | collective-permute-start | bytes 82952 | tf_op jit(solution)/shard_map/ppermute | solution.py:571
  47.7 4.0 %collective-permute-start.10 = (f32[6,1152]{1,0:T(8,128)S(1)}, f32[6,1152]{1,0:T(8,128)S(1)}, u32[]{:S(2)}, u32[]{:S(2)}) collective-permute-start(f32[6,1152]{1,0:T(8,128)S(1)} %add.28), channel_id=1, source_target_pairs={{0,2},{2,0},{4,6},{6,4},{1,3},{3,1},{5,7},{7,5},{8,10},{10,8},{12,... | collective-permute-start | bytes 82952 | tf_op jit(solution)/shard_map/ppermute | solution.py:571
